TPU v7x, 32 devices: a whole 2x2x4 slice. The times are simulated.
32 devices in a mesh: tp: 8 (over z, x), dp: 4 (over y, core).
Axes of the slice: x: 2, y: 2, z: 4, core: 2. Of those that a mesh axis runs over, the one named last changes fastest.
Arguments:
- hidden: bfloat16 [4096, 1600], P(('dp', 'tp')), parts along dimension 0
- gain: bfloat16 [1600], replicated, may hold values from 0.5 to 1.5
- head: bfloat16 [1600, 32000], P(None, 'tp')
- lengths: int32 [16], P('dp'), parts along dimension 0, may hold values from 64 to 256, as said below
- mask: int32 [4096], P(('dp', 'tp')), parts along dimension 0, may hold values 0 or 1
- targets: int32 [4096], P(('dp', 'tp')), parts along dimension 0, may hold values from 0 to 31999
Outputs:
- logprob: float32 [4096], P(('dp', 'tp')), parts along dimension 0
- entropy: float32 [4096], P(('dp', 'tp')), parts along dimension 0
There are 4 independent parts, one for each index of `dp`. A program takes and returns all parts, laid end to end along the dimension named above; an argument that names none is the same for every part. Nothing has to cross between parts.
Inputs may be any that keep to these rules, and one draw needn't show every extreme that they name: `lengths`: each sequence's live length; the longest sequence of a batch fills all 256 slots.
All inputs are finite; a program needn't handle non-finite values. No bound on the sum of `mask` on one device may be relied on, other than what follows from the above.
Results may differ from a plain program's by a relative error of at most 0.003.
The roundings to bfloat16 on the way count: a program that leaves them out, or rounds other values in their place, can miss the bound.
Values may be sent and summed in bfloat16 or wider, within the bound.
No kernel may reach another device: no remote copies, remote signals or barrier semaphores. Data moves between devices by JAX's collectives and lax.ppermute only.
A program may use at most 128 MiB of HBM per device.

v0:
```python
import jax
import jax.numpy as jnp
from jax import lax
from jax.sharding import PartitionSpec as P

SEQ_LEN = 256


EPS = 1e-06


def on_device(hidden, gain, head, lengths, mask, targets):
    rows = hidden.shape[0]
    width = head.shape[1]
    me = lax.axis_index("tp")
    xf = hidden.astype(jnp.float32)
    meansq = jnp.mean(xf * xf, axis=-1, keepdims=True)
    normed = (xf * lax.rsqrt(meansq + EPS) * gain.astype(jnp.float32)).astype(jnp.bfloat16)
    col_start = me * width
    col_ids = jnp.arange(width, dtype=jnp.int32)
    piece_rows = lax.all_gather(normed, "tp", axis=0, tiled=True)
    piece_tgt = lax.all_gather(targets, "tp", axis=0, tiled=True)
    logits = jnp.dot(piece_rows, head, preferred_element_type=jnp.float32)
    top = jnp.max(logits, axis=-1)
    shifted = logits - top[:, None]
    expo = jnp.exp(shifted)
    sums = jnp.sum(expo, axis=-1)
    ent = jnp.sum(expo * shifted, axis=-1)
    local_id = piece_tgt - col_start
    hit = col_ids[None, :] == local_id[:, None]
    tgt = jnp.sum(jnp.where(hit, logits, 0.0), axis=-1)
    fresh = (top, sums, tgt, ent)
    top, sums, tgt, ent = tuple((new for new in fresh))
    glob_top = lax.pmax(top, "tp")
    scale = jnp.exp(top - glob_top)
    all_sums, all_tgt, all_ent = lax.psum(
        (sums * scale, tgt, (ent + (top - glob_top) * sums) * scale), "tp"
    )
    own_sums = lax.dynamic_slice_in_dim(all_sums, me * rows, rows)
    own_tgt = lax.dynamic_slice_in_dim(all_tgt, me * rows, rows)
    own_ent = lax.dynamic_slice_in_dim(all_ent, me * rows, rows)
    own_top = lax.dynamic_slice_in_dim(glob_top, me * rows, rows)
    log_total = jnp.log(own_sums)
    logp = own_tgt - (own_top + log_total)
    entropy = log_total - own_ent / own_sums
    row_ids = me * rows + jnp.arange(rows, dtype=jnp.int32)
    slot = row_ids % SEQ_LEN
    seq_id = row_ids // SEQ_LEN
    seq_count = lengths.shape[0]
    match = seq_id[:, None] == jnp.arange(seq_count, dtype=jnp.int32)[None, :]
    seq_len = jnp.sum(jnp.where(match, lengths[None, :], 0), axis=1)
    valid = (slot < seq_len) & (mask == 1)
    zero = jnp.zeros_like(logp)
    return (jnp.where(valid, logp, zero), jnp.where(valid, entropy, zero))


def solution(mesh):
    return jax.shard_map(
        on_device,
        mesh=mesh,
        in_specs=(
            P(("dp", "tp"), None),
            P(),
            P(None, "tp"),
            P("dp"),
            P(("dp", "tp")),
            P(("dp", "tp")),
        ),
        out_specs=(P(("dp", "tp")), P(("dp", "tp"))),
        check_vma=False,
    )
```

profile of v0, /device:TPU:0, one launch (start us, length us, event | category | flops | bytes accessed | tf_op | source)
XLA Modules:
  0.0 168.2 jit_solution(18042996847578816531)
XLA Ops:
  7.2 0.0 all-gather.3.cloned.1.call-start
  7.2 0.7 convert_element_type.10
  7.9 1.2 fusion.1
  9.1 2.0 %fusion.3 = bf16[128,1600]{0,1:T(8,128)(2,1)} fusion(bf16[128,1600]{0,1:T(8,128)(2,1)} %param.6, f32[1600]{0:T(1024)S(1)} %convert_element_type.10, f32[128]{0:T(128)S(1)} %add_rsqrt_fusion), kind=kLoop, calls=%fused_computation.9 | loop fusion | flops 819200 | bytes 826112 | tf_op jit(solution)/shard_map/convert_element_type | solution.py:18
  11.2 0.0 all-gather.3.cloned.1.call-update
  11.2 22.4 %all-gather = s32[8,1,128]{2,1,0:T(1,128)S(1)} all-gather(s32[1,1,128]{2,1,0:T(1,128)} %bitcast.8), channel_id=1, replica_groups=mesh['tp'=8,'dp'=4] {'tp'}, dimensions={0}, use_global_device_ids=true | all-gather | bytes 4608 | tf_op jit(solution)/shard_map/all_gather | solution.py:22
  33.6 0.7 select_reduce_fusion.1
  34.3 44.3 %all-gather.3.cloned.1.call-done = bf16[1024,1600]{0,1:T(8,128)(2,1)} async-done(((bf16[128,1600]{0,1:T(8,128)(2,1)}), bf16[1024,1600]{0,1:T(8,128)(2,1)}) %all-gather.3.cloned.1.call-update) | async-done | bytes 3276816 | tf_op jit(solution)/shard_map/all_gather | solution.py:21
  78.6 20.9 %fusion.4 = (f32[1024]{0:T(1024)S(1)}, f32[1024,4000]{0,1:T(8,128)}) fusion(bf16[1024,1600]{0,1:T(8,128)(2,1)} %all-gather.3.cloned.1.call-done, bf16[1600,4000]{1,0:T(8,128)(2,1)} %param.8), kind=kOutput, calls=%fused_computation.25 | convolution fusion | flops 13111294976 | bytes 32464896 | tf_op jit(solution)/shard_map/dot_general | solution.py:23
  99.5 0.0 copy-start
  99.5 18.7 %pmax.7 = f32[1024]{0:T(1024)S(1)} all-reduce(f32[1024]{0:T(1024)S(1)} %get-tuple-element.12), channel_id=1, replica_groups=mesh['tp'=8,'dp'=4] {'tp'}, use_global_device_ids=true, to_apply=%region_5.6 | all-reduce | flops 1024 | bytes 8192 | tf_op jit(solution)/shard_map/pmax | solution.py:34
  118.2 8.5 %fusion = (f32[1024]{0:T(1024)S(1)}, f32[1024]{0:T(1024)S(1)}, f32[1024]{0:T(1024)S(1)}) fusion(f32[1024,4000]{0,1:T(8,128)} %get-tuple-element.13, f32[1024]{0:T(1024)S(1)} %get-tuple-element.12, s32[1024]{0:T(1024)S(1)} %bitcast.7), kind=kLoop, calls=%fused_computation.2 | loop fusion | flops 28668928 | bytes 16404480 | tf_op jit(solution)/shard_map/reduce_sum | solution.py:28
  126.8 33.4 %all-reduce = (f32[1024]{0:T(1024)S(1)}, f32[1024]{0:T(1024)S(1)}, f32[1024]{0:T(1024)S(1)}) all-reduce(f32[1024]{0:T(1024)S(1)} %get-tuple-element.4, f32[1024]{0:T(1024)S(1)} %get-tuple-element.11, f32[1024]{0:T(1024)S(1)} %get-tuple-element.10), channel_id=1, replica_groups=mesh['tp'=8,'dp'=4] {'tp'}, use_global_device_ids=true, to_apply=%region_3.0 | all-reduce | flops 3072 | bytes 24576 | tf_op jit(solution)/shard_map/psum | solution.py:36
  160.2 0.0 copy-done
  160.2 0.6 subtract_select_fusion
  160.8 0.6 subtract_select_fusion.1
  (4 shorter events, 0.0 us)
Async XLA Ops:
  7.2 71.5 %all-gather.3.cloned.1.call-start = ((), (), s32[]{:S(2)}) async-start(), calls=%async_computation | async-start | bytes 3686400 | tf_op jit(solution)/shard_map/all_gather | solution.py:21
  99.5 60.7 %copy-start = (s32[128]{0:T(128)S(1)}, s32[128]{0:T(128)}, u32[]{:S(2)}) copy-start(s32[128]{0:T(128)} %param.10) | copy-start | bytes 1540
Sparse Core Ops, SparseCore 0:
  11.3 67.2 all-gather.2
where the time goes:
time: 169 us; the launch traced here: 168 us
  blocking collectives  74.5 us (44%)
  waiting for transfers between devices  44.3 us (26%)
  matrix products  20.9 us (12%)
  other arithmetic  14.4 us (9%)
  between operations  14.1 us (8%)
    all_gather x1, waiting for transfers between devices, on_device(): piece_rows = lax.all_gather(normed, 'tp', axis=0, tiled=True)  44.3 us
    psum x1, blocking collectives, on_device(): lax.psum((sums * scale, tgt, (ent + (top - glob_top) * sums) * scale), 'tp')  33.4 us
    all_gather x1, blocking collectives, on_device(): piece_tgt = lax.all_gather(targets, 'tp', axis=0, tiled=True)  22.4 us
    dot_general x1, matrix products, on_device(): logits = jnp.dot(piece_rows, head, preferred_element_type=jnp.float32)  20.9 us
    pmax x1, blocking collectives, on_device(): glob_top = lax.pmax(top, 'tp')  18.7 us
    reduce_sum x1, other arithmetic, on_device(): ent = jnp.sum(expo * shifted, axis=-1)  8.53 us
  transfers between devices with their start and end apart: 1, of which 1 were waited for; matrix products, arithmetic and copies ran while one was open for 0% of the time, Pallas kernels for 0%

commit v1 on v0

v1 whole, which is shorter than its diff:
```python
import functools

import jax
import jax.numpy as jnp
from jax import lax
from jax.experimental import pallas as pl
from jax.experimental.pallas import tpu as pltpu
from jax.sharding import PartitionSpec as P

SEQ_LEN = 256
EPS = 1e-06
EXTRA = 16
BASE = 256
VMEM_LIMIT = 32 * 1024 * 1024

VMEM = pl.BlockSpec(memory_space=pltpu.VMEM)
SMEM = pl.BlockSpec(memory_space=pltpu.SMEM)


def norm_kernel(me, lengths, hidden_t, gain, mask, targets, first, second, valid):
    width, rows = hidden_t.shape
    cut = first.shape[0] - EXTRA
    x = hidden_t[...].astype(jnp.float32)
    meansq = jnp.sum(x * x, axis=0, keepdims=True) * (1.0 / width)
    scale = lax.rsqrt(meansq + EPS)
    g = jnp.broadcast_to(gain[...].astype(jnp.float32), (rows, width)).T
    normed = (x * scale * g).astype(jnp.bfloat16)
    first[:cut, :] = normed[:cut]
    second[...] = normed[cut:]
    ids = targets[...]
    high = ids // BASE
    digit = lax.broadcasted_iota(jnp.int32, (EXTRA, rows), 0)
    digits = jnp.where(digit == 0, high, jnp.where(digit == 1, ids - high * BASE, 0))
    first[cut:, :] = digits.astype(jnp.float32).astype(jnp.bfloat16)
    row = me[0] * rows + lax.broadcasted_iota(jnp.int32, (1, rows), 1)
    length = jnp.zeros((1, rows), jnp.int32)
    for s in range(lengths.shape[0]):
        length = jnp.where(row // SEQ_LEN == s, lengths[s], length)
    live = (row % SEQ_LEN < length) & (mask[...] == 1)
    valid[...] = live.astype(jnp.int32)


def wave_kernel(blocks, me, head, *refs):
    parts = refs[: 2 * blocks]
    stats = refs[2 * blocks : 3 * blocks]
    x_scr, id_scr, logit_scr = refs[3 * blocks :]
    vocab = head.shape[1]
    rows = parts[0].shape[1]
    cut = parts[0].shape[0] - EXTRA
    for b in range(blocks):
        first, second = parts[2 * b], parts[2 * b + 1]
        at = pl.ds(b * rows, rows)
        x_scr[at, :cut] = first[:cut, :].T
        x_scr[at, cut:] = second[...].T
        digits = first[cut:, :].astype(jnp.float32).T.astype(jnp.int32)
        id_scr[at, :] = digits[:, 0:1] * BASE + digits[:, 1:2] - me[0] * vocab
    chunk = 512
    for lo in range(0, vocab, chunk):
        hi = min(vocab, lo + chunk)
        logit_scr[:, lo:hi] = jnp.dot(
            x_scr[...], head[:, lo:hi], preferred_element_type=jnp.float32
        )
    group = 16
    lane = lax.broadcasted_iota(jnp.int32, (group, 128), 1)
    col = lax.broadcasted_iota(jnp.int32, (group, vocab), 1)
    for b in range(blocks):
        found = []
        for g in range(rows // group):
            at = pl.ds(b * rows + g * group, group)
            logits = logit_scr[at, :]
            top = jnp.max(logits, axis=1, keepdims=True)
            shifted = logits - top
            expo = jnp.exp(shifted)
            sums = jnp.sum(expo, axis=1, keepdims=True)
            ent = jnp.sum(expo * shifted, axis=1, keepdims=True)
            hit = col == id_scr[at, :]
            tgt = jnp.sum(jnp.where(hit, logits, 0.0), axis=1, keepdims=True)
            found.append(
                jnp.where(
                    lane == 0,
                    top,
                    jnp.where(lane == 1, sums, jnp.where(lane == 2, ent, tgt)),
                )
            )
        stats[b][...] = jnp.concatenate(found, axis=0).T[:8, :]


def final_kernel(count, valid, *refs):
    stats, (logprob, entropy) = refs[:count], refs[count:]
    tops = [s[0:1, :] for s in stats]
    top = functools.reduce(jnp.maximum, tops)
    sums = ent = tgt = jnp.zeros_like(top)
    for s, own in zip(stats, tops):
        delta = own - top
        scale = jnp.exp(delta)
        own_sums = s[1:2, :]
        sums = sums + own_sums * scale
        ent = ent + (s[2:3, :] + delta * own_sums) * scale
        tgt = tgt + s[3:4, :]
    log_total = jnp.log(sums)
    live = valid[...] == 1
    logprob[...] = jnp.where(live, tgt - (top + log_total), 0.0)
    entropy[...] = jnp.where(live, log_total - ent / sums, 0.0)


def wave(me, head, blocks):
    count = len(blocks)
    width, vocab = head.shape
    rows = blocks[0][0].shape[1]
    return pl.pallas_call(
        functools.partial(wave_kernel, count),
        out_shape=[jax.ShapeDtypeStruct((8, rows), jnp.float32)] * count,
        in_specs=[SMEM, VMEM] + [VMEM] * (2 * count),
        out_specs=[VMEM] * count,
        scratch_shapes=[
            pltpu.VMEM((count * rows, width), jnp.bfloat16),
            pltpu.VMEM((count * rows, 1), jnp.int32),
            pltpu.VMEM((count * rows, vocab), jnp.float32),
        ],
        compiler_params=pltpu.CompilerParams(vmem_limit_bytes=VMEM_LIMIT),
        cost_estimate=pl.CostEstimate(
            flops=2 * count * rows * width * vocab,
            bytes_accessed=2 * width * vocab,
            transcendentals=count * rows * vocab,
        ),
        name=f"wave{count}",
    )(me, head, *[part for block in blocks for part in block])


def on_device(n, hidden, gain, head, lengths, mask, targets):
    rows, width = hidden.shape
    cut = (width // 2) // 128 * 128
    me = lax.axis_index("tp").astype(jnp.int32).reshape(1)

    ring = list(range(0, n, 2)) + list(range(1, n, 2))[::-1]

    def hop(value, by):
        pairs = [(ring[i], ring[(i + by) % n]) for i in range(n)]
        return lax.ppermute(value, "tp", pairs)

    first, second, valid = pl.pallas_call(
        norm_kernel,
        out_shape=[
            jax.ShapeDtypeStruct((cut + EXTRA, rows), jnp.bfloat16),
            jax.ShapeDtypeStruct((width - cut, rows), jnp.bfloat16),
            jax.ShapeDtypeStruct((1, rows), jnp.int32),
        ],
        in_specs=[SMEM, SMEM, VMEM, VMEM, VMEM, VMEM],
        out_specs=[VMEM] * 3,
        compiler_params=pltpu.CompilerParams(vmem_limit_bytes=VMEM_LIMIT),
        name="norm",
    )(me, lengths, hidden.T, gain.reshape(1, width), mask.reshape(1, rows), targets.reshape(1, rows))

    stats = []
    up = down = (first, second)
    held = [up]
    for step in range(1, n // 2 + 1):
        last = 2 * step == n
        if last:
            arrived = [(hop(up[0], 1), hop(down[1], -1))]
        else:
            up = (hop(up[0], 1), hop(up[1], 1))
            down_second = hop(down[1], -1)
            down = (hop(down[0], -1), down_second)
            arrived = [up, down]
        for k, s in enumerate(wave(me, head, held)):
            by = 0 if step == 1 else (1 - step, step - 1)[k]
            stats.append(hop(s, by) if by else s)
        held = arrived
    for k, s in enumerate(wave(me, head, held)):
        stats.append(hop(s, (-(n // 2), n // 2)[k]))

    logprob, entropy = pl.pallas_call(
        functools.partial(final_kernel, n),
        out_shape=[jax.ShapeDtypeStruct((1, rows), jnp.float32)] * 2,
        in_specs=[VMEM] * (n + 1),
        out_specs=[VMEM] * 2,
        name="combine",
    )(valid, *stats)
    return logprob.reshape(rows), entropy.reshape(rows)


def solution(mesh):
    return jax.shard_map(
        functools.partial(on_device, mesh.shape["tp"]),
        mesh=mesh,
        in_specs=(
            P(("dp", "tp"), None),
            P(),
            P(None, "tp"),
            P("dp"),
            P(("dp", "tp")),
            P(("dp", "tp")),
        ),
        out_specs=(P(("dp", "tp")), P(("dp", "tp"))),
        check_vma=False,
    )
```

time: 169 us -> 70.9 us (0.42)
  blocking collectives: 74.5 us -> 0 us
  waiting for transfers between devices: 44.3 us -> 7.49 us
  starting transfers between devices: 0.04 us -> 29 us
  Pallas kernels: 0 us -> 23.8 us
  matrix products: 20.9 us -> 0 us
  other arithmetic: 14.4 us -> 0.01 us
  between operations: 14.1 us -> 0.78 us
  local copies, waits for them, and re-layouts: 0.01 us -> 9.59 us
    all_gather x1 -> x0, waiting for transfers between devices: 44.3 us -> none  [on_device(): piece_rows = lax.all_gather(normed, 'tp', axis=0, tiled=True)]
    psum x1 -> x0, blocking collectives: 33.4 us -> none  [on_device(): lax.psum((sums * scale, tgt, (ent + (top - glob_top) * sums) * scale), 'tp')]
    ppermute x0 -> x21, starting transfers between devices: none -> 29 us  [hop(): return lax.ppermute(value, 'tp', pairs)]
    pallas_call x0 -> x7, Pallas kernels: none -> 23.8 us  [the longest x5 21.6 us: wave(): pl.pallas_call(functools.partial(wave_kernel, count), out_shape=[jax.Shap...]
    all_gather x1 -> x0, blocking collectives: 22.4 us -> none  [on_device(): piece_tgt = lax.all_gather(targets, 'tp', axis=0, tiled=True)]
    dot_general x1 -> x0, matrix products: 20.9 us -> none  [on_device(): logits = jnp.dot(piece_rows, head, preferred_element_type=jnp.float32)]
    pmax x1 -> x0, blocking collectives: 18.7 us -> none  [on_device(): glob_top = lax.pmax(top, 'tp')]
    reduce_sum x3 -> x0, other arithmetic: 10.5 us -> none  [the longest x1 8.53 us: on_device(): ent = jnp.sum(expo * shifted, axis=-1)]
  transfers between devices with their start and end apart: 1 -> 21, of which waited for: 1 -> 1; matrix products, arithmetic and copies ran while one was open for 0% -> 0% of each run, Pallas kernels for 0% -> 31%
where the time goes in v1:
time: 70.9 us; the launch traced here: 70.6 us
  starting transfers between devices  29 us (41%)
  Pallas kernels  23.8 us (34%)
  local copies, waits for them, and re-layouts  9.59 us (14%)
  waiting for transfers between devices  7.49 us (11%)
  between operations  0.78 us (1%)
    ppermute x21, starting transfers between devices, hop(): return lax.ppermute(value, 'tp', pairs)  29 us
    pallas_call x5, Pallas kernels, wave(): pl.pallas_call(functools.partial(wave_kernel, count), out_shape=[jax.Shap...  21.6 us
    unnamed x36, local copies, waits for them, and re-layouts  8.9 us
    ppermute x21, waiting for transfers between devices, hop(): return lax.ppermute(value, 'tp', pairs)  7.49 us
  transfers between devices with their start and end apart: 21, of which 1 were waited for; matrix products, arithmetic and copies ran while one was open for 0% of the time, Pallas kernels for 31%

profile of v1, /device:TPU:0, one launch (start us, length us, event | category | flops | bytes accessed | tf_op | source)
XLA Modules:
  0.0 70.6 jit_solution(15778478559845698492)
XLA Ops:
  0.6 0.7 reshape.23.gain
  1.3 1.0 %copy-done.1 = bf16[128,1600]{0,1:T(8,128)(2,1)S(1)} copy-done((bf16[128,1600]{0,1:T(8,128)(2,1)S(1)}, bf16[128,1600]{0,1:T(8,128)(2,1)}, u32[]{:S(2)}) %copy-start.1) | copy-done | bytes 409624
  2.3 0.7 copy-done.3
  3.0 0.7 copy-done.4
  3.6 0.7 copy-done.5
  4.3 0.9 %norm.1 = (bf16[784,128]{1,0:T(8,128)(2,1)S(1)}, bf16[832,128]{1,0:T(8,128)(2,1)S(1)}, s32[1,128]{1,0:T(1,128)S(1)}) custom-call(s32[1]{0:T(128)} %bitcast.me, s32[4]{0:T(128)S(1)} %copy-done.3, bf16[1600,128]{1,0:T(8,128)(2,1)S(1)} %bitcast.8, bf16[1,1600]{1,0:T(2,128)(2,1)S(1)} %reshape.23.gain, s32[1,128]{1,0:T(1,128)S(1)} %bitcast.9, s32[1,128]{1,0:T(1,128)S(1)} %bitcast.10), custom_call_target="tpu_custom_call" | custom-call | tf_op jit(solution)/shard_map/norm/pallas_call | solution.py:141
  5.2 3.1 %collective-permute-start.1 = (bf16[832,128]{1,0:T(8,128)(2,1)S(1)}, bf16[832,128]{1,0:T(8,128)(2,1)S(1)}, u32[]{:S(2)}, u32[]{:S(2)}) collective-permute-start(bf16[832,128]{1,0:T(8,128)(2,1)S(1)} %get-tuple-element.15.refs_1_), channel_id=1, source_target_pairs={{0,8},{8,16},{16,24},{24,28},{28,20},{20,12},{12,4},{4,0},{1,9},{9... | collective-permute-start | bytes 638984 | tf_op jit(solution)/shard_map/ppermute | solution.py:139
  8.3 2.0 %collective-permute-start = (bf16[784,128]{1,0:T(8,128)(2,1)S(1)}, bf16[784,128]{1,0:T(8,128)(2,1)S(1)}, u32[]{:S(2)}, u32[]{:S(2)}) collective-permute-start(bf16[784,128]{1,0:T(8,128)(2,1)S(1)} %get-tuple-element.14.refs_0_), channel_id=1, source_target_pairs={{0,8},{8,16},{16,24},{24,28},{28,20},{20,12},{12,4},{4,0},{1,9},{9... | collective-permute-start | bytes 602120 | tf_op jit(solution)/shard_map/ppermute | solution.py:139
  10.3 0.0 collective-permute-start.2
  10.3 7.4 %collective-permute-done.refs_0_ = bf16[784,128]{1,0:T(8,128)(2,1)S(1)} collective-permute-done((bf16[784,128]{1,0:T(8,128)(2,1)S(1)}, bf16[784,128]{1,0:T(8,128)(2,1)S(1)}, u32[]{:S(2)}, u32[]{:S(2)}) %collective-permute-start) | collective-permute-done | bytes 200736 | tf_op jit(solution)/shard_map/ppermute | solution.py:139
  17.8 1.8 %collective-permute-start.6 = (bf16[784,128]{1,0:T(8,128)(2,1)S(1)}, bf16[784,128]{1,0:T(8,128)(2,1)S(1)}, u32[]{:S(2)}, u32[]{:S(2)}) collective-permute-start(bf16[784,128]{1,0:T(8,128)(2,1)S(1)} %collective-permute-done.refs_0_), channel_id=1, source_target_pairs={{0,8},{8,16},{16,24},{24,28},{28,20},{20,12},{12,4},{4,0},{1,9},{9... | collective-permute-start | bytes 602120 | tf_op jit(solution)/shard_map/ppermute | solution.py:139
  19.6 0.0 collective-permute-done.2.refs_2_
  19.6 0.2 collective-permute-start.8
  19.8 0.0 collective-permute-done.1.refs_1_
  19.8 1.8 %collective-permute-start.7 = (bf16[832,128]{1,0:T(8,128)(2,1)S(1)}, bf16[832,128]{1,0:T(8,128)(2,1)S(1)}, u32[]{:S(2)}, u32[]{:S(2)}) collective-permute-start(bf16[832,128]{1,0:T(8,128)(2,1)S(1)} %collective-permute-done.1.refs_1_), channel_id=1, source_target_pairs={{0,8},{8,16},{16,24},{24,28},{28,20},{20,12},{12,4},{4,0},{1,9},{9... | collective-permute-start | bytes 638984 | tf_op jit(solution)/shard_map/ppermute | solution.py:139
  21.6 0.0 collective-permute-done.3.refs_3_
  21.6 0.2 collective-permute-start.9
  21.8 4.7 %copy-done = bf16[1600,4000]{1,0:T(8,128)(2,1)S(1)} copy-done((bf16[1600,4000]{1,0:T(8,128)(2,1)S(1)}, bf16[1600,4000]{1,0:T(8,128)(2,1)}, u32[]{:S(2)}) %copy-start) | copy-done | bytes 12800024
  26.5 5.3 %wave2.3 = (f32[8,128]{1,0:T(8,128)S(1)}, f32[8,128]{1,0:T(8,128)S(1)}) custom-call(s32[1]{0:T(128)} %bitcast.me, bf16[1600,4000]{1,0:T(8,128)(2,1)S(1)} %copy-done, bf16[784,128]{1,0:T(8,128)(2,1)S(1)} %collective-permute-done.refs_0_, bf16[832,128]{1,0:T(8,128)(2,1)S(1)} %collective-permute-done.1.refs_1_, ...), custom_call_target="tpu_custom_call" | custom-call | flops 3276800000 | bytes 12800000 | tf_op jit(solution)/shard_map/wave2/pallas_call | solution.py:110
  31.8 1.8 %collective-permute-start.4 = (f32[8,128]{1,0:T(8,128)S(1)}, f32[8,128]{1,0:T(8,128)S(1)}, u32[]{:S(2)}, u32[]{:S(2)}) collective-permute-start(f32[8,128]{1,0:T(8,128)S(1)} %get-tuple-element.16), channel_id=1, source_target_pairs={{0,4},{8,0},{16,8},{24,16},{28,24},{20,28},{12,20},{4,12},{1,5},{9... | collective-permute-start | bytes 12296 | tf_op jit(solution)/shard_map/ppermute | solution.py:139
  33.6 0.0 collective-permute-done.6.refs_0_
  33.6 0.3 collective-permute-start.12
  33.9 1.7 %collective-permute-start.14 = (bf16[784,128]{1,0:T(8,128)(2,1)S(1)}, bf16[784,128]{1,0:T(8,128)(2,1)S(1)}, u32[]{:S(2)}, u32[]{:S(2)}) collective-permute-start(bf16[784,128]{1,0:T(8,128)(2,1)S(1)} %collective-permute-done.8.refs_2_), channel_id=1, source_target_pairs={{0,4},{8,0},{16,8},{24,16},{28,24},{20,28},{12,20},{4,12},{1,5},{9... | collective-permute-start | bytes 602120 | tf_op jit(solution)/shard_map/ppermute | solution.py:139
  35.6 0.3 collective-permute-start.13
  35.9 0.0 collective-permute-done.9.refs_3_
  35.9 1.7 %collective-permute-start.15 = (bf16[832,128]{1,0:T(8,128)(2,1)S(1)}, bf16[832,128]{1,0:T(8,128)(2,1)S(1)}, u32[]{:S(2)}, u32[]{:S(2)}) collective-permute-start(bf16[832,128]{1,0:T(8,128)(2,1)S(1)} %collective-permute-done.9.refs_3_), channel_id=1, source_target_pairs={{0,4},{8,0},{16,8},{24,16},{28,24},{20,28},{12,20},{4,12},{1,5},{9... | collective-permute-start | bytes 638984 | tf_op jit(solution)/shard_map/ppermute | solution.py:139
  37.7 5.3 %wave2.4 = (f32[8,128]{1,0:T(8,128)S(1)}, f32[8,128]{1,0:T(8,128)S(1)}) custom-call(s32[1]{0:T(128)} %bitcast.me, bf16[1600,4000]{1,0:T(8,128)(2,1)S(1)} %copy-done, bf16[784,128]{1,0:T(8,128)(2,1)S(1)} %collective-permute-done.6.refs_0_, bf16[832,128]{1,0:T(8,128)(2,1)S(1)} %collective-permute-done.7.refs_1_, ...), custom_call_target="tpu_custom_call" | custom-call | flops 3276800000 | bytes 12800000 | tf_op jit(solution)/shard_map/wave2/pallas_call | solution.py:110
  42.9 0.0 collective-permute-done.12.refs_0_
  42.9 0.3 collective-permute-start.5
  43.2 0.0 collective-permute-done.14.refs_2_
  43.3 2.8 %collective-permute-start.10 = (f32[8,128]{1,0:T(8,128)S(1)}, f32[8,128]{1,0:T(8,128)S(1)}, u32[]{:S(2)}, u32[]{:S(2)}) collective-permute-start(f32[8,128]{1,0:T(8,128)S(1)} %get-tuple-element.18), channel_id=1, source_target_pairs={{0,12},{8,4},{16,0},{24,8},{28,16},{20,24},{12,28},{4,20},{1,13},{... | collective-permute-start | bytes 12296 | tf_op jit(solution)/shard_map/ppermute | solution.py:139
  46.1 0.4 collective-permute-start.18
  46.5 0.0 collective-permute-done.15.refs_3_
  46.5 1.6 %collective-permute-start.19 = (bf16[832,128]{1,0:T(8,128)(2,1)S(1)}, bf16[832,128]{1,0:T(8,128)(2,1)S(1)}, u32[]{:S(2)}, u32[]{:S(2)}) collective-permute-start(bf16[832,128]{1,0:T(8,128)(2,1)S(1)} %collective-permute-done.15.refs_3_), channel_id=1, source_target_pairs={{0,4},{8,0},{16,8},{24,16},{28,24},{20,28},{12,20},{4,12},{1,5},{9... | collective-permute-start | bytes 638984 | tf_op jit(solution)/shard_map/ppermute | solution.py:139
  48.1 5.3 %wave2.5 = (f32[8,128]{1,0:T(8,128)S(1)}, f32[8,128]{1,0:T(8,128)S(1)}) custom-call(s32[1]{0:T(128)} %bitcast.me, bf16[1600,4000]{1,0:T(8,128)(2,1)S(1)} %copy-done, bf16[784,128]{1,0:T(8,128)(2,1)S(1)} %collective-permute-done.12.refs_0_, bf16[832,128]{1,0:T(8,128)(2,1)S(1)} %collective-permute-done.13.refs_1_, ...), custom_call_target="tpu_custom_call" | custom-call | flops 3276800000 | bytes 12800000 | tf_op jit(solution)/shard_map/wave2/pallas_call | solution.py:110
  53.4 0.2 collective-permute-start.11
  53.6 3.8 %collective-permute-start.16 = (f32[8,128]{1,0:T(8,128)S(1)}, f32[8,128]{1,0:T(8,128)S(1)}, u32[]{:S(2)}, u32[]{:S(2)}) collective-permute-start(f32[8,128]{1,0:T(8,128)S(1)} %get-tuple-element.20), channel_id=1, source_target_pairs={{0,20},{8,12},{16,4},{24,0},{28,8},{20,16},{12,24},{4,28},{1,21},{... | collective-permute-start | bytes 12296 | tf_op jit(solution)/shard_map/ppermute | solution.py:139
  57.4 2.9 %wave1.3 = f32[8,128]{1,0:T(8,128)S(1)} custom-call(s32[1]{0:T(128)} %bitcast.me, bf16[1600,4000]{1,0:T(8,128)(2,1)S(1)} %copy-done, bf16[784,128]{1,0:T(8,128)(2,1)S(1)} %collective-permute-done.18.refs_0_, bf16[832,128]{1,0:T(8,128)(2,1)S(1)} %collective-permute-done.19.refs_1_), custom_call_target="tpu_custom_call" | custom-call | flops 1638400000 | bytes 12800000 | tf_op jit(solution)/shard_map/wave1/pallas_call | solution.py:110
  60.3 0.1 collective-permute-start.17
  60.4 4.8 %collective-permute-start.20 = (f32[8,128]{1,0:T(8,128)S(1)}, f32[8,128]{1,0:T(8,128)S(1)}, u32[]{:S(2)}, u32[]{:S(2)}) collective-permute-start(f32[8,128]{1,0:T(8,128)S(1)} %wave1.3), channel_id=1, source_target_pairs={{0,28},{8,20},{16,12},{24,4},{28,0},{20,8},{12,16},{4,24},{1,29},{... | collective-permute-start | bytes 12296 | tf_op jit(solution)/shard_map/ppermute | solution.py:139
  65.2 2.9 %wave1.2.refs_0_ = f32[8,128]{1,0:T(8,128)S(1)} custom-call(s32[1]{0:T(128)} %bitcast.me, bf16[1600,4000]{1,0:T(8,128)(2,1)S(1)} %bitcast.7, bf16[784,128]{1,0:T(8,128)(2,1)S(1)} %get-tuple-element.14.refs_0_, bf16[832,128]{1,0:T(8,128)(2,1)S(1)} %get-tuple-element.15.refs_1_), custom_call_target="tpu_custom_call" | custom-call | flops 1638400000 | bytes 12800000 | tf_op jit(solution)/shard_map/wave1/pallas_call | solution.py:110
  68.1 0.6 copy-done.2
  68.8 0.5 copy-done.9
  69.3 0.0 copy-done.10
  69.3 0.0 copy-done.11
  69.3 0.0 copy-done.12
  69.3 0.0 copy-done.13
  69.4 1.3 %combine.1 = (f32[1,128]{1,0:T(1,128)}, f32[1,128]{1,0:T(1,128)}) custom-call(s32[1,128]{1,0:T(1,128)} %copy-done.6, f32[8,128]{1,0:T(8,128)} %copy-done.2, f32[8,128]{1,0:T(8,128)} %copy-done.7, f32[8,128]{1,0:T(8,128)} %copy-done.8, f32[8,128]{1,0:T(8,128)} %copy-done.9, f32[8,128]{1,0:T(8,128)} %copy-done.10, f32[8,128]{1,0:T(8,128)} %copy-done.11, ...), custom_call_target="tpu_custom_call" | custom-call | tf_op jit(solution)/shard_map/combine/pallas_call | solution.py:173
  (39 shorter events, 0.1 us)
Async XLA Ops:
  1.3 1.0 %copy-start.1 = (bf16[128,1600]{0,1:T(8,128)(2,1)S(1)}, bf16[128,1600]{0,1:T(8,128)(2,1)}, u32[]{:S(2)}) copy-start(bf16[128,1600]{0,1:T(8,128)(2,1)} %param.6) | copy-start | bytes 1228804
  2.3 0.7 copy-start.3
  3.0 0.7 copy-start.4
  3.6 0.7 copy-start.5
  5.2 16.4 %copy-start.6 = (s32[1,128]{1,0:T(1,128)}, s32[1,128]{1,0:T(1,128)S(1)}, u32[]{:S(2)}) copy-start(s32[1,128]{1,0:T(1,128)S(1)} %get-tuple-element.13.valid) | copy-start | bytes 1540
  5.2 14.6 %collective-permute-start.1 = (bf16[832,128]{1,0:T(8,128)(2,1)S(1)}, bf16[832,128]{1,0:T(8,128)(2,1)S(1)}, u32[]{:S(2)}, u32[]{:S(2)}) collective-permute-start(bf16[832,128]{1,0:T(8,128)(2,1)S(1)} %get-tuple-element.15.refs_1_), channel_id=1, source_target_pairs={{0,8},{8,16},{16,24},{24,28},{28,20},{20,12},{12,4},{4,0},{1,9},{9... | collective-permute-start | bytes 638984 | tf_op jit(solution)/shard_map/ppermute | solution.py:139
  8.3 13.3 %collective-permute-start.3 = (bf16[832,128]{1,0:T(8,128)(2,1)S(1)}, bf16[832,128]{1,0:T(8,128)(2,1)S(1)}, u32[]{:S(2)}, u32[]{:S(2)}) collective-permute-start(bf16[832,128]{1,0:T(8,128)(2,1)S(1)} %get-tuple-element.15.refs_1_), channel_id=1, source_target_pairs={{0,4},{8,0},{16,8},{24,16},{28,24},{20,28},{12,20},{4,12},{1,5},{9... | collective-permute-start | bytes 638984 | tf_op jit(solution)/shard_map/ppermute | solution.py:139
  8.3 9.5 %collective-permute-start = (bf16[784,128]{1,0:T(8,128)(2,1)S(1)}, bf16[784,128]{1,0:T(8,128)(2,1)S(1)}, u32[]{:S(2)}, u32[]{:S(2)}) collective-permute-start(bf16[784,128]{1,0:T(8,128)(2,1)S(1)} %get-tuple-element.14.refs_0_), channel_id=1, source_target_pairs={{0,8},{8,16},{16,24},{24,28},{28,20},{20,12},{12,4},{4,0},{1,9},{9... | collective-permute-start | bytes 602120 | tf_op jit(solution)/shard_map/ppermute | solution.py:139
  10.3 9.3 %collective-permute-start.2 = (bf16[784,128]{1,0:T(8,128)(2,1)S(1)}, bf16[784,128]{1,0:T(8,128)(2,1)S(1)}, u32[]{:S(2)}, u32[]{:S(2)}) collective-permute-start(bf16[784,128]{1,0:T(8,128)(2,1)S(1)} %get-tuple-element.14.refs_0_), channel_id=1, source_target_pairs={{0,4},{8,0},{16,8},{24,16},{28,24},{20,28},{12,20},{4,12},{1,5},{9... | collective-permute-start | bytes 602120 | tf_op jit(solution)/shard_map/ppermute | solution.py:139
  17.8 15.8 %collective-permute-start.6 = (bf16[784,128]{1,0:T(8,128)(2,1)S(1)}, bf16[784,128]{1,0:T(8,128)(2,1)S(1)}, u32[]{:S(2)}, u32[]{:S(2)}) collective-permute-start(bf16[784,128]{1,0:T(8,128)(2,1)S(1)} %collective-permute-done.refs_0_), channel_id=1, source_target_pairs={{0,8},{8,16},{16,24},{24,28},{28,20},{20,12},{12,4},{4,0},{1,9},{9... | collective-permute-start | bytes 602120 | tf_op jit(solution)/shard_map/ppermute | solution.py:139
  19.6 14.3 %collective-permute-start.8 = (bf16[784,128]{1,0:T(8,128)(2,1)S(1)}, bf16[784,128]{1,0:T(8,128)(2,1)S(1)}, u32[]{:S(2)}, u32[]{:S(2)}) collective-permute-start(bf16[784,128]{1,0:T(8,128)(2,1)S(1)} %collective-permute-done.2.refs_2_), channel_id=1, source_target_pairs={{0,4},{8,0},{16,8},{24,16},{28,24},{20,28},{12,20},{4,12},{1,5},{9... | collective-permute-start | bytes 602120 | tf_op jit(solution)/shard_map/ppermute | solution.py:139
  19.8 15.8 %collective-permute-start.7 = (bf16[832,128]{1,0:T(8,128)(2,1)S(1)}, bf16[832,128]{1,0:T(8,128)(2,1)S(1)}, u32[]{:S(2)}, u32[]{:S(2)}) collective-permute-start(bf16[832,128]{1,0:T(8,128)(2,1)S(1)} %collective-permute-done.1.refs_1_), channel_id=1, source_target_pairs={{0,8},{8,16},{16,24},{24,28},{28,20},{20,12},{12,4},{4,0},{1,9},{9... | collective-permute-start | bytes 638984 | tf_op jit(solution)/shard_map/ppermute | solution.py:139
  21.6 14.3 %collective-permute-start.9 = (bf16[832,128]{1,0:T(8,128)(2,1)S(1)}, bf16[832,128]{1,0:T(8,128)(2,1)S(1)}, u32[]{:S(2)}, u32[]{:S(2)}) collective-permute-start(bf16[832,128]{1,0:T(8,128)(2,1)S(1)} %collective-permute-done.3.refs_3_), channel_id=1, source_target_pairs={{0,4},{8,0},{16,8},{24,16},{28,24},{20,28},{12,20},{4,12},{1,5},{9... | collective-permute-start | bytes 638984 | tf_op jit(solution)/shard_map/ppermute | solution.py:139
  21.8 4.7 %copy-start = (bf16[1600,4000]{1,0:T(8,128)(2,1)S(1)}, bf16[1600,4000]{1,0:T(8,128)(2,1)}, u32[]{:S(2)}) copy-start(bf16[1600,4000]{1,0:T(8,128)(2,1)} %head.9) | copy-start | bytes 38400004
  31.8 28.4 %collective-permute-start.4 = (f32[8,128]{1,0:T(8,128)S(1)}, f32[8,128]{1,0:T(8,128)S(1)}, u32[]{:S(2)}, u32[]{:S(2)}) collective-permute-start(f32[8,128]{1,0:T(8,128)S(1)} %get-tuple-element.16), channel_id=1, source_target_pairs={{0,4},{8,0},{16,8},{24,16},{28,24},{20,28},{12,20},{4,12},{1,5},{9... | collective-permute-start | bytes 12296 | tf_op jit(solution)/shard_map/ppermute | solution.py:139
  33.6 9.3 %collective-permute-start.12 = (bf16[784,128]{1,0:T(8,128)(2,1)S(1)}, bf16[784,128]{1,0:T(8,128)(2,1)S(1)}, u32[]{:S(2)}, u32[]{:S(2)}) collective-permute-start(bf16[784,128]{1,0:T(8,128)(2,1)S(1)} %collective-permute-done.6.refs_0_), channel_id=1, source_target_pairs={{0,8},{8,16},{16,24},{24,28},{28,20},{20,12},{12,4},{4,0},{1,9},{9... | collective-permute-start | bytes 602120 | tf_op jit(solution)/shard_map/ppermute | solution.py:139
  33.9 9.4 %collective-permute-start.14 = (bf16[784,128]{1,0:T(8,128)(2,1)S(1)}, bf16[784,128]{1,0:T(8,128)(2,1)S(1)}, u32[]{:S(2)}, u32[]{:S(2)}) collective-permute-start(bf16[784,128]{1,0:T(8,128)(2,1)S(1)} %collective-permute-done.8.refs_2_), channel_id=1, source_target_pairs={{0,4},{8,0},{16,8},{24,16},{28,24},{20,28},{12,20},{4,12},{1,5},{9... | collective-permute-start | bytes 602120 | tf_op jit(solution)/shard_map/ppermute | solution.py:139
  35.6 10.4 %collective-permute-start.13 = (bf16[832,128]{1,0:T(8,128)(2,1)S(1)}, bf16[832,128]{1,0:T(8,128)(2,1)S(1)}, u32[]{:S(2)}, u32[]{:S(2)}) collective-permute-start(bf16[832,128]{1,0:T(8,128)(2,1)S(1)} %collective-permute-done.7.refs_1_), channel_id=1, source_target_pairs={{0,8},{8,16},{16,24},{24,28},{28,20},{20,12},{12,4},{4,0},{1,9},{9... | collective-permute-start | bytes 638984 | tf_op jit(solution)/shard_map/ppermute | solution.py:139
  35.9 10.6 %collective-permute-start.15 = (bf16[832,128]{1,0:T(8,128)(2,1)S(1)}, bf16[832,128]{1,0:T(8,128)(2,1)S(1)}, u32[]{:S(2)}, u32[]{:S(2)}) collective-permute-start(bf16[832,128]{1,0:T(8,128)(2,1)S(1)} %collective-permute-done.9.refs_3_), channel_id=1, source_target_pairs={{0,4},{8,0},{16,8},{24,16},{28,24},{20,28},{12,20},{4,12},{1,5},{9... | collective-permute-start | bytes 638984 | tf_op jit(solution)/shard_map/ppermute | solution.py:139
  42.9 17.5 %collective-permute-start.5 = (f32[8,128]{1,0:T(8,128)S(1)}, f32[8,128]{1,0:T(8,128)S(1)}, u32[]{:S(2)}, u32[]{:S(2)}) collective-permute-start(f32[8,128]{1,0:T(8,128)S(1)} %get-tuple-element.17), channel_id=1, source_target_pairs={{0,8},{8,16},{16,24},{24,28},{28,20},{20,12},{12,4},{4,0},{1,9},{9... | collective-permute-start | bytes 12296 | tf_op jit(solution)/shard_map/ppermute | solution.py:139
  43.2 21.9 %slice-start = ((s8[13107200]{0:T(1024)(128)(4,1)}), s8[524288]{0:T(1024)(128)(4,1)S(1)}, s32[]{:S(2)}) async-start(s8[13107200]{0:T(1024)(128)(4,1)} %bitcast.6), calls=%async_computation | async-start | bytes 1048576
  43.2 21.9 %slice-start.1 = ((s8[13107200]{0:T(1024)(128)(4,1)}), s8[4194304]{0:T(1024)(128)(4,1)S(1)}, s32[]{:S(2)}) async-start(s8[13107200]{0:T(1024)(128)(4,1)} %bitcast.6), calls=%async_computation.1 | async-start | bytes 8388608
  43.3 21.9 %slice-start.2 = ((s8[13107200]{0:T(1024)(128)(4,1)}), s8[4194304]{0:T(1024)(128)(4,1)S(1)}, s32[]{:S(2)}) async-start(s8[13107200]{0:T(1024)(128)(4,1)} %bitcast.6), calls=%async_computation.2 | async-start | bytes 8388608
  43.3 25.4 %collective-permute-start.10 = (f32[8,128]{1,0:T(8,128)S(1)}, f32[8,128]{1,0:T(8,128)S(1)}, u32[]{:S(2)}, u32[]{:S(2)}) collective-permute-start(f32[8,128]{1,0:T(8,128)S(1)} %get-tuple-element.18), channel_id=1, source_target_pairs={{0,12},{8,4},{16,0},{24,8},{28,16},{20,24},{12,28},{4,20},{1,13},{... | collective-permute-start | bytes 12296 | tf_op jit(solution)/shard_map/ppermute | solution.py:139
  46.1 7.3 %collective-permute-start.18 = (bf16[784,128]{1,0:T(8,128)(2,1)S(1)}, bf16[784,128]{1,0:T(8,128)(2,1)S(1)}, u32[]{:S(2)}, u32[]{:S(2)}) collective-permute-start(bf16[784,128]{1,0:T(8,128)(2,1)S(1)} %collective-permute-done.12.refs_0_), channel_id=1, source_target_pairs={{0,8},{8,16},{16,24},{24,28},{28,20},{20,12},{12,4},{4,0},{1,9},{9... | collective-permute-start | bytes 602120 | tf_op jit(solution)/shard_map/ppermute | solution.py:139
  46.5 7.1 %collective-permute-start.19 = (bf16[832,128]{1,0:T(8,128)(2,1)S(1)}, bf16[832,128]{1,0:T(8,128)(2,1)S(1)}, u32[]{:S(2)}, u32[]{:S(2)}) collective-permute-start(bf16[832,128]{1,0:T(8,128)(2,1)S(1)} %collective-permute-done.15.refs_3_), channel_id=1, source_target_pairs={{0,4},{8,0},{16,8},{24,16},{28,24},{20,28},{12,20},{4,12},{1,5},{9... | collective-permute-start | bytes 638984 | tf_op jit(solution)/shard_map/ppermute | solution.py:139
  53.4 15.3 %collective-permute-start.11 = (f32[8,128]{1,0:T(8,128)S(1)}, f32[8,128]{1,0:T(8,128)S(1)}, u32[]{:S(2)}, u32[]{:S(2)}) collective-permute-start(f32[8,128]{1,0:T(8,128)S(1)} %get-tuple-element.19), channel_id=1, source_target_pairs={{0,16},{8,24},{16,28},{24,20},{28,12},{20,4},{12,0},{4,8},{1,17},{... | collective-permute-start | bytes 12296 | tf_op jit(solution)/shard_map/ppermute | solution.py:139
  53.6 11.6 %slice-start.3 = ((s8[13107200]{0:T(1024)(128)(4,1)}), s8[4194304]{0:T(1024)(128)(4,1)S(1)}, s32[]{:S(2)}) async-start(s8[13107200]{0:T(1024)(128)(4,1)} %bitcast.6), calls=%async_computation.3 | async-start | bytes 8388608
  53.6 15.1 %collective-permute-start.16 = (f32[8,128]{1,0:T(8,128)S(1)}, f32[8,128]{1,0:T(8,128)S(1)}, u32[]{:S(2)}, u32[]{:S(2)}) collective-permute-start(f32[8,128]{1,0:T(8,128)S(1)} %get-tuple-element.20), channel_id=1, source_target_pairs={{0,20},{8,12},{16,4},{24,0},{28,8},{20,16},{12,24},{4,28},{1,21},{... | collective-permute-start | bytes 12296 | tf_op jit(solution)/shard_map/ppermute | solution.py:139
  60.3 8.5 %copy-start.7 = (f32[8,128]{1,0:T(8,128)}, f32[8,128]{1,0:T(8,128)S(1)}, u32[]{:S(2)}) copy-start(f32[8,128]{1,0:T(8,128)S(1)} %collective-permute-done.4.refs_1_) | copy-start | bytes 12292
  60.3 8.5 %collective-permute-start.17 = (f32[8,128]{1,0:T(8,128)S(1)}, f32[8,128]{1,0:T(8,128)S(1)}, u32[]{:S(2)}, u32[]{:S(2)}) collective-permute-start(f32[8,128]{1,0:T(8,128)S(1)} %get-tuple-element.21), channel_id=1, source_target_pairs={{0,24},{8,28},{16,20},{24,12},{28,4},{20,0},{12,8},{4,16},{1,25},{... | collective-permute-start | bytes 12296 | tf_op jit(solution)/shard_map/ppermute | solution.py:139
  60.4 8.4 %copy-start.8 = (f32[8,128]{1,0:T(8,128)}, f32[8,128]{1,0:T(8,128)S(1)}, u32[]{:S(2)}) copy-start(f32[8,128]{1,0:T(8,128)S(1)} %collective-permute-done.5.refs_2_) | copy-start | bytes 12292
  60.4 8.4 %collective-permute-start.20 = (f32[8,128]{1,0:T(8,128)S(1)}, f32[8,128]{1,0:T(8,128)S(1)}, u32[]{:S(2)}, u32[]{:S(2)}) collective-permute-start(f32[8,128]{1,0:T(8,128)S(1)} %wave1.3), channel_id=1, source_target_pairs={{0,28},{8,20},{16,12},{24,4},{28,0},{20,8},{12,16},{4,24},{1,29},{... | collective-permute-start | bytes 12296 | tf_op jit(solution)/shard_map/ppermute | solution.py:139
  68.1 0.6 copy-start.2
  68.7 0.6 copy-start.9
  68.7 0.6 copy-start.10
  68.7 0.6 copy-start.11
  68.8 0.6 copy-start.12
  68.8 0.6 copy-start.13

commit v2 on v1

v2 whole, which is shorter than its diff:
```python
import functools

import jax
import jax.numpy as jnp
from jax import lax
from jax.experimental import pallas as pl
from jax.experimental.pallas import tpu as pltpu
from jax.sharding import PartitionSpec as P

SEQ_LEN = 256
EPS = 1e-06
EXTRA = 16
BASE = 256
VMEM_LIMIT = 32 * 1024 * 1024
NORM_LIMIT = 60 * 1024 * 1024
FINAL_LIMIT = 4 * 1024 * 1024
CHUNK = 512
GROUP = 16

VMEM = pl.BlockSpec(memory_space=pltpu.VMEM)
ANY = pl.BlockSpec(memory_space=pl.ANY)


def norm_kernel(hidden_any, gain_any, targets_any, lengths_any, mask_any, block, valid, *scratch):
    hidden_t, gain, targets, lengths, mask, sems = scratch
    width, rows = hidden_t.shape
    copies = [
        pltpu.make_async_copy(src, dst, sems.at[i])
        for i, (src, dst) in enumerate(
            [
                (hidden_any, hidden_t),
                (gain_any, gain),
                (targets_any, targets),
                (lengths_any, lengths),
                (mask_any, mask),
            ]
        )
    ]
    for copy in copies:
        copy.start()
    for copy in copies:
        copy.wait()
    x = hidden_t[...].astype(jnp.float32)
    meansq = jnp.sum(x * x, axis=0, keepdims=True) * (1.0 / width)
    scale = lax.rsqrt(meansq + EPS)
    g = jnp.broadcast_to(gain[...].astype(jnp.float32).reshape(1, width), (rows, width)).T
    block[:width, :] = (x * scale * g).astype(jnp.bfloat16)
    ids = targets[...].reshape(1, rows)
    high = ids // BASE
    digit = lax.broadcasted_iota(jnp.int32, (EXTRA, rows), 0)
    digits = jnp.where(digit == 0, high, jnp.where(digit == 1, ids - high * BASE, 0))
    block[width:, :] = digits.astype(jnp.float32).astype(jnp.bfloat16)
    row = lax.axis_index("tp") * rows + lax.broadcasted_iota(jnp.int32, (1, rows), 1)
    length = jnp.zeros((1, rows), jnp.int32)
    for s in range(lengths.shape[0]):
        length = jnp.where(row // SEQ_LEN == s, lengths[s], length)
    live = (row % SEQ_LEN < length) & (mask[...].reshape(1, rows) == 1)
    valid[...] = live.astype(jnp.int32)


def final_kernel(count, valid, *refs):
    stats, (logprob, entropy) = refs[:count], refs[count:]
    tops = [s[0:1, :] for s in stats]
    top = functools.reduce(jnp.maximum, tops)
    sums = ent = tgt = jnp.zeros_like(top)
    for s, own in zip(stats, tops):
        delta = own - top
        scale = jnp.exp(delta)
        own_sums = s[1:2, :]
        sums = sums + own_sums * scale
        ent = ent + (s[2:3, :] + delta * own_sums) * scale
        tgt = tgt + s[3:4, :]
    log_total = jnp.log(sums)
    live = valid[...] == 1
    logprob[...] = jnp.where(live, tgt - (top + log_total), 0.0)
    entropy[...] = jnp.where(live, log_total - ent / sums, 0.0)


def unpack(blocks, x_scr, id_scr, vocab):
    width = x_scr.shape[1]
    start = lax.axis_index("tp") * vocab
    for b, pieces in enumerate(blocks):
        rows = pieces[0].shape[1]
        at = pl.ds(b * rows, rows)
        low = 0
        for piece in pieces:
            high = min(low + piece.shape[0], width)
            x_scr[at, low:high] = piece[: high - low, :].T
            if piece.shape[0] > high - low:
                digits = piece[high - low :, :]
            low = high
        digits = digits.astype(jnp.float32).T.astype(jnp.int32)
        id_scr[at, :] = digits[:, 0:1] * BASE + digits[:, 1:2] - start


def chunks_of(vocab):
    return [(lo, min(vocab, lo + CHUNK)) for lo in range(0, vocab, CHUNK)]


def update(logits, lo, id_scr, acc):
    top_s, sum_s, ent_s, tgt_s = acc
    rows, wide = logits.shape
    tail = wide % 128
    if tail:
        pad = jnp.full((rows, 128 - tail), -jnp.inf, jnp.float32)
        logits = jnp.concatenate([logits, pad], axis=1)
    lane = lax.broadcasted_iota(jnp.int32, (GROUP, 128), 1)
    count = logits.shape[1] // 128
    for g in range(rows // GROUP):
        at = pl.ds(g * GROUP, GROUP)
        cols = [
            logits[g * GROUP : (g + 1) * GROUP, k * 128 : (k + 1) * 128] for k in range(count)
        ]
        top = functools.reduce(jnp.maximum, cols)
        if lo == 0:
            sums = ent = tgt = jnp.zeros((GROUP, 128), jnp.float32)
        else:
            old = top_s[at, :]
            top = jnp.maximum(old, top)
            delta = old - top
            scale = jnp.exp(delta)
            old_sums = sum_s[at, :]
            sums = old_sums * scale
            ent = (ent_s[at, :] + delta * old_sums) * scale
            tgt = tgt_s[at, :]
        ids = id_scr[at, :] - lo
        for k, col in enumerate(cols):
            shifted = col - top
            expo = jnp.exp(shifted)
            weighted = expo * shifted
            hit = lane == ids - k * 128
            if tail and k == count - 1:
                real = lane < tail
                expo = jnp.where(real, expo, 0.0)
                weighted = jnp.where(real, weighted, 0.0)
                hit = hit & real
            sums = sums + expo
            ent = ent + weighted
            tgt = jnp.where(hit, col, tgt)
        top_s[at, :] = top
        sum_s[at, :] = sums
        ent_s[at, :] = ent
        tgt_s[at, :] = tgt


def collect(stats, acc):
    top_s, sum_s, ent_s, tgt_s = acc
    for b, out in enumerate(stats):
        rows = out.shape[1]
        at = pl.ds(b * rows, rows)
        tops = top_s[at, :].T
        sums = sum_s[at, :].T
        ents = ent_s[at, :].T
        top = jnp.max(tops, axis=0, keepdims=True)
        delta = tops - top
        scale = jnp.exp(delta)
        out[0:1, :] = top
        out[1:2, :] = jnp.sum(sums * scale, axis=0, keepdims=True)
        out[2:3, :] = jnp.sum((ents + delta * sums) * scale, axis=0, keepdims=True)
        out[3:4, :] = jnp.sum(tgt_s[at, :].T, axis=0, keepdims=True)
        out[4:8, :] = jnp.zeros((4, rows), jnp.float32)


def wave_kernel(counts, head, *refs):
    blocks = []
    for count in counts:
        blocks.append(refs[:count])
        refs = refs[count:]
    stats, (x_scr, id_scr, *acc) = refs[: len(counts)], refs[len(counts) :]
    vocab = head.shape[1]
    unpack(blocks, x_scr, id_scr, vocab)
    for lo, hi in chunks_of(vocab):
        logits = jnp.dot(x_scr[...], head[:, lo:hi], preferred_element_type=jnp.float32)
        update(logits, lo, id_scr, acc)
    collect(stats, acc)


def own_kernel(head_any, block, stats, head, x_scr, id_scr, *rest):
    acc, sems = rest[:4], rest[4]
    vocab = head.shape[1]
    rows = stats.shape[1]
    spans = chunks_of(vocab)
    copies = [
        pltpu.make_async_copy(head_any.at[:, lo:hi], head.at[:, lo:hi], sems.at[i])
        for i, (lo, hi) in enumerate(spans)
    ]
    for copy in copies:
        copy.start()
    unpack([[block]], x_scr, id_scr, vocab)
    for (lo, hi), copy in zip(spans, copies):
        copy.wait()
        logits = jnp.dot(x_scr[...], head[:, lo:hi], preferred_element_type=jnp.float32)
        update(logits, lo, id_scr, acc)
    collect([stats], acc)


def wave_scratch(count, rows, width):
    return [
        pltpu.VMEM((count * rows, width), jnp.bfloat16),
        pltpu.VMEM((count * rows, 1), jnp.int32),
    ] + [pltpu.VMEM((count * rows, 128), jnp.float32)] * 4


def cost(rows, width, vocab):
    return pl.CostEstimate(
        flops=2 * rows * width * vocab,
        bytes_accessed=2 * width * vocab,
        transcendentals=rows * vocab,
    )


def wave(head, blocks):
    counts = [len(pieces) for pieces in blocks]
    width, vocab = head.shape
    rows = blocks[0][0].shape[1]
    return pl.pallas_call(
        functools.partial(wave_kernel, counts),
        out_shape=[jax.ShapeDtypeStruct((8, rows), jnp.float32)] * len(blocks),
        in_specs=[VMEM] * (1 + sum(counts)),
        out_specs=[VMEM] * len(blocks),
        scratch_shapes=wave_scratch(len(blocks), rows, width),
        compiler_params=pltpu.CompilerParams(vmem_limit_bytes=VMEM_LIMIT),
        cost_estimate=cost(len(blocks) * rows, width, vocab),
        name=f"wave{len(blocks)}",
    )(head, *[piece for pieces in blocks for piece in pieces])


def on_device(n, hidden, gain, head, lengths, mask, targets):
    rows, width = hidden.shape
    vocab = head.shape[1]
    cut = (width // 2) // 128 * 128

    ring = list(range(0, n, 2)) + list(range(1, n, 2))[::-1]

    def hop(value, by):
        pairs = [(ring[i], ring[(i + by) % n]) for i in range(n)]
        return lax.ppermute(value, "tp", pairs)

    block, valid = pl.pallas_call(
        norm_kernel,
        out_shape=[
            jax.ShapeDtypeStruct((width + EXTRA, rows), jnp.bfloat16),
            jax.ShapeDtypeStruct((1, rows), jnp.int32),
        ],
        in_specs=[ANY] * 5,
        out_specs=[VMEM] * 2,
        scratch_shapes=[
            pltpu.VMEM((width, rows), jnp.bfloat16),
            pltpu.VMEM((width,), jnp.bfloat16),
            pltpu.VMEM((rows,), jnp.int32),
            pltpu.SMEM(lengths.shape, jnp.int32),
            pltpu.VMEM((rows,), jnp.int32),
            pltpu.SemaphoreType.DMA((5,)),
        ],
        compiler_params=pltpu.CompilerParams(vmem_limit_bytes=NORM_LIMIT),
        name="norm",
    )(hidden.T, gain, targets, lengths, mask)

    own, head_near = pl.pallas_call(
        own_kernel,
        out_shape=[
            jax.ShapeDtypeStruct((8, rows), jnp.float32),
            jax.ShapeDtypeStruct(head.shape, head.dtype),
        ],
        in_specs=[ANY, VMEM],
        out_specs=[VMEM] * 2,
        scratch_shapes=wave_scratch(1, rows, width)
        + [pltpu.SemaphoreType.DMA((len(chunks_of(vocab)),))],
        compiler_params=pltpu.CompilerParams(vmem_limit_bytes=VMEM_LIMIT),
        cost_estimate=cost(rows, width, vocab),
        name="own",
    )(head, block)

    stats = [own]
    full = (n - 1) // 2
    up, down = hop(block, 1), hop(block, -1)
    up, down, head_near = lax.optimization_barrier((up, down, head_near))
    for step in range(2, full + 1):
        next_up, next_down = hop(up, 1), hop(down, -1)
        mine = wave(head_near, [[up], [down]])
        up, down, *mine = lax.optimization_barrier((next_up, next_down, *mine))
        stats += [hop(mine[0], 1 - step), hop(mine[1], step - 1)]
    if n % 2:
        mine = wave(head_near, [[up], [down]])
        stats += [hop(mine[0], -full), hop(mine[1], full)]
    else:
        halves = [hop(up[:cut], 1), hop(down[cut:], -1)]
        mine = wave(head_near, [[up], [down]])
        stats += [hop(mine[0], -full), hop(mine[1], full)]
        (far,) = wave(head_near, [halves])
        stats.append(hop(far, n // 2))

    logprob, entropy = pl.pallas_call(
        functools.partial(final_kernel, n),
        out_shape=[jax.ShapeDtypeStruct((1, rows), jnp.float32)] * 2,
        in_specs=[VMEM] * (n + 1),
        out_specs=[VMEM] * 2,
        compiler_params=pltpu.CompilerParams(vmem_limit_bytes=FINAL_LIMIT),
        name="combine",
    )(valid, *stats)
    return logprob.reshape(rows), entropy.reshape(rows)


def solution(mesh):
    return jax.shard_map(
        functools.partial(on_device, mesh.shape["tp"]),
        mesh=mesh,
        in_specs=(
            P(("dp", "tp"), None),
            P(),
            P(None, "tp"),
            P("dp"),
            P(("dp", "tp")),
            P(("dp", "tp")),
        ),
        out_specs=(P(("dp", "tp")), P(("dp", "tp"))),
        check_vma=False,
    )
```

time: 70.9 us -> 61.8 us (0.87)
  local copies, waits for them, and re-layouts: 9.59 us -> 1.07 us
  starting transfers between devices: 29 us -> 22 us
  waiting for transfers between devices: 7.49 us -> 12 us
  Pallas kernels: 23.8 us -> 25.8 us
    unnamed x36 -> x4, local copies, waits for them, and re-layouts: 8.9 us -> 1.04 us
    ppermute x21 -> x15, starting transfers between devices: 29 us -> 22 us  [hop(): return lax.ppermute(value, 'tp', pairs)]
    ppermute x21 -> x15, waiting for transfers between devices: 7.49 us -> 12 us  [hop(): return lax.ppermute(value, 'tp', pairs)]
    pallas_call x6, Pallas kernels: 22.5 us -> 25.3 us  [the longest x4 17.5 us: wave(): pl.pallas_call(functools.partial(wave_kernel, counts), out_shape=[jax.Sha...]
    pallas_call x1, Pallas kernels: 1.28 us -> 0.55 us  [on_device(): pl.pallas_call(functools.partial(final_kernel, n), out_shape=[jax.ShapeDt...]
  transfers between devices with their start and end apart: 21 -> 15, of which waited for: 1 -> 7; matrix products, arithmetic and copies ran while one was open for 0% -> 0% of each run, Pallas kernels for 31% -> 37%
where the time goes in v2:
time: 61.8 us; the launch traced here: 61.7 us
  Pallas kernels  25.8 us (42%)
  starting transfers between devices  22 us (36%)
  waiting for transfers between devices  12 us (19%)
  local copies, waits for them, and re-layouts  1.07 us (2%)
  between operations  0.71 us (1%)
    ppermute x15, starting transfers between devices, hop(): return lax.ppermute(value, 'tp', pairs)  22 us
    pallas_call x4, Pallas kernels, wave(): pl.pallas_call(functools.partial(wave_kernel, counts), out_shape=[jax.Sha...  17.5 us
    ppermute x15, waiting for transfers between devices, hop(): return lax.ppermute(value, 'tp', pairs)  12 us
    pallas_call x1, Pallas kernels, on_device(): pl.pallas_call(own_kernel, out_shape=[jax.ShapeDtypeStruct((8, rows), jnp...  5.62 us
    pallas_call x1, Pallas kernels, on_device(): pl.pallas_call(norm_kernel, out_shape=[jax.ShapeDtypeStruct((width + EXTR...  2.17 us
  transfers between devices with their start and end apart: 15, of which 7 were waited for; matrix products, arithmetic and copies ran while one was open for 0% of the time, Pallas kernels for 37%

profile of v2, /device:TPU:0, one launch (start us, length us, event | category | flops | bytes accessed | tf_op | source)
XLA Modules:
  0.0 61.7 jit_solution(11265018768044928406)
XLA Ops:
  0.6 2.2 %norm.1 = (bf16[1616,128]{1,0:T(8,128)(2,1)}, s32[1,128]{1,0:T(1,128)}) custom-call(bf16[1600,128]{1,0:T(8,128)(2,1)} %bitcast.3, bf16[1600]{0:T(1024)(128)(2,1)} %gain_any.1, s32[128]{0:T(128)} %targets_any.1, s32[4]{0:T(128)} %lengths_any.1, s32[128]{0:T(128)} %mask_any.1), custom_call_target="tpu_custom_call" | custom-call | tf_op jit(solution)/shard_map/norm/pallas_call | solution.py:239
  2.8 3.0 %collective-permute-start.1 = (bf16[1616,128]{1,0:T(8,128)(2,1)}, bf16[1616,128]{1,0:T(8,128)(2,1)S(1)}, u32[]{:S(2)}, u32[]{:S(2)}) collective-permute-start(bf16[1616,128]{1,0:T(8,128)(2,1)} %get-tuple-element.26.block), channel_id=1, source_target_pairs={{0,4},{8,0},{16,8},{24,16},{28,24},{20,28},{12,20},{4,12},{1,5},{9... | collective-permute-start | bytes 1241096 | tf_op jit(solution)/shard_map/ppermute | solution.py:237
  5.8 0.1 collective-permute-start
  5.9 0.0 copy-start
  5.9 1.0 %copy-done = bf16[1616,128]{1,0:T(8,128)(2,1)S(1)} copy-done((bf16[1616,128]{1,0:T(8,128)(2,1)S(1)}, bf16[1616,128]{1,0:T(8,128)(2,1)}, u32[]{:S(2)}) %copy-start) | copy-done | bytes 413720
  7.0 5.6 %own.1 = (f32[8,128]{1,0:T(8,128)S(1)}, bf16[1600,4000]{1,0:T(8,128)(2,1)S(1)}) custom-call(bf16[1600,4000]{1,0:T(8,128)(2,1)} %head_any.1, bf16[1616,128]{1,0:T(8,128)(2,1)S(1)} %copy-done), custom_call_target="tpu_custom_call" | custom-call | flops 1638400000 | bytes 12800000 | tf_op jit(solution)/shard_map/own/pallas_call | solution.py:259
  12.6 3.0 %collective-permute-done.1.refs_1_ = bf16[1616,128]{1,0:T(8,128)(2,1)S(1)} collective-permute-done((bf16[1616,128]{1,0:T(8,128)(2,1)}, bf16[1616,128]{1,0:T(8,128)(2,1)S(1)}, u32[]{:S(2)}, u32[]{:S(2)}) %collective-permute-start.1) | collective-permute-done | bytes 413728 | tf_op jit(solution)/shard_map/ppermute | solution.py:237
  15.6 1.4 %collective-permute-done.refs_0_ = bf16[1616,128]{1,0:T(8,128)(2,1)S(1)} collective-permute-done((bf16[1616,128]{1,0:T(8,128)(2,1)}, bf16[1616,128]{1,0:T(8,128)(2,1)S(1)}, u32[]{:S(2)}, u32[]{:S(2)}) %collective-permute-start) | collective-permute-done | bytes 413728 | tf_op jit(solution)/shard_map/ppermute | solution.py:237
  17.0 0.4 collective-permute-start.2
  17.4 1.6 %collective-permute-start.3 = (bf16[1616,128]{1,0:T(8,128)(2,1)S(1)}, bf16[1616,128]{1,0:T(8,128)(2,1)S(1)}, u32[]{:S(2)}, u32[]{:S(2)}) collective-permute-start(bf16[1616,128]{1,0:T(8,128)(2,1)S(1)} %collective-permute-done.1.refs_1_), channel_id=1, source_target_pairs={{0,4},{8,0},{16,8},{24,16},{28,24},{20,28},{12,20},{4,12},{1,5},{9... | collective-permute-start | bytes 1241096 | tf_op jit(solution)/shard_map/ppermute | solution.py:237
  19.0 4.9 %wave2.3 = (f32[8,128]{1,0:T(8,128)S(1)}, f32[8,128]{1,0:T(8,128)S(1)}) custom-call(bf16[1600,4000]{1,0:T(8,128)(2,1)S(1)} %get-tuple-element.31.head, bf16[1616,128]{1,0:T(8,128)(2,1)S(1)} %collective-permute-done.refs_0_, bf16[1616,128]{1,0:T(8,128)(2,1)S(1)} %collective-permute-done.1.refs_1_), custom_call_target="tpu_custom_call" | custom-call | flops 3276800000 | bytes 12800000 | tf_op jit(solution)/shard_map/wave2/pallas_call | solution.py:216
  23.9 3.2 %collective-permute-done.2.refs_0_ = bf16[1616,128]{1,0:T(8,128)(2,1)S(1)} collective-permute-done((bf16[1616,128]{1,0:T(8,128)(2,1)S(1)}, bf16[1616,128]{1,0:T(8,128)(2,1)S(1)}, u32[]{:S(2)}, u32[]{:S(2)}) %collective-permute-start.2) | collective-permute-done | bytes 413728 | tf_op jit(solution)/shard_map/ppermute | solution.py:237
  27.1 0.5 collective-permute-done.3.refs_1_
  27.6 1.5 %collective-permute-start.6 = (bf16[1616,128]{1,0:T(8,128)(2,1)S(1)}, bf16[1616,128]{1,0:T(8,128)(2,1)S(1)}, u32[]{:S(2)}, u32[]{:S(2)}) collective-permute-start(bf16[1616,128]{1,0:T(8,128)(2,1)S(1)} %collective-permute-done.2.refs_0_), channel_id=1, source_target_pairs={{0,8},{8,16},{16,24},{24,28},{28,20},{20,12},{12,4},{4,0},{1,9},{9... | collective-permute-start | bytes 1241096 | tf_op jit(solution)/shard_map/ppermute | solution.py:237
  29.1 0.5 collective-permute-start.7
  29.6 1.3 %collective-permute-start.4 = (f32[8,128]{1,0:T(8,128)S(1)}, f32[8,128]{1,0:T(8,128)S(1)}, u32[]{:S(2)}, u32[]{:S(2)}) collective-permute-start(f32[8,128]{1,0:T(8,128)S(1)} %get-tuple-element.34), channel_id=1, source_target_pairs={{0,4},{8,0},{16,8},{24,16},{28,24},{20,28},{12,20},{4,12},{1,5},{9... | collective-permute-start | bytes 12296 | tf_op jit(solution)/shard_map/ppermute | solution.py:237
  30.9 0.7 %collective-permute-start.5 = (f32[8,128]{1,0:T(8,128)S(1)}, f32[8,128]{1,0:T(8,128)S(1)}, u32[]{:S(2)}, u32[]{:S(2)}) collective-permute-start(f32[8,128]{1,0:T(8,128)S(1)} %get-tuple-element.35), channel_id=1, source_target_pairs={{0,8},{8,16},{16,24},{24,28},{28,20},{20,12},{12,4},{4,0},{1,9},{9... | collective-permute-start | bytes 12296 | tf_op jit(solution)/shard_map/ppermute | solution.py:237
  31.6 4.9 %wave2.4 = (f32[8,128]{1,0:T(8,128)S(1)}, f32[8,128]{1,0:T(8,128)S(1)}) custom-call(bf16[1600,4000]{1,0:T(8,128)(2,1)S(1)} %get-tuple-element.31.head, bf16[1616,128]{1,0:T(8,128)(2,1)S(1)} %collective-permute-done.2.refs_0_, bf16[1616,128]{1,0:T(8,128)(2,1)S(1)} %collective-permute-done.3.refs_1_), custom_call_target="tpu_custom_call" | custom-call | flops 3276800000 | bytes 12800000 | tf_op jit(solution)/shard_map/wave2/pallas_call | solution.py:216
  36.5 0.3 collective-permute-done.6.refs_0_
  36.9 1.1 %collective-permute-done.7.refs_1_ = bf16[1616,128]{1,0:T(8,128)(2,1)S(1)} collective-permute-done((bf16[1616,128]{1,0:T(8,128)(2,1)S(1)}, bf16[1616,128]{1,0:T(8,128)(2,1)S(1)}, u32[]{:S(2)}, u32[]{:S(2)}) %collective-permute-start.7) | collective-permute-done | bytes 413728 | tf_op jit(solution)/shard_map/ppermute | solution.py:237
  38.0 0.0 copy-start.1
  38.0 1.6 %collective-permute-start.12 = (bf16[768,128]{1,0:T(8,128)(2,1)S(1)}, bf16[768,128]{1,0:T(8,128)(2,1)S(1)}, u32[]{:S(2)}, u32[]{:S(2)}) collective-permute-start(bf16[768,128]{1,0:T(8,128)(2,1)S(1)} %slice.6), channel_id=1, source_target_pairs={{0,8},{8,16},{16,24},{24,28},{28,20},{20,12},{12,4},{4,0},{1,9},{9... | collective-permute-start | bytes 589832 | tf_op jit(solution)/shard_map/ppermute | solution.py:237
  39.6 0.5 collective-permute-start.13
  40.1 4.9 %wave2.5 = (f32[8,128]{1,0:T(8,128)S(1)}, f32[8,128]{1,0:T(8,128)S(1)}) custom-call(bf16[1600,4000]{1,0:T(8,128)(2,1)S(1)} %get-tuple-element.31.head, bf16[1616,128]{1,0:T(8,128)(2,1)S(1)} %collective-permute-done.6.refs_0_, bf16[1616,128]{1,0:T(8,128)(2,1)S(1)} %collective-permute-done.7.refs_1_), custom_call_target="tpu_custom_call" | custom-call | flops 3276800000 | bytes 12800000 | tf_op jit(solution)/shard_map/wave2/pallas_call | solution.py:216
  44.9 2.9 %collective-permute-start.10 = (f32[8,128]{1,0:T(8,128)S(1)}, f32[8,128]{1,0:T(8,128)S(1)}, u32[]{:S(2)}, u32[]{:S(2)}) collective-permute-start(f32[8,128]{1,0:T(8,128)S(1)} %get-tuple-element.44), channel_id=1, source_target_pairs={{0,20},{8,12},{16,4},{24,0},{28,8},{20,16},{12,24},{4,28},{1,21},{... | collective-permute-start | bytes 12296 | tf_op jit(solution)/shard_map/ppermute | solution.py:237
  47.8 0.0 collective-permute-done.12.refs_0_
  47.8 1.1 %collective-permute-start.11 = (f32[8,128]{1,0:T(8,128)S(1)}, f32[8,128]{1,0:T(8,128)S(1)}, u32[]{:S(2)}, u32[]{:S(2)}) collective-permute-start(f32[8,128]{1,0:T(8,128)S(1)} %get-tuple-element.45), channel_id=1, source_target_pairs={{0,24},{8,28},{16,20},{24,12},{28,4},{20,0},{12,8},{4,16},{1,25},{... | collective-permute-start | bytes 12296 | tf_op jit(solution)/shard_map/ppermute | solution.py:237
  48.9 0.0 collective-permute-done.13.refs_1_
  48.9 1.4 %collective-permute-start.8 = (f32[8,128]{1,0:T(8,128)S(1)}, f32[8,128]{1,0:T(8,128)S(1)}, u32[]{:S(2)}, u32[]{:S(2)}) collective-permute-start(f32[8,128]{1,0:T(8,128)S(1)} %get-tuple-element.40), channel_id=1, source_target_pairs={{0,12},{8,4},{16,0},{24,8},{28,16},{20,24},{12,28},{4,20},{1,13},{... | collective-permute-start | bytes 12296 | tf_op jit(solution)/shard_map/ppermute | solution.py:237
  50.3 2.9 %wave1.1 = f32[8,128]{1,0:T(8,128)S(1)} custom-call(bf16[1600,4000]{1,0:T(8,128)(2,1)S(1)} %get-tuple-element.31.head, bf16[768,128]{1,0:T(8,128)(2,1)S(1)} %collective-permute-done.12.refs_0_, bf16[848,128]{1,0:T(8,128)(2,1)S(1)} %collective-permute-done.13.refs_1_), custom_call_target="tpu_custom_call" | custom-call | flops 1638400000 | bytes 12800000 | tf_op jit(solution)/shard_map/wave1/pallas_call | solution.py:216
  53.2 0.0 collective-permute-done.4.refs_1_
  53.3 1.5 %collective-permute-start.9 = (f32[8,128]{1,0:T(8,128)S(1)}, f32[8,128]{1,0:T(8,128)S(1)}, u32[]{:S(2)}, u32[]{:S(2)}) collective-permute-start(f32[8,128]{1,0:T(8,128)S(1)} %get-tuple-element.41), channel_id=1, source_target_pairs={{0,16},{8,24},{16,28},{24,20},{28,12},{20,4},{12,0},{4,8},{1,17},{... | collective-permute-start | bytes 12296 | tf_op jit(solution)/shard_map/ppermute | solution.py:237
  54.8 0.0 collective-permute-done.5.refs_2_
  54.8 3.8 %collective-permute-start.14 = (f32[8,128]{1,0:T(8,128)S(1)}, f32[8,128]{1,0:T(8,128)S(1)}, u32[]{:S(2)}, u32[]{:S(2)}) collective-permute-start(f32[8,128]{1,0:T(8,128)S(1)} %wave1.1), channel_id=1, source_target_pairs={{0,28},{8,20},{16,12},{24,4},{28,0},{20,8},{12,16},{4,24},{1,29},{... | collective-permute-start | bytes 12296 | tf_op jit(solution)/shard_map/ppermute | solution.py:237
  58.6 0.0 collective-permute-done.10.refs_5_
  58.6 0.0 collective-permute-done.11.refs_6_
  58.6 0.0 collective-permute-done.8.refs_3_
  58.6 0.0 collective-permute-done.9.refs_4_
  58.6 2.5 %collective-permute-done.14.refs_7_ = f32[8,128]{1,0:T(8,128)S(1)} collective-permute-done((f32[8,128]{1,0:T(8,128)S(1)}, f32[8,128]{1,0:T(8,128)S(1)}, u32[]{:S(2)}, u32[]{:S(2)}) %collective-permute-start.14) | collective-permute-done | bytes 4128 | tf_op jit(solution)/shard_map/ppermute | solution.py:237
  61.1 0.0 copy-done.1
  61.1 0.6 combine.1
  (2 shorter events, 0.0 us)
Async XLA Ops:
  2.8 12.8 %collective-permute-start.1 = (bf16[1616,128]{1,0:T(8,128)(2,1)}, bf16[1616,128]{1,0:T(8,128)(2,1)S(1)}, u32[]{:S(2)}, u32[]{:S(2)}) collective-permute-start(bf16[1616,128]{1,0:T(8,128)(2,1)} %get-tuple-element.26.block), channel_id=1, source_target_pairs={{0,4},{8,0},{16,8},{24,16},{28,24},{20,28},{12,20},{4,12},{1,5},{9... | collective-permute-start | bytes 1241096 | tf_op jit(solution)/shard_map/ppermute | solution.py:237
  5.8 11.2 %collective-permute-start = (bf16[1616,128]{1,0:T(8,128)(2,1)}, bf16[1616,128]{1,0:T(8,128)(2,1)S(1)}, u32[]{:S(2)}, u32[]{:S(2)}) collective-permute-start(bf16[1616,128]{1,0:T(8,128)(2,1)} %get-tuple-element.26.block), channel_id=1, source_target_pairs={{0,8},{8,16},{16,24},{24,28},{28,20},{20,12},{12,4},{4,0},{1,9},{9... | collective-permute-start | bytes 1241096 | tf_op jit(solution)/shard_map/ppermute | solution.py:237
  5.9 1.0 %copy-start = (bf16[1616,128]{1,0:T(8,128)(2,1)S(1)}, bf16[1616,128]{1,0:T(8,128)(2,1)}, u32[]{:S(2)}) copy-start(bf16[1616,128]{1,0:T(8,128)(2,1)} %get-tuple-element.26.block) | copy-start | bytes 1241092
  17.0 10.1 %collective-permute-start.2 = (bf16[1616,128]{1,0:T(8,128)(2,1)S(1)}, bf16[1616,128]{1,0:T(8,128)(2,1)S(1)}, u32[]{:S(2)}, u32[]{:S(2)}) collective-permute-start(bf16[1616,128]{1,0:T(8,128)(2,1)S(1)} %collective-permute-done.refs_0_), channel_id=1, source_target_pairs={{0,8},{8,16},{16,24},{24,28},{28,20},{20,12},{12,4},{4,0},{1,9},{9... | collective-permute-start | bytes 1241096 | tf_op jit(solution)/shard_map/ppermute | solution.py:237
  17.4 10.1 %collective-permute-start.3 = (bf16[1616,128]{1,0:T(8,128)(2,1)S(1)}, bf16[1616,128]{1,0:T(8,128)(2,1)S(1)}, u32[]{:S(2)}, u32[]{:S(2)}) collective-permute-start(bf16[1616,128]{1,0:T(8,128)(2,1)S(1)} %collective-permute-done.1.refs_1_), channel_id=1, source_target_pairs={{0,4},{8,0},{16,8},{24,16},{28,24},{20,28},{12,20},{4,12},{1,5},{9... | collective-permute-start | bytes 1241096 | tf_op jit(solution)/shard_map/ppermute | solution.py:237
  27.6 9.3 %collective-permute-start.6 = (bf16[1616,128]{1,0:T(8,128)(2,1)S(1)}, bf16[1616,128]{1,0:T(8,128)(2,1)S(1)}, u32[]{:S(2)}, u32[]{:S(2)}) collective-permute-start(bf16[1616,128]{1,0:T(8,128)(2,1)S(1)} %collective-permute-done.2.refs_0_), channel_id=1, source_target_pairs={{0,8},{8,16},{16,24},{24,28},{28,20},{20,12},{12,4},{4,0},{1,9},{9... | collective-permute-start | bytes 1241096 | tf_op jit(solution)/shard_map/ppermute | solution.py:237
  29.1 8.8 %collective-permute-start.7 = (bf16[1616,128]{1,0:T(8,128)(2,1)S(1)}, bf16[1616,128]{1,0:T(8,128)(2,1)S(1)}, u32[]{:S(2)}, u32[]{:S(2)}) collective-permute-start(bf16[1616,128]{1,0:T(8,128)(2,1)S(1)} %collective-permute-done.3.refs_1_), channel_id=1, source_target_pairs={{0,4},{8,0},{16,8},{24,16},{28,24},{20,28},{12,20},{4,12},{1,5},{9... | collective-permute-start | bytes 1241096 | tf_op jit(solution)/shard_map/ppermute | solution.py:237
  29.6 23.6 %collective-permute-start.4 = (f32[8,128]{1,0:T(8,128)S(1)}, f32[8,128]{1,0:T(8,128)S(1)}, u32[]{:S(2)}, u32[]{:S(2)}) collective-permute-start(f32[8,128]{1,0:T(8,128)S(1)} %get-tuple-element.34), channel_id=1, source_target_pairs={{0,4},{8,0},{16,8},{24,16},{28,24},{20,28},{12,20},{4,12},{1,5},{9... | collective-permute-start | bytes 12296 | tf_op jit(solution)/shard_map/ppermute | solution.py:237
  30.9 23.9 %collective-permute-start.5 = (f32[8,128]{1,0:T(8,128)S(1)}, f32[8,128]{1,0:T(8,128)S(1)}, u32[]{:S(2)}, u32[]{:S(2)}) collective-permute-start(f32[8,128]{1,0:T(8,128)S(1)} %get-tuple-element.35), channel_id=1, source_target_pairs={{0,8},{8,16},{16,24},{24,28},{28,20},{20,12},{12,4},{4,0},{1,9},{9... | collective-permute-start | bytes 12296 | tf_op jit(solution)/shard_map/ppermute | solution.py:237
  38.0 23.1 %copy-start.1 = (s32[1,128]{1,0:T(1,128)S(1)}, s32[1,128]{1,0:T(1,128)}, u32[]{:S(2)}) copy-start(s32[1,128]{1,0:T(1,128)} %get-tuple-element.25.valid) | copy-start | bytes 1540
  38.0 9.8 %collective-permute-start.12 = (bf16[768,128]{1,0:T(8,128)(2,1)S(1)}, bf16[768,128]{1,0:T(8,128)(2,1)S(1)}, u32[]{:S(2)}, u32[]{:S(2)}) collective-permute-start(bf16[768,128]{1,0:T(8,128)(2,1)S(1)} %slice.6), channel_id=1, source_target_pairs={{0,8},{8,16},{16,24},{24,28},{28,20},{20,12},{12,4},{4,0},{1,9},{9... | collective-permute-start | bytes 589832 | tf_op jit(solution)/shard_map/ppermute | solution.py:237
  39.6 9.3 %collective-permute-start.13 = (bf16[848,128]{1,0:T(8,128)(2,1)S(1)}, bf16[848,128]{1,0:T(8,128)(2,1)S(1)}, u32[]{:S(2)}, u32[]{:S(2)}) collective-permute-start(bf16[848,128]{1,0:T(8,128)(2,1)S(1)} %slice.7), channel_id=1, source_target_pairs={{0,4},{8,0},{16,8},{24,16},{28,24},{20,28},{12,20},{4,12},{1,5},{9... | collective-permute-start | bytes 651272 | tf_op jit(solution)/shard_map/ppermute | solution.py:237
  44.9 13.6 %collective-permute-start.10 = (f32[8,128]{1,0:T(8,128)S(1)}, f32[8,128]{1,0:T(8,128)S(1)}, u32[]{:S(2)}, u32[]{:S(2)}) collective-permute-start(f32[8,128]{1,0:T(8,128)S(1)} %get-tuple-element.44), channel_id=1, source_target_pairs={{0,20},{8,12},{16,4},{24,0},{28,8},{20,16},{12,24},{4,28},{1,21},{... | collective-permute-start | bytes 12296 | tf_op jit(solution)/shard_map/ppermute | solution.py:237
  47.8 10.8 %collective-permute-start.11 = (f32[8,128]{1,0:T(8,128)S(1)}, f32[8,128]{1,0:T(8,128)S(1)}, u32[]{:S(2)}, u32[]{:S(2)}) collective-permute-start(f32[8,128]{1,0:T(8,128)S(1)} %get-tuple-element.45), channel_id=1, source_target_pairs={{0,24},{8,28},{16,20},{24,12},{28,4},{20,0},{12,8},{4,16},{1,25},{... | collective-permute-start | bytes 12296 | tf_op jit(solution)/shard_map/ppermute | solution.py:237
  48.9 9.7 %collective-permute-start.8 = (f32[8,128]{1,0:T(8,128)S(1)}, f32[8,128]{1,0:T(8,128)S(1)}, u32[]{:S(2)}, u32[]{:S(2)}) collective-permute-start(f32[8,128]{1,0:T(8,128)S(1)} %get-tuple-element.40), channel_id=1, source_target_pairs={{0,12},{8,4},{16,0},{24,8},{28,16},{20,24},{12,28},{4,20},{1,13},{... | collective-permute-start | bytes 12296 | tf_op jit(solution)/shard_map/ppermute | solution.py:237
  53.3 5.3 %collective-permute-start.9 = (f32[8,128]{1,0:T(8,128)S(1)}, f32[8,128]{1,0:T(8,128)S(1)}, u32[]{:S(2)}, u32[]{:S(2)}) collective-permute-start(f32[8,128]{1,0:T(8,128)S(1)} %get-tuple-element.41), channel_id=1, source_target_pairs={{0,16},{8,24},{16,28},{24,20},{28,12},{20,4},{12,0},{4,8},{1,17},{... | collective-permute-start | bytes 12296 | tf_op jit(solution)/shard_map/ppermute | solution.py:237
  54.8 6.3 %collective-permute-start.14 = (f32[8,128]{1,0:T(8,128)S(1)}, f32[8,128]{1,0:T(8,128)S(1)}, u32[]{:S(2)}, u32[]{:S(2)}) collective-permute-start(f32[8,128]{1,0:T(8,128)S(1)} %wave1.1), channel_id=1, source_target_pairs={{0,28},{8,20},{16,12},{24,4},{28,0},{20,8},{12,16},{4,24},{1,29},{... | collective-permute-start | bytes 12296 | tf_op jit(solution)/shard_map/ppermute | solution.py:237

commit v3 on v2

--- a/solution.py
+++ b/solution.py
@@ -12,7 +12,7 @@
 EXTRA = 16
 BASE = 256
 VMEM_LIMIT = 32 * 1024 * 1024
-NORM_LIMIT = 60 * 1024 * 1024
+NORM_LIMIT = 16 * 1024 * 1024
 FINAL_LIMIT = 4 * 1024 * 1024
 CHUNK = 512
 GROUP = 16
@@ -21,7 +21,7 @@
 ANY = pl.BlockSpec(memory_space=pl.ANY)
 
 
-def norm_kernel(hidden_any, gain_any, targets_any, lengths_any, mask_any, block, valid, *scratch):
+def norm_kernel(hidden_any, gain_any, targets_any, lengths_any, mask_any, first, second, valid, *scratch):
     hidden_t, gain, targets, lengths, mask, sems = scratch
     width, rows = hidden_t.shape
     copies = [
@@ -44,36 +44,21 @@
     meansq = jnp.sum(x * x, axis=0, keepdims=True) * (1.0 / width)
     scale = lax.rsqrt(meansq + EPS)
     g = jnp.broadcast_to(gain[...].astype(jnp.float32).reshape(1, width), (rows, width)).T
-    block[:width, :] = (x * scale * g).astype(jnp.bfloat16)
+    normed = (x * scale * g).astype(jnp.bfloat16)
+    cut = first.shape[0]
+    first[...] = normed[:cut]
+    second[: width - cut, :] = normed[cut:]
     ids = targets[...].reshape(1, rows)
     high = ids // BASE
     digit = lax.broadcasted_iota(jnp.int32, (EXTRA, rows), 0)
     digits = jnp.where(digit == 0, high, jnp.where(digit == 1, ids - high * BASE, 0))
-    block[width:, :] = digits.astype(jnp.float32).astype(jnp.bfloat16)
+    second[width - cut :, :] = digits.astype(jnp.float32).astype(jnp.bfloat16)
     row = lax.axis_index("tp") * rows + lax.broadcasted_iota(jnp.int32, (1, rows), 1)
     length = jnp.zeros((1, rows), jnp.int32)
     for s in range(lengths.shape[0]):
         length = jnp.where(row // SEQ_LEN == s, lengths[s], length)
     live = (row % SEQ_LEN < length) & (mask[...].reshape(1, rows) == 1)
     valid[...] = live.astype(jnp.int32)
-
-
-def final_kernel(count, valid, *refs):
-    stats, (logprob, entropy) = refs[:count], refs[count:]
-    tops = [s[0:1, :] for s in stats]
-    top = functools.reduce(jnp.maximum, tops)
-    sums = ent = tgt = jnp.zeros_like(top)
-    for s, own in zip(stats, tops):
-        delta = own - top
-        scale = jnp.exp(delta)
-        own_sums = s[1:2, :]
-        sums = sums + own_sums * scale
-        ent = ent + (s[2:3, :] + delta * own_sums) * scale
-        tgt = tgt + s[3:4, :]
-    log_total = jnp.log(sums)
-    live = valid[...] == 1
-    logprob[...] = jnp.where(live, tgt - (top + log_total), 0.0)
-    entropy[...] = jnp.where(live, log_total - ent / sums, 0.0)
 
 
 def unpack(blocks, x_scr, id_scr, vocab):
@@ -175,7 +160,23 @@
     collect(stats, acc)
 
 
-def own_kernel(head_any, block, stats, head, x_scr, id_scr, *rest):
+def last_wave_kernel(n, away, head, first, second, *refs):
+    count = len(away)
+    found, table, scratch = refs[:count], refs[count], refs[count + 1 :]
+    wave_kernel([2], head, first, second, table.at[owner(n, n // 2)], *scratch)
+    for places, stats in zip(away, found):
+        table[owner(n, places)] = stats[...]
+
+
+def owner(n, places):
+    me = lax.axis_index("tp")
+    half = (n + 1) // 2
+    here = jnp.where(me % 2 == 0, me // 2, n - 1 - me // 2)
+    there = (here + places + n) % n
+    return jnp.where(there < half, 2 * there, 2 * (n - 1 - there) + 1)
+
+
+def own_kernel(head_any, first, second, stats, head, x_scr, id_scr, *rest):
     acc, sems = rest[:4], rest[4]
     vocab = head.shape[1]
     rows = stats.shape[1]
@@ -186,12 +187,30 @@
     ]
     for copy in copies:
         copy.start()
-    unpack([[block]], x_scr, id_scr, vocab)
+    unpack([[first, second]], x_scr, id_scr, vocab)
     for (lo, hi), copy in zip(spans, copies):
         copy.wait()
         logits = jnp.dot(x_scr[...], head[:, lo:hi], preferred_element_type=jnp.float32)
         update(logits, lo, id_scr, acc)
     collect([stats], acc)
+
+
+def final_kernel(valid, shares, logprob, entropy):
+    stats = [shares[i] for i in range(shares.shape[0])]
+    tops = [s[0:1, :] for s in stats]
+    top = functools.reduce(jnp.maximum, tops)
+    sums = ent = tgt = jnp.zeros_like(top)
+    for s, own in zip(stats, tops):
+        delta = own - top
+        scale = jnp.exp(delta)
+        own_sums = s[1:2, :]
+        sums = sums + own_sums * scale
+        ent = ent + (s[2:3, :] + delta * own_sums) * scale
+        tgt = tgt + s[3:4, :]
+    log_total = jnp.log(sums)
+    live = valid[...] == 1
+    logprob[...] = jnp.where(live, tgt - (top + log_total), 0.0)
+    entropy[...] = jnp.where(live, log_total - ent / sums, 0.0)
 
 
 def wave_scratch(count, rows, width):
@@ -225,6 +244,25 @@
     )(head, *[piece for pieces in blocks for piece in pieces])
 
 
+def last_wave(n, head, pieces, found):
+    width, vocab = head.shape
+    rows = pieces[0].shape[1]
+    return pl.pallas_call(
+        functools.partial(last_wave_kernel, n, list(found)),
+        out_shape=jax.ShapeDtypeStruct((n, 8, rows), jnp.float32),
+        in_specs=[VMEM] * (3 + len(found)),
+        out_specs=VMEM,
+        scratch_shapes=wave_scratch(1, rows, width),
+        compiler_params=pltpu.CompilerParams(vmem_limit_bytes=VMEM_LIMIT),
+        cost_estimate=cost(rows, width, vocab),
+        name="last",
+    )(head, *pieces, *found.values())
+
+
+def in_hbm(x):
+    return pltpu.with_memory_space_constraint(x, pltpu.HBM)
+
+
 def on_device(n, hidden, gain, head, lengths, mask, targets):
     rows, width = hidden.shape
     vocab = head.shape[1]
@@ -236,14 +274,15 @@
         pairs = [(ring[i], ring[(i + by) % n]) for i in range(n)]
         return lax.ppermute(value, "tp", pairs)
 
-    block, valid = pl.pallas_call(
+    *block, valid = pl.pallas_call(
         norm_kernel,
         out_shape=[
-            jax.ShapeDtypeStruct((width + EXTRA, rows), jnp.bfloat16),
+            jax.ShapeDtypeStruct((cut, rows), jnp.bfloat16),
+            jax.ShapeDtypeStruct((width - cut + EXTRA, rows), jnp.bfloat16),
             jax.ShapeDtypeStruct((1, rows), jnp.int32),
         ],
         in_specs=[ANY] * 5,
-        out_specs=[VMEM] * 2,
+        out_specs=[VMEM] * 3,
         scratch_shapes=[
             pltpu.VMEM((width, rows), jnp.bfloat16),
             pltpu.VMEM((width,), jnp.bfloat16),
@@ -254,7 +293,7 @@
         ],
         compiler_params=pltpu.CompilerParams(vmem_limit_bytes=NORM_LIMIT),
         name="norm",
-    )(hidden.T, gain, targets, lengths, mask)
+    )(*map(in_hbm, (hidden.T, gain, targets, lengths, mask)))
 
     own, head_near = pl.pallas_call(
         own_kernel,
@@ -262,42 +301,48 @@
             jax.ShapeDtypeStruct((8, rows), jnp.float32),
             jax.ShapeDtypeStruct(head.shape, head.dtype),
         ],
-        in_specs=[ANY, VMEM],
+        in_specs=[ANY, VMEM, VMEM],
         out_specs=[VMEM] * 2,
         scratch_shapes=wave_scratch(1, rows, width)
         + [pltpu.SemaphoreType.DMA((len(chunks_of(vocab)),))],
         compiler_params=pltpu.CompilerParams(vmem_limit_bytes=VMEM_LIMIT),
         cost_estimate=cost(rows, width, vocab),
         name="own",
-    )(head, block)
-
-    stats = [own]
-    full = (n - 1) // 2
-    up, down = hop(block, 1), hop(block, -1)
+    )(in_hbm(head), *block)
+
+    half = n // 2
+    found = {0: own}
+    up = [hop(piece, 1) for piece in block]
+    down = [hop(piece, -1) for piece in block]
     up, down, head_near = lax.optimization_barrier((up, down, head_near))
-    for step in range(2, full + 1):
-        next_up, next_down = hop(up, 1), hop(down, -1)
-        mine = wave(head_near, [[up], [down]])
-        up, down, *mine = lax.optimization_barrier((next_up, next_down, *mine))
-        stats += [hop(mine[0], 1 - step), hop(mine[1], step - 1)]
-    if n % 2:
-        mine = wave(head_near, [[up], [down]])
-        stats += [hop(mine[0], -full), hop(mine[1], full)]
-    else:
-        halves = [hop(up[:cut], 1), hop(down[cut:], -1)]
-        mine = wave(head_near, [[up], [down]])
-        stats += [hop(mine[0], -full), hop(mine[1], full)]
-        (far,) = wave(head_near, [halves])
-        stats.append(hop(far, n // 2))
-
+    for step in range(1, half):
+        if step < half - 1:
+            next_up = [hop(piece, 1) for piece in up]
+            next_down = [hop(piece, -1) for piece in down]
+        else:
+            next_up, next_down = [hop(up[0], 1)], [hop(down[1], -1)]
+        found[-step], found[step] = wave(head_near, [up, down])
+        if step < half - 1:
+            for i in range(2):
+                next_up[i], next_down[i], found[step] = lax.optimization_barrier(
+                    (next_up[i], next_down[i], found[step])
+                )
+        else:
+            next_up, next_down, found[step] = lax.optimization_barrier(
+                (next_up, next_down, found[step])
+            )
+        up, down = next_up, next_down
+    table = last_wave(n, head_near, up + down, found)
+
+    shares = lax.all_to_all(table, "tp", 0, 0, tiled=True)
     logprob, entropy = pl.pallas_call(
-        functools.partial(final_kernel, n),
+        final_kernel,
         out_shape=[jax.ShapeDtypeStruct((1, rows), jnp.float32)] * 2,
-        in_specs=[VMEM] * (n + 1),
+        in_specs=[VMEM] * 2,
         out_specs=[VMEM] * 2,
         compiler_params=pltpu.CompilerParams(vmem_limit_bytes=FINAL_LIMIT),
         name="combine",
-    )(valid, *stats)
+    )(valid, shares)
     return logprob.reshape(rows), entropy.reshape(rows)
 
 

time: 61.8 us -> 58.1 us (0.940)
  blocking collectives: 0 us -> 11.6 us
  starting transfers between devices: 22 us -> 15.3 us
  waiting for transfers between devices: 12 us -> 5.37 us
  local copies, waits for them, and re-layouts: 1.07 us -> 0 us
  Pallas kernels: 25.8 us -> 25 us
    all_to_all x0 -> x1, blocking collectives: none -> 11.6 us  [on_device(): shares = lax.all_to_all(table, 'tp', 0, 0, tiled=True)]
    ppermute x15 -> x14, starting transfers between devices: 22 us -> 15.3 us  [hop(): return lax.ppermute(value, 'tp', pairs)]
    ppermute x15 -> x14, waiting for transfers between devices: 12 us -> 5.37 us  [hop(): return lax.ppermute(value, 'tp', pairs)]
    pallas_call x4 -> x3, Pallas kernels: 17.5 us -> 14.5 us  [wave(): pl.pallas_call(functools.partial(wave_kernel, counts), out_shape=[jax.Sha...]
    pallas_call x2 -> x3, Pallas kernels: 2.72 us -> 4.82 us  [the longest x1 2.9 us: last_wave(): pl.pallas_call(functools.partial(last_wave_kernel, n, list(found)), out_s...]
    unnamed x4 -> x0, local copies, waits for them, and re-layouts: 1.04 us -> none
  transfers between devices with their start and end apart: 15 -> 14, of which waited for: 7 -> 5; matrix products, arithmetic and copies ran while one was open for 0% -> 0% of each run, Pallas kernels for 37% -> 35%
where the time goes in v3:
time: 58.1 us; the launch traced here: 57.9 us
  Pallas kernels  25 us (43%)
  starting transfers between devices  15.3 us (26%)
  blocking collectives  11.6 us (20%)
  waiting for transfers between devices  5.37 us (9%)
  between operations  0.7 us (1%)
    ppermute x14, starting transfers between devices, hop(): return lax.ppermute(value, 'tp', pairs)  15.3 us
    pallas_call x3, Pallas kernels, wave(): pl.pallas_call(functools.partial(wave_kernel, counts), out_shape=[jax.Sha...  14.5 us
    all_to_all x1, blocking collectives, on_device(): shares = lax.all_to_all(table, 'tp', 0, 0, tiled=True)  11.6 us
    pallas_call x1, Pallas kernels, on_device(): pl.pallas_call(own_kernel, out_shape=[jax.ShapeDtypeStruct((8, rows), jnp...  5.61 us
    ppermute x14, waiting for transfers between devices, hop(): return lax.ppermute(value, 'tp', pairs)  5.37 us
    pallas_call x1, Pallas kernels, last_wave(): pl.pallas_call(functools.partial(last_wave_kernel, n, list(found)), out_s...  2.9 us
    pallas_call x1, Pallas kernels, on_device(): pl.pallas_call(norm_kernel, out_shape=[jax.ShapeDtypeStruct((cut, rows),...  1.36 us
  transfers between devices with their start and end apart: 14, of which 5 were waited for; matrix products, arithmetic and copies ran while one was open for 0% of the time, Pallas kernels for 35%

profile of v3, /device:TPU:0, one launch (start us, length us, event | category | flops | bytes accessed | tf_op | source)
XLA Modules:
  0.0 57.9 jit_solution(1005695427760110786)
XLA Ops:
  0.6 1.4 %norm.1 = (bf16[768,128]{1,0:T(8,128)(2,1)S(1)}, bf16[848,128]{1,0:T(8,128)(2,1)S(1)}, s32[1,128]{1,0:T(1,128)S(1)}) custom-call(bf16[1600,128]{1,0:T(8,128)(2,1)} %bitcast.3, bf16[1600]{0:T(1024)(128)(2,1)} %gain_any.1, s32[128]{0:T(128)} %targets_any.1, s32[4]{0:T(128)} %lengths_any.1, s32[128]{0:T(128)} %mask_any.1), custom_call_target="tpu_custom_call" | custom-call | tf_op jit(solution)/shard_map/norm/pallas_call | solution.py:277
  2.0 3.1 %collective-permute-start.1 = (bf16[848,128]{1,0:T(8,128)(2,1)S(1)}, bf16[848,128]{1,0:T(8,128)(2,1)S(1)}, u32[]{:S(2)}, u32[]{:S(2)}) collective-permute-start(bf16[848,128]{1,0:T(8,128)(2,1)S(1)} %get-tuple-element.37.second), channel_id=1, source_target_pairs={{0,8},{8,16},{16,24},{24,28},{28,20},{20,12},{12,4},{4,0},{1,9},{9... | collective-permute-start | bytes 651272 | tf_op jit(solution)/shard_map/ppermute | solution.py:275
  5.1 0.0 collective-permute-start.3
  5.1 2.0 %collective-permute-start = (bf16[768,128]{1,0:T(8,128)(2,1)S(1)}, bf16[768,128]{1,0:T(8,128)(2,1)S(1)}, u32[]{:S(2)}, u32[]{:S(2)}) collective-permute-start(bf16[768,128]{1,0:T(8,128)(2,1)S(1)} %get-tuple-element.36.first), channel_id=1, source_target_pairs={{0,8},{8,16},{16,24},{24,28},{28,20},{20,12},{12,4},{4,0},{1,9},{9... | collective-permute-start | bytes 589832 | tf_op jit(solution)/shard_map/ppermute | solution.py:275
  7.1 0.0 collective-permute-start.2
  7.1 5.6 %own.1 = (f32[8,128]{1,0:T(8,128)S(1)}, bf16[1600,4000]{1,0:T(8,128)(2,1)S(1)}) custom-call(bf16[1600,4000]{1,0:T(8,128)(2,1)} %head_any.1, bf16[768,128]{1,0:T(8,128)(2,1)S(1)} %get-tuple-element.36.first, bf16[848,128]{1,0:T(8,128)(2,1)S(1)} %get-tuple-element.37.second), custom_call_target="tpu_custom_call" | custom-call | flops 1638400000 | bytes 12800000 | tf_op jit(solution)/shard_map/own/pallas_call | solution.py:298
  12.7 1.8 %collective-permute-done.refs_0_ = bf16[768,128]{1,0:T(8,128)(2,1)S(1)} collective-permute-done((bf16[768,128]{1,0:T(8,128)(2,1)S(1)}, bf16[768,128]{1,0:T(8,128)(2,1)S(1)}, u32[]{:S(2)}, u32[]{:S(2)}) %collective-permute-start) | collective-permute-done | bytes 196640 | tf_op jit(solution)/shard_map/ppermute | solution.py:275
  14.5 1.5 %collective-permute-done.2.refs_2_ = bf16[768,128]{1,0:T(8,128)(2,1)S(1)} collective-permute-done((bf16[768,128]{1,0:T(8,128)(2,1)S(1)}, bf16[768,128]{1,0:T(8,128)(2,1)S(1)}, u32[]{:S(2)}, u32[]{:S(2)}) %collective-permute-start.2) | collective-permute-done | bytes 196640 | tf_op jit(solution)/shard_map/ppermute | solution.py:275
  16.1 0.0 collective-permute-done.1.refs_1_
  16.1 0.0 collective-permute-done.3.refs_3_
  16.1 1.6 %collective-permute-start.4 = (bf16[768,128]{1,0:T(8,128)(2,1)S(1)}, bf16[768,128]{1,0:T(8,128)(2,1)S(1)}, u32[]{:S(2)}, u32[]{:S(2)}) collective-permute-start(bf16[768,128]{1,0:T(8,128)(2,1)S(1)} %collective-permute-done.refs_0_), channel_id=1, source_target_pairs={{0,8},{8,16},{16,24},{24,28},{28,20},{20,12},{12,4},{4,0},{1,9},{9... | collective-permute-start | bytes 589832 | tf_op jit(solution)/shard_map/ppermute | solution.py:275
  17.7 0.4 collective-permute-start.5
  18.1 1.6 %collective-permute-start.8 = (bf16[848,128]{1,0:T(8,128)(2,1)S(1)}, bf16[848,128]{1,0:T(8,128)(2,1)S(1)}, u32[]{:S(2)}, u32[]{:S(2)}) collective-permute-start(bf16[848,128]{1,0:T(8,128)(2,1)S(1)} %collective-permute-done.1.refs_1_), channel_id=1, source_target_pairs={{0,8},{8,16},{16,24},{24,28},{28,20},{20,12},{12,4},{4,0},{1,9},{9... | collective-permute-start | bytes 651272 | tf_op jit(solution)/shard_map/ppermute | solution.py:275
  19.7 0.4 collective-permute-start.9
  20.2 4.8 %wave2.3 = (f32[8,128]{1,0:T(8,128)S(1)}, f32[8,128]{1,0:T(8,128)S(1)}) custom-call(bf16[1600,4000]{1,0:T(8,128)(2,1)S(1)} %get-tuple-element.39.head, bf16[768,128]{1,0:T(8,128)(2,1)S(1)} %collective-permute-done.refs_0_, bf16[848,128]{1,0:T(8,128)(2,1)S(1)} %collective-permute-done.1.refs_1_, bf16[768,128]{1,0:T(8,128)(2,1)S(1)} %collective-permute-done.2.refs_2_, ...), custom_call_target="tpu_custom_call" | custom-call | flops 3276800000 | bytes 12800000 | tf_op jit(solution)/shard_map/wave2/pallas_call | solution.py:235
  25.0 0.0 collective-permute-done.4.refs_0_
  25.0 0.2 collective-permute-done.5.refs_2_
  25.2 1.6 %collective-permute-start.6 = (bf16[768,128]{1,0:T(8,128)(2,1)S(1)}, bf16[768,128]{1,0:T(8,128)(2,1)S(1)}, u32[]{:S(2)}, u32[]{:S(2)}) collective-permute-start(bf16[768,128]{1,0:T(8,128)(2,1)S(1)} %collective-permute-done.4.refs_0_), channel_id=1, source_target_pairs={{0,8},{8,16},{16,24},{24,28},{28,20},{20,12},{12,4},{4,0},{1,9},{9... | collective-permute-start | bytes 589832 | tf_op jit(solution)/shard_map/ppermute | solution.py:275
  26.8 0.4 collective-permute-start.7
  27.2 0.0 collective-permute-done.8.refs_1_
  27.2 1.2 %collective-permute-done.9.refs_3_ = bf16[848,128]{1,0:T(8,128)(2,1)S(1)} collective-permute-done((bf16[848,128]{1,0:T(8,128)(2,1)S(1)}, bf16[848,128]{1,0:T(8,128)(2,1)S(1)}, u32[]{:S(2)}, u32[]{:S(2)}) %collective-permute-start.9) | collective-permute-done | bytes 217120 | tf_op jit(solution)/shard_map/ppermute | solution.py:275
  28.4 1.6 %collective-permute-start.11 = (bf16[848,128]{1,0:T(8,128)(2,1)S(1)}, bf16[848,128]{1,0:T(8,128)(2,1)S(1)}, u32[]{:S(2)}, u32[]{:S(2)}) collective-permute-start(bf16[848,128]{1,0:T(8,128)(2,1)S(1)} %collective-permute-done.8.refs_1_), channel_id=1, source_target_pairs={{0,8},{8,16},{16,24},{24,28},{28,20},{20,12},{12,4},{4,0},{1,9},{9... | collective-permute-start | bytes 651272 | tf_op jit(solution)/shard_map/ppermute | solution.py:275
  30.0 0.4 collective-permute-start.12
  30.5 4.8 %wave2.4 = (f32[8,128]{1,0:T(8,128)S(1)}, f32[8,128]{1,0:T(8,128)S(1)}) custom-call(bf16[1600,4000]{1,0:T(8,128)(2,1)S(1)} %get-tuple-element.39.head, bf16[768,128]{1,0:T(8,128)(2,1)S(1)} %collective-permute-done.4.refs_0_, bf16[848,128]{1,0:T(8,128)(2,1)S(1)} %collective-permute-done.8.refs_1_, bf16[768,128]{1,0:T(8,128)(2,1)S(1)} %collective-permute-done.5.refs_2_, ...), custom_call_target="tpu_custom_call" | custom-call | flops 3276800000 | bytes 12800000 | tf_op jit(solution)/shard_map/wave2/pallas_call | solution.py:235
  35.3 0.0 collective-permute-done.6.refs_0_
  35.3 0.0 collective-permute-done.7.refs_2_
  35.3 1.6 %collective-permute-start.10 = (bf16[768,128]{1,0:T(8,128)(2,1)S(1)}, bf16[768,128]{1,0:T(8,128)(2,1)S(1)}, u32[]{:S(2)}, u32[]{:S(2)}) collective-permute-start(bf16[768,128]{1,0:T(8,128)(2,1)S(1)} %collective-permute-done.6.refs_0_), channel_id=1, source_target_pairs={{0,8},{8,16},{16,24},{24,28},{28,20},{20,12},{12,4},{4,0},{1,9},{9... | collective-permute-start | bytes 589832 | tf_op jit(solution)/shard_map/ppermute | solution.py:275
  37.0 0.0 collective-permute-done.11.refs_1_
  37.0 0.0 collective-permute-done.12.refs_3_
  37.0 0.4 collective-permute-start.13
  37.4 4.9 %wave2.5 = (f32[8,128]{1,0:T(8,128)S(1)}, f32[8,128]{1,0:T(8,128)S(1)}) custom-call(bf16[1600,4000]{1,0:T(8,128)(2,1)S(1)} %get-tuple-element.39.head, bf16[768,128]{1,0:T(8,128)(2,1)S(1)} %collective-permute-done.6.refs_0_, bf16[848,128]{1,0:T(8,128)(2,1)S(1)} %collective-permute-done.11.refs_1_, bf16[768,128]{1,0:T(8,128)(2,1)S(1)} %collective-permute-done.7.refs_2_, ...), custom_call_target="tpu_custom_call" | custom-call | flops 3276800000 | bytes 12800000 | tf_op jit(solution)/shard_map/wave2/pallas_call | solution.py:235
  42.3 0.0 collective-permute-done.10.first
  42.3 0.6 %collective-permute-done.13.second = bf16[848,128]{1,0:T(8,128)(2,1)S(1)} collective-permute-done((bf16[848,128]{1,0:T(8,128)(2,1)S(1)}, bf16[848,128]{1,0:T(8,128)(2,1)S(1)}, u32[]{:S(2)}, u32[]{:S(2)}) %collective-permute-start.13) | collective-permute-done | bytes 217120 | tf_op jit(solution)/shard_map/ppermute | solution.py:275
  42.9 2.9 %last.1 = f32[8,8,128]{2,1,0:T(8,128)S(1)} custom-call(bf16[1600,4000]{1,0:T(8,128)(2,1)S(1)} %get-tuple-element.39.head, bf16[768,128]{1,0:T(8,128)(2,1)S(1)} %collective-permute-done.10.first, bf16[848,128]{1,0:T(8,128)(2,1)S(1)} %collective-permute-done.13.second, f32[8,128]{1,0:T(8,128)S(1)} %get-tuple-element.59.refs_0_, ...), custom_call_target="tpu_custom_call" | custom-call | flops 1638400000 | bytes 12800000 | tf_op jit(solution)/shard_map/last/pallas_call | solution.py:250
  45.8 11.6 %all_to_all.5.shares = f32[8,8,128]{2,1,0:T(8,128)S(1)} all-to-all(f32[8,8,128]{2,1,0:T(8,128)S(1)} %last.1), channel_id=1, replica_groups=mesh['tp'=8,'dp'=4] {'tp'}, dimensions={0} | all-to-all | bytes 65536 | tf_op jit(solution)/shard_map/all_to_all | solution.py:337
  57.4 0.6 combine.1
Async XLA Ops:
  2.0 14.1 %collective-permute-start.1 = (bf16[848,128]{1,0:T(8,128)(2,1)S(1)}, bf16[848,128]{1,0:T(8,128)(2,1)S(1)}, u32[]{:S(2)}, u32[]{:S(2)}) collective-permute-start(bf16[848,128]{1,0:T(8,128)(2,1)S(1)} %get-tuple-element.37.second), channel_id=1, source_target_pairs={{0,8},{8,16},{16,24},{24,28},{28,20},{20,12},{12,4},{4,0},{1,9},{9... | collective-permute-start | bytes 651272 | tf_op jit(solution)/shard_map/ppermute | solution.py:275
  5.1 11.0 %collective-permute-start.3 = (bf16[848,128]{1,0:T(8,128)(2,1)S(1)}, bf16[848,128]{1,0:T(8,128)(2,1)S(1)}, u32[]{:S(2)}, u32[]{:S(2)}) collective-permute-start(bf16[848,128]{1,0:T(8,128)(2,1)S(1)} %get-tuple-element.37.second), channel_id=1, source_target_pairs={{0,4},{8,0},{16,8},{24,16},{28,24},{20,28},{12,20},{4,12},{1,5},{9... | collective-permute-start | bytes 651272 | tf_op jit(solution)/shard_map/ppermute | solution.py:275
  5.1 9.5 %collective-permute-start = (bf16[768,128]{1,0:T(8,128)(2,1)S(1)}, bf16[768,128]{1,0:T(8,128)(2,1)S(1)}, u32[]{:S(2)}, u32[]{:S(2)}) collective-permute-start(bf16[768,128]{1,0:T(8,128)(2,1)S(1)} %get-tuple-element.36.first), channel_id=1, source_target_pairs={{0,8},{8,16},{16,24},{24,28},{28,20},{20,12},{12,4},{4,0},{1,9},{9... | collective-permute-start | bytes 589832 | tf_op jit(solution)/shard_map/ppermute | solution.py:275
  7.1 9.0 %collective-permute-start.2 = (bf16[768,128]{1,0:T(8,128)(2,1)S(1)}, bf16[768,128]{1,0:T(8,128)(2,1)S(1)}, u32[]{:S(2)}, u32[]{:S(2)}) collective-permute-start(bf16[768,128]{1,0:T(8,128)(2,1)S(1)} %get-tuple-element.36.first), channel_id=1, source_target_pairs={{0,4},{8,0},{16,8},{24,16},{28,24},{20,28},{12,20},{4,12},{1,5},{9... | collective-permute-start | bytes 589832 | tf_op jit(solution)/shard_map/ppermute | solution.py:275
  16.1 8.9 %collective-permute-start.4 = (bf16[768,128]{1,0:T(8,128)(2,1)S(1)}, bf16[768,128]{1,0:T(8,128)(2,1)S(1)}, u32[]{:S(2)}, u32[]{:S(2)}) collective-permute-start(bf16[768,128]{1,0:T(8,128)(2,1)S(1)} %collective-permute-done.refs_0_), channel_id=1, source_target_pairs={{0,8},{8,16},{16,24},{24,28},{28,20},{20,12},{12,4},{4,0},{1,9},{9... | collective-permute-start | bytes 589832 | tf_op jit(solution)/shard_map/ppermute | solution.py:275
  17.7 7.5 %collective-permute-start.5 = (bf16[768,128]{1,0:T(8,128)(2,1)S(1)}, bf16[768,128]{1,0:T(8,128)(2,1)S(1)}, u32[]{:S(2)}, u32[]{:S(2)}) collective-permute-start(bf16[768,128]{1,0:T(8,128)(2,1)S(1)} %collective-permute-done.2.refs_2_), channel_id=1, source_target_pairs={{0,4},{8,0},{16,8},{24,16},{28,24},{20,28},{12,20},{4,12},{1,5},{9... | collective-permute-start | bytes 589832 | tf_op jit(solution)/shard_map/ppermute | solution.py:275
  18.1 9.1 %collective-permute-start.8 = (bf16[848,128]{1,0:T(8,128)(2,1)S(1)}, bf16[848,128]{1,0:T(8,128)(2,1)S(1)}, u32[]{:S(2)}, u32[]{:S(2)}) collective-permute-start(bf16[848,128]{1,0:T(8,128)(2,1)S(1)} %collective-permute-done.1.refs_1_), channel_id=1, source_target_pairs={{0,8},{8,16},{16,24},{24,28},{28,20},{20,12},{12,4},{4,0},{1,9},{9... | collective-permute-start | bytes 651272 | tf_op jit(solution)/shard_map/ppermute | solution.py:275
  19.7 8.7 %collective-permute-start.9 = (bf16[848,128]{1,0:T(8,128)(2,1)S(1)}, bf16[848,128]{1,0:T(8,128)(2,1)S(1)}, u32[]{:S(2)}, u32[]{:S(2)}) collective-permute-start(bf16[848,128]{1,0:T(8,128)(2,1)S(1)} %collective-permute-done.3.refs_3_), channel_id=1, source_target_pairs={{0,4},{8,0},{16,8},{24,16},{28,24},{20,28},{12,20},{4,12},{1,5},{9... | collective-permute-start | bytes 651272 | tf_op jit(solution)/shard_map/ppermute | solution.py:275
  25.2 10.1 %collective-permute-start.6 = (bf16[768,128]{1,0:T(8,128)(2,1)S(1)}, bf16[768,128]{1,0:T(8,128)(2,1)S(1)}, u32[]{:S(2)}, u32[]{:S(2)}) collective-permute-start(bf16[768,128]{1,0:T(8,128)(2,1)S(1)} %collective-permute-done.4.refs_0_), channel_id=1, source_target_pairs={{0,8},{8,16},{16,24},{24,28},{28,20},{20,12},{12,4},{4,0},{1,9},{9... | collective-permute-start | bytes 589832 | tf_op jit(solution)/shard_map/ppermute | solution.py:275
  26.8 8.6 %collective-permute-start.7 = (bf16[768,128]{1,0:T(8,128)(2,1)S(1)}, bf16[768,128]{1,0:T(8,128)(2,1)S(1)}, u32[]{:S(2)}, u32[]{:S(2)}) collective-permute-start(bf16[768,128]{1,0:T(8,128)(2,1)S(1)} %collective-permute-done.5.refs_2_), channel_id=1, source_target_pairs={{0,4},{8,0},{16,8},{24,16},{28,24},{20,28},{12,20},{4,12},{1,5},{9... | collective-permute-start | bytes 589832 | tf_op jit(solution)/shard_map/ppermute | solution.py:275
  28.4 8.5 %collective-permute-start.11 = (bf16[848,128]{1,0:T(8,128)(2,1)S(1)}, bf16[848,128]{1,0:T(8,128)(2,1)S(1)}, u32[]{:S(2)}, u32[]{:S(2)}) collective-permute-start(bf16[848,128]{1,0:T(8,128)(2,1)S(1)} %collective-permute-done.8.refs_1_), channel_id=1, source_target_pairs={{0,8},{8,16},{16,24},{24,28},{28,20},{20,12},{12,4},{4,0},{1,9},{9... | collective-permute-start | bytes 651272 | tf_op jit(solution)/shard_map/ppermute | solution.py:275
  30.0 6.9 %collective-permute-start.12 = (bf16[848,128]{1,0:T(8,128)(2,1)S(1)}, bf16[848,128]{1,0:T(8,128)(2,1)S(1)}, u32[]{:S(2)}, u32[]{:S(2)}) collective-permute-start(bf16[848,128]{1,0:T(8,128)(2,1)S(1)} %collective-permute-done.9.refs_3_), channel_id=1, source_target_pairs={{0,4},{8,0},{16,8},{24,16},{28,24},{20,28},{12,20},{4,12},{1,5},{9... | collective-permute-start | bytes 651272 | tf_op jit(solution)/shard_map/ppermute | solution.py:275
  35.3 6.9 %collective-permute-start.10 = (bf16[768,128]{1,0:T(8,128)(2,1)S(1)}, bf16[768,128]{1,0:T(8,128)(2,1)S(1)}, u32[]{:S(2)}, u32[]{:S(2)}) collective-permute-start(bf16[768,128]{1,0:T(8,128)(2,1)S(1)} %collective-permute-done.6.refs_0_), channel_id=1, source_target_pairs={{0,8},{8,16},{16,24},{24,28},{28,20},{20,12},{12,4},{4,0},{1,9},{9... | collective-permute-start | bytes 589832 | tf_op jit(solution)/shard_map/ppermute | solution.py:275
  37.0 5.9 %collective-permute-start.13 = (bf16[848,128]{1,0:T(8,128)(2,1)S(1)}, bf16[848,128]{1,0:T(8,128)(2,1)S(1)}, u32[]{:S(2)}, u32[]{:S(2)}) collective-permute-start(bf16[848,128]{1,0:T(8,128)(2,1)S(1)} %collective-permute-done.12.refs_3_), channel_id=1, source_target_pairs={{0,4},{8,0},{16,8},{24,16},{28,24},{20,28},{12,20},{4,12},{1,5},{9... | collective-permute-start | bytes 651272 | tf_op jit(solution)/shard_map/ppermute | solution.py:275

commit v4 on v3

--- a/solution.py
+++ b/solution.py
@@ -9,7 +9,7 @@
 
 SEQ_LEN = 256
 EPS = 1e-06
-EXTRA = 16
+EXTRA = 64
 BASE = 256
 VMEM_LIMIT = 32 * 1024 * 1024
 NORM_LIMIT = 16 * 1024 * 1024
@@ -21,7 +21,7 @@
 ANY = pl.BlockSpec(memory_space=pl.ANY)
 
 
-def norm_kernel(hidden_any, gain_any, targets_any, lengths_any, mask_any, first, second, valid, *scratch):
+def norm_kernel(hidden_any, gain_any, targets_any, lengths_any, mask_any, first, second, rest, place, *scratch):
     hidden_t, gain, targets, lengths, mask, sems = scratch
     width, rows = hidden_t.shape
     copies = [
@@ -40,42 +40,57 @@
         copy.start()
     for copy in copies:
         copy.wait()
+    row = lax.axis_index("tp") * rows + lax.broadcasted_iota(jnp.int32, (1, rows), 1)
+    length = jnp.zeros((1, rows), jnp.int32)
+    for s in range(lengths.shape[0]):
+        length = jnp.where(row // SEQ_LEN == s, lengths[s], length)
+    live = (row % SEQ_LEN < length) & (mask[...].reshape(1, rows) == 1)
+    alive = jnp.where(live, 1.0, 0.0)
+    down = lax.broadcasted_iota(jnp.int32, (rows, rows), 0)
+    across = lax.broadcasted_iota(jnp.int32, (rows, rows), 1)
+    before = jnp.where(down < across, 1.0, 0.0).astype(jnp.bfloat16)
+    many = jnp.broadcast_to(alive, (16, rows)).astype(jnp.bfloat16)
+    rank = jnp.dot(many, before, preferred_element_type=jnp.float32)[0:1]
+    place[...] = jnp.where(live, rank, -1.0)
+    select = (rank == down.astype(jnp.float32)) & live
+    select = jnp.where(select, 1.0, 0.0).astype(jnp.bfloat16)
+
     x = hidden_t[...].astype(jnp.float32)
     meansq = jnp.sum(x * x, axis=0, keepdims=True) * (1.0 / width)
     scale = lax.rsqrt(meansq + EPS)
     g = jnp.broadcast_to(gain[...].astype(jnp.float32).reshape(1, width), (rows, width)).T
     normed = (x * scale * g).astype(jnp.bfloat16)
-    cut = first.shape[0]
-    first[...] = normed[:cut]
-    second[: width - cut, :] = normed[cut:]
     ids = targets[...].reshape(1, rows)
     high = ids // BASE
     digit = lax.broadcasted_iota(jnp.int32, (EXTRA, rows), 0)
     digits = jnp.where(digit == 0, high, jnp.where(digit == 1, ids - high * BASE, 0))
-    second[width - cut :, :] = digits.astype(jnp.float32).astype(jnp.bfloat16)
-    row = lax.axis_index("tp") * rows + lax.broadcasted_iota(jnp.int32, (1, rows), 1)
-    length = jnp.zeros((1, rows), jnp.int32)
-    for s in range(lengths.shape[0]):
-        length = jnp.where(row // SEQ_LEN == s, lengths[s], length)
-    live = (row % SEQ_LEN < length) & (mask[...].reshape(1, rows) == 1)
-    valid[...] = live.astype(jnp.int32)
+    digits = jnp.where(digit == 2, jnp.sum(alive), digits.astype(jnp.float32))
+    full = jnp.concatenate([normed, digits.astype(jnp.bfloat16)], axis=0)
+    packed = lax.dot_general(
+        select, full, (((1,), (1,)), ((), ())), preferred_element_type=jnp.float32
+    ).astype(jnp.bfloat16)
+    kept, cut = first.shape
+    first[...] = packed[:kept, :cut]
+    second[...] = packed[:kept, cut:]
+    rest[...] = packed[kept:]
 
 
 def unpack(blocks, x_scr, id_scr, vocab):
     width = x_scr.shape[1]
-    start = lax.axis_index("tp") * vocab
-    for b, pieces in enumerate(blocks):
-        rows = pieces[0].shape[1]
+    shard = lax.axis_index("tp") * vocab
+    counts = []
+    for b, (first, second) in enumerate(blocks):
+        rows, cut = first.shape
         at = pl.ds(b * rows, rows)
-        low = 0
-        for piece in pieces:
-            high = min(low + piece.shape[0], width)
-            x_scr[at, low:high] = piece[: high - low, :].T
-            if piece.shape[0] > high - low:
-                digits = piece[high - low :, :]
-            low = high
-        digits = digits.astype(jnp.float32).T.astype(jnp.int32)
-        id_scr[at, :] = digits[:, 0:1] * BASE + digits[:, 1:2] - start
+        x_scr[at, :cut] = first[...]
+        x_scr[at, cut:] = second[:, : width - cut]
+        low = (width - cut) // 128 * 128
+        extra = second[:, low:].astype(jnp.float32)
+        counts.append(jnp.max(extra[:, width - cut - low + 2 :][:, :1], axis=0, keepdims=True))
+        extra = extra.astype(jnp.int32)
+        digits = [extra[:, width - cut - low + i :][:, :1] for i in range(2)]
+        id_scr[at, :] = digits[0] * BASE + digits[1] - shard
+    return counts
 
 
 def chunks_of(vocab):
@@ -128,10 +143,9 @@
         tgt_s[at, :] = tgt
 
 
-def collect(stats, acc):
+def collect(stats, rows, counts, acc):
     top_s, sum_s, ent_s, tgt_s = acc
-    for b, out in enumerate(stats):
-        rows = out.shape[1]
+    for b, (out, count) in enumerate(zip(stats, counts)):
         at = pl.ds(b * rows, rows)
         tops = top_s[at, :].T
         sums = sum_s[at, :].T
@@ -139,33 +153,33 @@
         top = jnp.max(tops, axis=0, keepdims=True)
         delta = tops - top
         scale = jnp.exp(delta)
-        out[0:1, :] = top
-        out[1:2, :] = jnp.sum(sums * scale, axis=0, keepdims=True)
-        out[2:3, :] = jnp.sum((ents + delta * sums) * scale, axis=0, keepdims=True)
-        out[3:4, :] = jnp.sum(tgt_s[at, :].T, axis=0, keepdims=True)
-        out[4:8, :] = jnp.zeros((4, rows), jnp.float32)
-
-
-def wave_kernel(counts, head, *refs):
-    blocks = []
-    for count in counts:
-        blocks.append(refs[:count])
-        refs = refs[count:]
-    stats, (x_scr, id_scr, *acc) = refs[: len(counts)], refs[len(counts) :]
-    vocab = head.shape[1]
-    unpack(blocks, x_scr, id_scr, vocab)
+        out[0:1, :rows] = top
+        out[1:2, :rows] = jnp.sum(sums * scale, axis=0, keepdims=True)
+        out[2:3, :rows] = jnp.sum((ents + delta * sums) * scale, axis=0, keepdims=True)
+        out[3:4, :rows] = jnp.sum(tgt_s[at, :].T, axis=0, keepdims=True)
+        out[4:5, :] = jnp.broadcast_to(count, (1, out.shape[1]))
+        out[5:8, :] = jnp.zeros((3, out.shape[1]), jnp.float32)
+
+
+def wave_kernel(count, head, *refs):
+    pieces, stats, (x_scr, id_scr, *acc) = refs[: 2 * count], refs[2 * count : 3 * count], refs[3 * count :]
+    rows, vocab = pieces[0].shape[0], head.shape[1]
+    counts = unpack(list(zip(pieces[::2], pieces[1::2])), x_scr, id_scr, vocab)
     for lo, hi in chunks_of(vocab):
         logits = jnp.dot(x_scr[...], head[:, lo:hi], preferred_element_type=jnp.float32)
         update(logits, lo, id_scr, acc)
-    collect(stats, acc)
-
-
-def last_wave_kernel(n, away, head, first, second, *refs):
-    count = len(away)
-    found, table, scratch = refs[:count], refs[count], refs[count + 1 :]
-    wave_kernel([2], head, first, second, table.at[owner(n, n // 2)], *scratch)
-    for places, stats in zip(away, found):
+    collect(stats, rows, counts, acc)
+
+
+def last_wave_kernel(n, new, away, head, *refs):
+    pieces, refs = refs[: 2 * new], refs[2 * new :]
+    found, refs = refs[: len(away) - new], refs[len(away) - new :]
+    table, most, *scratch = refs
+    mine = [table.at[owner(n, places)] for places in away[:new]]
+    wave_kernel(new, head, *pieces, *mine, *scratch)
+    for places, stats in zip(away[new:], found):
         table[owner(n, places)] = stats[...]
+    most[...] = functools.reduce(jnp.maximum, [table[i, 4:5, :] for i in range(n)])
 
 
 def owner(n, places):
@@ -187,15 +201,16 @@
     ]
     for copy in copies:
         copy.start()
-    unpack([[first, second]], x_scr, id_scr, vocab)
+    rows = first.shape[0]
+    counts = unpack([(first, second)], x_scr, id_scr, vocab)
     for (lo, hi), copy in zip(spans, copies):
         copy.wait()
         logits = jnp.dot(x_scr[...], head[:, lo:hi], preferred_element_type=jnp.float32)
         update(logits, lo, id_scr, acc)
-    collect([stats], acc)
-
-
-def final_kernel(valid, shares, logprob, entropy):
+    collect([stats], rows, counts, acc)
+
+
+def merge(shares):
     stats = [shares[i] for i in range(shares.shape[0])]
     tops = [s[0:1, :] for s in stats]
     top = functools.reduce(jnp.maximum, tops)
@@ -208,9 +223,19 @@
         ent = ent + (s[2:3, :] + delta * own_sums) * scale
         tgt = tgt + s[3:4, :]
     log_total = jnp.log(sums)
-    live = valid[...] == 1
-    logprob[...] = jnp.where(live, tgt - (top + log_total), 0.0)
-    entropy[...] = jnp.where(live, log_total - ent / sums, 0.0)
+    return tgt - (top + log_total), log_total - ent / sums
+
+
+def final_kernel(kept, place, shares, more, logprob, entropy):
+    rows = place.shape[1]
+    down = lax.broadcasted_iota(jnp.int32, (rows, rows), 0)
+    here = (down.astype(jnp.float32) == place[...]) & (down < kept)
+    there = (down + kept).astype(jnp.float32) == place[...]
+    for out, first, rest in zip((logprob, entropy), merge(shares), merge(more)):
+        first = jnp.broadcast_to(first, (rows, rows)).T
+        rest = jnp.broadcast_to(rest, (rows, rows)).T
+        both = jnp.where(here, first, jnp.where(there, rest, 0.0))
+        out[...] = jnp.sum(both, axis=0, keepdims=True)
 
 
 def wave_scratch(count, rows, width):
@@ -228,34 +253,38 @@
     )
 
 
-def wave(head, blocks):
-    counts = [len(pieces) for pieces in blocks]
+def wave(head, blocks, lanes):
+    count = len(blocks)
     width, vocab = head.shape
-    rows = blocks[0][0].shape[1]
+    rows = blocks[0][0].shape[0]
     return pl.pallas_call(
-        functools.partial(wave_kernel, counts),
-        out_shape=[jax.ShapeDtypeStruct((8, rows), jnp.float32)] * len(blocks),
-        in_specs=[VMEM] * (1 + sum(counts)),
-        out_specs=[VMEM] * len(blocks),
-        scratch_shapes=wave_scratch(len(blocks), rows, width),
+        functools.partial(wave_kernel, count),
+        out_shape=[jax.ShapeDtypeStruct((8, lanes), jnp.float32)] * count,
+        in_specs=[VMEM] * (1 + 2 * count),
+        out_specs=[VMEM] * count,
+        scratch_shapes=wave_scratch(count, rows, width),
         compiler_params=pltpu.CompilerParams(vmem_limit_bytes=VMEM_LIMIT),
-        cost_estimate=cost(len(blocks) * rows, width, vocab),
-        name=f"wave{len(blocks)}",
-    )(head, *[piece for pieces in blocks for piece in pieces])
-
-
-def last_wave(n, head, pieces, found):
+        cost_estimate=cost(count * rows, width, vocab),
+        name=f"wave{count}",
+    )(head, *[piece for block in blocks for piece in block])
+
+
+def last_wave(n, head, blocks, found, lanes):
     width, vocab = head.shape
-    rows = pieces[0].shape[1]
+    pieces = [piece for block in blocks.values() for piece in block]
+    rows, new = pieces[0].shape[0], len(blocks)
     return pl.pallas_call(
-        functools.partial(last_wave_kernel, n, list(found)),
-        out_shape=jax.ShapeDtypeStruct((n, 8, rows), jnp.float32),
-        in_specs=[VMEM] * (3 + len(found)),
-        out_specs=VMEM,
-        scratch_shapes=wave_scratch(1, rows, width),
+        functools.partial(last_wave_kernel, n, new, [*blocks, *found]),
+        out_shape=[
+            jax.ShapeDtypeStruct((n, 8, lanes), jnp.float32),
+            jax.ShapeDtypeStruct((1, lanes), jnp.float32),
+        ],
+        in_specs=[VMEM] * (1 + len(pieces) + len(found)),
+        out_specs=[VMEM] * 2,
+        scratch_shapes=wave_scratch(new, rows, width),
         compiler_params=pltpu.CompilerParams(vmem_limit_bytes=VMEM_LIMIT),
-        cost_estimate=cost(rows, width, vocab),
-        name="last",
+        cost_estimate=cost(new * rows, width, vocab),
+        name=f"last{new}",
     )(head, *pieces, *found.values())
 
 
@@ -267,6 +296,7 @@
     rows, width = hidden.shape
     vocab = head.shape[1]
     cut = (width // 2) // 128 * 128
+    kept = rows * 7 // 8 // GROUP * GROUP
 
     ring = list(range(0, n, 2)) + list(range(1, n, 2))[::-1]
 
@@ -274,15 +304,16 @@
         pairs = [(ring[i], ring[(i + by) % n]) for i in range(n)]
         return lax.ppermute(value, "tp", pairs)
 
-    *block, valid = pl.pallas_call(
+    *block, rest, place = pl.pallas_call(
         norm_kernel,
         out_shape=[
-            jax.ShapeDtypeStruct((cut, rows), jnp.bfloat16),
-            jax.ShapeDtypeStruct((width - cut + EXTRA, rows), jnp.bfloat16),
-            jax.ShapeDtypeStruct((1, rows), jnp.int32),
+            jax.ShapeDtypeStruct((kept, cut), jnp.bfloat16),
+            jax.ShapeDtypeStruct((kept, width - cut + EXTRA), jnp.bfloat16),
+            jax.ShapeDtypeStruct((rows - kept, width + EXTRA), jnp.bfloat16),
+            jax.ShapeDtypeStruct((1, rows), jnp.float32),
         ],
         in_specs=[ANY] * 5,
-        out_specs=[VMEM] * 3,
+        out_specs=[VMEM] * 4,
         scratch_shapes=[
             pltpu.VMEM((width, rows), jnp.bfloat16),
             pltpu.VMEM((width,), jnp.bfloat16),
@@ -303,10 +334,10 @@
         ],
         in_specs=[ANY, VMEM, VMEM],
         out_specs=[VMEM] * 2,
-        scratch_shapes=wave_scratch(1, rows, width)
+        scratch_shapes=wave_scratch(1, kept, width)
         + [pltpu.SemaphoreType.DMA((len(chunks_of(vocab)),))],
         compiler_params=pltpu.CompilerParams(vmem_limit_bytes=VMEM_LIMIT),
-        cost_estimate=cost(rows, width, vocab),
+        cost_estimate=cost(kept, width, vocab),
         name="own",
     )(in_hbm(head), *block)
 
@@ -321,7 +352,7 @@
             next_down = [hop(piece, -1) for piece in down]
         else:
             next_up, next_down = [hop(up[0], 1)], [hop(down[1], -1)]
-        found[-step], found[step] = wave(head_near, [up, down])
+        found[-step], found[step] = wave(head_near, [up, down], rows)
         if step < half - 1:
             for i in range(2):
                 next_up[i], next_down[i], found[step] = lax.optimization_barrier(
@@ -332,17 +363,24 @@
                 (next_up, next_down, found[step])
             )
         up, down = next_up, next_down
-    table = last_wave(n, head_near, up + down, found)
+    table, most = last_wave(n, head_near, {half: up + down}, found, rows)
 
     shares = lax.all_to_all(table, "tp", 0, 0, tiled=True)
+
+    def others():
+        blocks = {-k: (b[:, :cut], b[:, cut:]) for k, b in enumerate([rest] + [hop(rest, k) for k in range(1, n)])}
+        table, _ = last_wave(n, head, blocks, {}, rows)
+        return lax.all_to_all(table, "tp", 0, 0, tiled=True)
+
+    more = lax.cond(most[0, 0] > kept, others, lambda: jnp.zeros_like(shares))
     logprob, entropy = pl.pallas_call(
-        final_kernel,
+        functools.partial(final_kernel, kept),
         out_shape=[jax.ShapeDtypeStruct((1, rows), jnp.float32)] * 2,
-        in_specs=[VMEM] * 2,
+        in_specs=[VMEM] * 3,
         out_specs=[VMEM] * 2,
         compiler_params=pltpu.CompilerParams(vmem_limit_bytes=FINAL_LIMIT),
         name="combine",
-    )(valid, shares)
+    )(place, shares, more)
     return logprob.reshape(rows), entropy.reshape(rows)
 
 

time: 58.1 us -> 55.4 us (0.954)
  waiting for transfers between devices: 5.37 us -> 2.39 us
    ppermute x14, waiting for transfers between devices: 5.37 us -> 2.39 us  [hop(): return lax.ppermute(value, 'tp', pairs)]
  transfers between devices with their start and end apart: 14 -> 14, of which waited for: 5 -> 1; matrix products, arithmetic and copies ran while one was open for 0% -> 0% of each run, Pallas kernels for 35% -> 35%
where the time goes in v4:
time: 55.4 us; the launch traced here: 55.2 us
  Pallas kernels  24.5 us (44%)
  starting transfers between devices  15.6 us (28%)
  blocking collectives  12 us (22%)
  waiting for transfers between devices  2.39 us (4%)
  between operations  0.78 us (1%)
    ppermute x14, starting transfers between devices, hop(): return lax.ppermute(value, 'tp', pairs)  15.6 us
    pallas_call x3, Pallas kernels, wave(): pl.pallas_call(functools.partial(wave_kernel, count), out_shape=[jax.Shap...  13.6 us
    all_to_all x1, blocking collectives, on_device(): shares = lax.all_to_all(table, 'tp', 0, 0, tiled=True)  12 us
    pallas_call x1, Pallas kernels, on_device(): pl.pallas_call(own_kernel, out_shape=[jax.ShapeDtypeStruct((8, rows), jnp...  5.59 us
    pallas_call x1, Pallas kernels, last_wave(): pl.pallas_call(functools.partial(last_wave_kernel, n, new, [*blocks, *fou...  2.92 us
    ppermute x14, waiting for transfers between devices, hop(): return lax.ppermute(value, 'tp', pairs)  2.39 us
    pallas_call x1, Pallas kernels, on_device(): pl.pallas_call(norm_kernel, out_shape=[jax.ShapeDtypeStruct((kept, cut),...  1.64 us
  transfers between devices with their start and end apart: 14, of which 1 were waited for; matrix products, arithmetic and copies ran while one was open for 0% of the time, Pallas kernels for 35%

profile of v4, /device:TPU:0, one launch (start us, length us, event | category | flops | bytes accessed | tf_op | source)
XLA Modules:
  0.0 55.2 jit_solution(3532274107746716507)
XLA Ops:
  0.6 1.6 %norm.1 = (bf16[112,768]{1,0:T(8,128)(2,1)S(1)}, bf16[112,896]{1,0:T(8,128)(2,1)S(1)}, bf16[16,1664]{1,0:T(8,128)(2,1)S(1)}, f32[1,128]{1,0:T(1,128)S(1)}) custom-call(bf16[1600,128]{1,0:T(8,128)(2,1)} %bitcast.6, bf16[1600]{0:T(1024)(128)(2,1)} %gain_any.1, s32[128]{0:T(128)} %targets_any.1, s32[4]{0:T(128)} %lengths_any.1, s32[128]{0:T(128)} %mask_any.1), custom_call_target="tpu_custom_call" | custom-call | tf_op jit(solution)/shard_map/norm/pallas_call | solution.py:307
  2.3 3.0 %collective-permute-start.10 = (bf16[112,896]{1,0:T(8,128)(2,1)S(1)}, bf16[112,896]{1,0:T(8,128)(2,1)S(1)}, u32[]{:S(2)}, u32[]{:S(2)}) collective-permute-start(bf16[112,896]{1,0:T(8,128)(2,1)S(1)} %get-tuple-element.50.second), channel_id=1, source_target_pairs={{0,4},{8,0},{16,8},{24,16},{28,24},{20,28},{12,20},{4,12},{1,5},{9... | collective-permute-start | bytes 602120 | tf_op jit(solution)/shard_map/ppermute | solution.py:305
  5.3 0.2 collective-permute-start.8
  5.4 2.0 %collective-permute-start.7 = (bf16[112,768]{1,0:T(8,128)(2,1)S(1)}, bf16[112,768]{1,0:T(8,128)(2,1)S(1)}, u32[]{:S(2)}, u32[]{:S(2)}) collective-permute-start(bf16[112,768]{1,0:T(8,128)(2,1)S(1)} %get-tuple-element.49.first), channel_id=1, source_target_pairs={{0,8},{8,16},{16,24},{24,28},{28,20},{20,12},{12,4},{4,0},{1,9},{9... | collective-permute-start | bytes 516104 | tf_op jit(solution)/shard_map/ppermute | solution.py:305
  7.4 0.1 collective-permute-start.9
  7.4 5.6 %own.1 = (f32[8,128]{1,0:T(8,128)S(1)}, bf16[1600,4000]{1,0:T(8,128)(2,1)S(1)}) custom-call(bf16[1600,4000]{1,0:T(8,128)(2,1)} %head_any.1, bf16[112,768]{1,0:T(8,128)(2,1)S(1)} %get-tuple-element.49.first, bf16[112,896]{1,0:T(8,128)(2,1)S(1)} %get-tuple-element.50.second), custom_call_target="tpu_custom_call" | custom-call | flops 1433600000 | bytes 12800000 | tf_op jit(solution)/shard_map/own/pallas_call | solution.py:329
  13.0 2.4 %collective-permute-done.7.refs_0_ = bf16[112,768]{1,0:T(8,128)(2,1)S(1)} collective-permute-done((bf16[112,768]{1,0:T(8,128)(2,1)S(1)}, bf16[112,768]{1,0:T(8,128)(2,1)S(1)}, u32[]{:S(2)}, u32[]{:S(2)}) %collective-permute-start.7) | collective-permute-done | bytes 172064 | tf_op jit(solution)/shard_map/ppermute | solution.py:305
  15.4 0.0 collective-permute-done.9.refs_2_
  15.4 0.0 collective-permute-done.10.refs_3_
  15.4 0.0 collective-permute-done.8.refs_1_
  15.4 0.5 collective-permute-start.11
  15.9 1.6 %collective-permute-start.12 = (bf16[112,768]{1,0:T(8,128)(2,1)S(1)}, bf16[112,768]{1,0:T(8,128)(2,1)S(1)}, u32[]{:S(2)}, u32[]{:S(2)}) collective-permute-start(bf16[112,768]{1,0:T(8,128)(2,1)S(1)} %collective-permute-done.9.refs_2_), channel_id=1, source_target_pairs={{0,4},{8,0},{16,8},{24,16},{28,24},{20,28},{12,20},{4,12},{1,5},{9... | collective-permute-start | bytes 516104 | tf_op jit(solution)/shard_map/ppermute | solution.py:305
  17.5 0.4 collective-permute-start.15
  17.9 1.6 %collective-permute-start.16 = (bf16[112,896]{1,0:T(8,128)(2,1)S(1)}, bf16[112,896]{1,0:T(8,128)(2,1)S(1)}, u32[]{:S(2)}, u32[]{:S(2)}) collective-permute-start(bf16[112,896]{1,0:T(8,128)(2,1)S(1)} %collective-permute-done.10.refs_3_), channel_id=1, source_target_pairs={{0,4},{8,0},{16,8},{24,16},{28,24},{20,28},{12,20},{4,12},{1,5},{9... | collective-permute-start | bytes 602120 | tf_op jit(solution)/shard_map/ppermute | solution.py:305
  19.5 4.5 %wave2.3 = (f32[8,128]{1,0:T(8,128)S(1)}, f32[8,128]{1,0:T(8,128)S(1)}) custom-call(bf16[1600,4000]{1,0:T(8,128)(2,1)S(1)} %get-tuple-element.52.head, bf16[112,768]{1,0:T(8,128)(2,1)S(1)} %collective-permute-done.7.refs_0_, bf16[112,896]{1,0:T(8,128)(2,1)S(1)} %collective-permute-done.8.refs_1_, bf16[112,768]{1,0:T(8,128)(2,1)S(1)} %collective-permute-done.9.refs_2_, ...), custom_call_target="tpu_custom_call" | custom-call | flops 2867200000 | bytes 12800000 | tf_op jit(solution)/shard_map/wave2/pallas_call | solution.py:260
  24.1 0.0 collective-permute-done.11.refs_0_
  24.1 0.0 collective-permute-done.12.refs_2_
  24.1 0.5 collective-permute-start.13
  24.6 1.6 %collective-permute-start.14 = (bf16[112,768]{1,0:T(8,128)(2,1)S(1)}, bf16[112,768]{1,0:T(8,128)(2,1)S(1)}, u32[]{:S(2)}, u32[]{:S(2)}) collective-permute-start(bf16[112,768]{1,0:T(8,128)(2,1)S(1)} %collective-permute-done.12.refs_2_), channel_id=1, source_target_pairs={{0,4},{8,0},{16,8},{24,16},{28,24},{20,28},{12,20},{4,12},{1,5},{9... | collective-permute-start | bytes 516104 | tf_op jit(solution)/shard_map/ppermute | solution.py:305
  26.2 0.0 collective-permute-done.15.refs_1_
  26.2 0.0 collective-permute-done.16.refs_3_
  26.2 0.8 %collective-permute-start.18 = (bf16[112,896]{1,0:T(8,128)(2,1)S(1)}, bf16[112,896]{1,0:T(8,128)(2,1)S(1)}, u32[]{:S(2)}, u32[]{:S(2)}) collective-permute-start(bf16[112,896]{1,0:T(8,128)(2,1)S(1)} %collective-permute-done.15.refs_1_), channel_id=1, source_target_pairs={{0,8},{8,16},{16,24},{24,28},{28,20},{20,12},{12,4},{4,0},{1,9},{9... | collective-permute-start | bytes 602120 | tf_op jit(solution)/shard_map/ppermute | solution.py:305
  27.0 1.2 %collective-permute-start.19 = (bf16[112,896]{1,0:T(8,128)(2,1)S(1)}, bf16[112,896]{1,0:T(8,128)(2,1)S(1)}, u32[]{:S(2)}, u32[]{:S(2)}) collective-permute-start(bf16[112,896]{1,0:T(8,128)(2,1)S(1)} %collective-permute-done.16.refs_3_), channel_id=1, source_target_pairs={{0,4},{8,0},{16,8},{24,16},{28,24},{20,28},{12,20},{4,12},{1,5},{9... | collective-permute-start | bytes 602120 | tf_op jit(solution)/shard_map/ppermute | solution.py:305
  28.2 4.5 %wave2.4 = (f32[8,128]{1,0:T(8,128)S(1)}, f32[8,128]{1,0:T(8,128)S(1)}) custom-call(bf16[1600,4000]{1,0:T(8,128)(2,1)S(1)} %get-tuple-element.52.head, bf16[112,768]{1,0:T(8,128)(2,1)S(1)} %collective-permute-done.11.refs_0_, bf16[112,896]{1,0:T(8,128)(2,1)S(1)} %collective-permute-done.15.refs_1_, bf16[112,768]{1,0:T(8,128)(2,1)S(1)} %collective-permute-done.12.refs_2_, ...), custom_call_target="tpu_custom_call" | custom-call | flops 2867200000 | bytes 12800000 | tf_op jit(solution)/shard_map/wave2/pallas_call | solution.py:260
  32.7 0.0 collective-permute-done.13.refs_0_
  32.8 0.0 collective-permute-done.14.refs_2_
  32.8 0.9 %collective-permute-start.17 = (bf16[112,768]{1,0:T(8,128)(2,1)S(1)}, bf16[112,768]{1,0:T(8,128)(2,1)S(1)}, u32[]{:S(2)}, u32[]{:S(2)}) collective-permute-start(bf16[112,768]{1,0:T(8,128)(2,1)S(1)} %collective-permute-done.13.refs_0_), channel_id=1, source_target_pairs={{0,8},{8,16},{16,24},{24,28},{28,20},{20,12},{12,4},{4,0},{1,9},{9... | collective-permute-start | bytes 516104 | tf_op jit(solution)/shard_map/ppermute | solution.py:305
  33.6 0.0 collective-permute-done.18.refs_1_
  33.6 0.0 collective-permute-done.19.refs_3_
  33.6 1.4 %collective-permute-start.20 = (bf16[112,896]{1,0:T(8,128)(2,1)S(1)}, bf16[112,896]{1,0:T(8,128)(2,1)S(1)}, u32[]{:S(2)}, u32[]{:S(2)}) collective-permute-start(bf16[112,896]{1,0:T(8,128)(2,1)S(1)} %collective-permute-done.19.refs_3_), channel_id=1, source_target_pairs={{0,4},{8,0},{16,8},{24,16},{28,24},{20,28},{12,20},{4,12},{1,5},{9... | collective-permute-start | bytes 602120 | tf_op jit(solution)/shard_map/ppermute | solution.py:305
  35.0 4.5 %wave2.5 = (f32[8,128]{1,0:T(8,128)S(1)}, f32[8,128]{1,0:T(8,128)S(1)}) custom-call(bf16[1600,4000]{1,0:T(8,128)(2,1)S(1)} %get-tuple-element.52.head, bf16[112,768]{1,0:T(8,128)(2,1)S(1)} %collective-permute-done.13.refs_0_, bf16[112,896]{1,0:T(8,128)(2,1)S(1)} %collective-permute-done.18.refs_1_, bf16[112,768]{1,0:T(8,128)(2,1)S(1)} %collective-permute-done.14.refs_2_, ...), custom_call_target="tpu_custom_call" | custom-call | flops 2867200000 | bytes 12800000 | tf_op jit(solution)/shard_map/wave2/pallas_call | solution.py:260
  39.5 0.0 collective-permute-done.17.refs_0_
  39.5 0.0 collective-permute-done.20.refs_1_
  39.6 2.9 %last1.1 = (f32[8,8,128]{2,1,0:T(8,128)S(1)}, f32[1,128]{1,0:T(1,128)S(1)}) custom-call(bf16[1600,4000]{1,0:T(8,128)(2,1)S(1)} %get-tuple-element.52.head, bf16[112,768]{1,0:T(8,128)(2,1)S(1)} %collective-permute-done.17.refs_0_, bf16[112,896]{1,0:T(8,128)(2,1)S(1)} %collective-permute-done.20.refs_1_, f32[8,128]{1,0:T(8,128)S(1)} %get-tuple-element.72.refs_2_, ...), custom_call_target="tpu_custom_call" | custom-call | flops 1433600000 | bytes 12800000 | tf_op jit(solution)/shard_map/last1/pallas_call | solution.py:276
  42.6 12.0 %all_to_all.10.shares = f32[8,8,128]{2,1,0:T(8,128)S(1)} all-to-all(f32[8,8,128]{2,1,0:T(8,128)S(1)} %get-tuple-element.79), channel_id=1, replica_groups=mesh['tp'=8,'dp'=4] {'tp'}, dimensions={0} | all-to-all | bytes 65536 | tf_op jit(solution)/shard_map/all_to_all | solution.py:368
  54.5 0.7 %combine.1 = (f32[1,128]{1,0:T(1,128)}, f32[1,128]{1,0:T(1,128)}) custom-call(f32[1,128]{1,0:T(1,128)S(1)} %get-tuple-element.48.place, f32[8,8,128]{2,1,0:T(8,128)S(1)} %all_to_all.10.shares, f32[8,8,128]{2,1,0:T(8,128)S(1)} %get-tuple-element.84.more), custom_call_target="tpu_custom_call" | custom-call | tf_op jit(solution)/shard_map/combine/pallas_call | solution.py:376
  (2 shorter events, 0.0 us)
Async XLA Ops:
  2.3 13.1 %collective-permute-start.10 = (bf16[112,896]{1,0:T(8,128)(2,1)S(1)}, bf16[112,896]{1,0:T(8,128)(2,1)S(1)}, u32[]{:S(2)}, u32[]{:S(2)}) collective-permute-start(bf16[112,896]{1,0:T(8,128)(2,1)S(1)} %get-tuple-element.50.second), channel_id=1, source_target_pairs={{0,4},{8,0},{16,8},{24,16},{28,24},{20,28},{12,20},{4,12},{1,5},{9... | collective-permute-start | bytes 602120 | tf_op jit(solution)/shard_map/ppermute | solution.py:305
  5.3 10.1 %collective-permute-start.8 = (bf16[112,896]{1,0:T(8,128)(2,1)S(1)}, bf16[112,896]{1,0:T(8,128)(2,1)S(1)}, u32[]{:S(2)}, u32[]{:S(2)}) collective-permute-start(bf16[112,896]{1,0:T(8,128)(2,1)S(1)} %get-tuple-element.50.second), channel_id=1, source_target_pairs={{0,8},{8,16},{16,24},{24,28},{28,20},{20,12},{12,4},{4,0},{1,9},{9... | collective-permute-start | bytes 602120 | tf_op jit(solution)/shard_map/ppermute | solution.py:305
  5.4 10.0 %collective-permute-start.7 = (bf16[112,768]{1,0:T(8,128)(2,1)S(1)}, bf16[112,768]{1,0:T(8,128)(2,1)S(1)}, u32[]{:S(2)}, u32[]{:S(2)}) collective-permute-start(bf16[112,768]{1,0:T(8,128)(2,1)S(1)} %get-tuple-element.49.first), channel_id=1, source_target_pairs={{0,8},{8,16},{16,24},{24,28},{28,20},{20,12},{12,4},{4,0},{1,9},{9... | collective-permute-start | bytes 516104 | tf_op jit(solution)/shard_map/ppermute | solution.py:305
  7.4 8.0 %collective-permute-start.9 = (bf16[112,768]{1,0:T(8,128)(2,1)S(1)}, bf16[112,768]{1,0:T(8,128)(2,1)S(1)}, u32[]{:S(2)}, u32[]{:S(2)}) collective-permute-start(bf16[112,768]{1,0:T(8,128)(2,1)S(1)} %get-tuple-element.49.first), channel_id=1, source_target_pairs={{0,4},{8,0},{16,8},{24,16},{28,24},{20,28},{12,20},{4,12},{1,5},{9... | collective-permute-start | bytes 516104 | tf_op jit(solution)/shard_map/ppermute | solution.py:305
  15.4 8.7 %collective-permute-start.11 = (bf16[112,768]{1,0:T(8,128)(2,1)S(1)}, bf16[112,768]{1,0:T(8,128)(2,1)S(1)}, u32[]{:S(2)}, u32[]{:S(2)}) collective-permute-start(bf16[112,768]{1,0:T(8,128)(2,1)S(1)} %collective-permute-done.7.refs_0_), channel_id=1, source_target_pairs={{0,8},{8,16},{16,24},{24,28},{28,20},{20,12},{12,4},{4,0},{1,9},{9... | collective-permute-start | bytes 516104 | tf_op jit(solution)/shard_map/ppermute | solution.py:305
  15.9 8.2 %collective-permute-start.12 = (bf16[112,768]{1,0:T(8,128)(2,1)S(1)}, bf16[112,768]{1,0:T(8,128)(2,1)S(1)}, u32[]{:S(2)}, u32[]{:S(2)}) collective-permute-start(bf16[112,768]{1,0:T(8,128)(2,1)S(1)} %collective-permute-done.9.refs_2_), channel_id=1, source_target_pairs={{0,4},{8,0},{16,8},{24,16},{28,24},{20,28},{12,20},{4,12},{1,5},{9... | collective-permute-start | bytes 516104 | tf_op jit(solution)/shard_map/ppermute | solution.py:305
  17.5 8.7 %collective-permute-start.15 = (bf16[112,896]{1,0:T(8,128)(2,1)S(1)}, bf16[112,896]{1,0:T(8,128)(2,1)S(1)}, u32[]{:S(2)}, u32[]{:S(2)}) collective-permute-start(bf16[112,896]{1,0:T(8,128)(2,1)S(1)} %collective-permute-done.8.refs_1_), channel_id=1, source_target_pairs={{0,8},{8,16},{16,24},{24,28},{28,20},{20,12},{12,4},{4,0},{1,9},{9... | collective-permute-start | bytes 602120 | tf_op jit(solution)/shard_map/ppermute | solution.py:305
  17.9 8.2 %collective-permute-start.16 = (bf16[112,896]{1,0:T(8,128)(2,1)S(1)}, bf16[112,896]{1,0:T(8,128)(2,1)S(1)}, u32[]{:S(2)}, u32[]{:S(2)}) collective-permute-start(bf16[112,896]{1,0:T(8,128)(2,1)S(1)} %collective-permute-done.10.refs_3_), channel_id=1, source_target_pairs={{0,4},{8,0},{16,8},{24,16},{28,24},{20,28},{12,20},{4,12},{1,5},{9... | collective-permute-start | bytes 602120 | tf_op jit(solution)/shard_map/ppermute | solution.py:305
  24.1 8.7 %collective-permute-start.13 = (bf16[112,768]{1,0:T(8,128)(2,1)S(1)}, bf16[112,768]{1,0:T(8,128)(2,1)S(1)}, u32[]{:S(2)}, u32[]{:S(2)}) collective-permute-start(bf16[112,768]{1,0:T(8,128)(2,1)S(1)} %collective-permute-done.11.refs_0_), channel_id=1, source_target_pairs={{0,8},{8,16},{16,24},{24,28},{28,20},{20,12},{12,4},{4,0},{1,9},{9... | collective-permute-start | bytes 516104 | tf_op jit(solution)/shard_map/ppermute | solution.py:305
  24.6 8.2 %collective-permute-start.14 = (bf16[112,768]{1,0:T(8,128)(2,1)S(1)}, bf16[112,768]{1,0:T(8,128)(2,1)S(1)}, u32[]{:S(2)}, u32[]{:S(2)}) collective-permute-start(bf16[112,768]{1,0:T(8,128)(2,1)S(1)} %collective-permute-done.12.refs_2_), channel_id=1, source_target_pairs={{0,4},{8,0},{16,8},{24,16},{28,24},{20,28},{12,20},{4,12},{1,5},{9... | collective-permute-start | bytes 516104 | tf_op jit(solution)/shard_map/ppermute | solution.py:305
  26.2 7.4 %collective-permute-start.18 = (bf16[112,896]{1,0:T(8,128)(2,1)S(1)}, bf16[112,896]{1,0:T(8,128)(2,1)S(1)}, u32[]{:S(2)}, u32[]{:S(2)}) collective-permute-start(bf16[112,896]{1,0:T(8,128)(2,1)S(1)} %collective-permute-done.15.refs_1_), channel_id=1, source_target_pairs={{0,8},{8,16},{16,24},{24,28},{28,20},{20,12},{12,4},{4,0},{1,9},{9... | collective-permute-start | bytes 602120 | tf_op jit(solution)/shard_map/ppermute | solution.py:305
  27.0 6.6 %collective-permute-start.19 = (bf16[112,896]{1,0:T(8,128)(2,1)S(1)}, bf16[112,896]{1,0:T(8,128)(2,1)S(1)}, u32[]{:S(2)}, u32[]{:S(2)}) collective-permute-start(bf16[112,896]{1,0:T(8,128)(2,1)S(1)} %collective-permute-done.16.refs_3_), channel_id=1, source_target_pairs={{0,4},{8,0},{16,8},{24,16},{28,24},{20,28},{12,20},{4,12},{1,5},{9... | collective-permute-start | bytes 602120 | tf_op jit(solution)/shard_map/ppermute | solution.py:305
  32.8 6.8 %collective-permute-start.17 = (bf16[112,768]{1,0:T(8,128)(2,1)S(1)}, bf16[112,768]{1,0:T(8,128)(2,1)S(1)}, u32[]{:S(2)}, u32[]{:S(2)}) collective-permute-start(bf16[112,768]{1,0:T(8,128)(2,1)S(1)} %collective-permute-done.13.refs_0_), channel_id=1, source_target_pairs={{0,8},{8,16},{16,24},{24,28},{28,20},{20,12},{12,4},{4,0},{1,9},{9... | collective-permute-start | bytes 516104 | tf_op jit(solution)/shard_map/ppermute | solution.py:305
  33.6 5.9 %collective-permute-start.20 = (bf16[112,896]{1,0:T(8,128)(2,1)S(1)}, bf16[112,896]{1,0:T(8,128)(2,1)S(1)}, u32[]{:S(2)}, u32[]{:S(2)}) collective-permute-start(bf16[112,896]{1,0:T(8,128)(2,1)S(1)} %collective-permute-done.19.refs_3_), channel_id=1, source_target_pairs={{0,4},{8,0},{16,8},{24,16},{28,24},{20,28},{12,20},{4,12},{1,5},{9... | collective-permute-start | bytes 602120 | tf_op jit(solution)/shard_map/ppermute | solution.py:305

commit v5 on v4

--- a/solution.py
+++ b/solution.py
@@ -38,7 +38,7 @@
     ]
     for copy in copies:
         copy.start()
-    for copy in copies:
+    for copy in copies[1:]:
         copy.wait()
     row = lax.axis_index("tp") * rows + lax.broadcasted_iota(jnp.int32, (1, rows), 1)
     length = jnp.zeros((1, rows), jnp.int32)
@@ -55,16 +55,17 @@
     select = (rank == down.astype(jnp.float32)) & live
     select = jnp.where(select, 1.0, 0.0).astype(jnp.bfloat16)
 
-    x = hidden_t[...].astype(jnp.float32)
-    meansq = jnp.sum(x * x, axis=0, keepdims=True) * (1.0 / width)
-    scale = lax.rsqrt(meansq + EPS)
     g = jnp.broadcast_to(gain[...].astype(jnp.float32).reshape(1, width), (rows, width)).T
-    normed = (x * scale * g).astype(jnp.bfloat16)
     ids = targets[...].reshape(1, rows)
     high = ids // BASE
     digit = lax.broadcasted_iota(jnp.int32, (EXTRA, rows), 0)
     digits = jnp.where(digit == 0, high, jnp.where(digit == 1, ids - high * BASE, 0))
     digits = jnp.where(digit == 2, jnp.sum(alive), digits.astype(jnp.float32))
+    copies[0].wait()
+    x = hidden_t[...].astype(jnp.float32)
+    meansq = jnp.sum(x * x, axis=0, keepdims=True) * (1.0 / width)
+    scale = lax.rsqrt(meansq + EPS)
+    normed = (x * scale * g).astype(jnp.bfloat16)
     full = jnp.concatenate([normed, digits.astype(jnp.bfloat16)], axis=0)
     packed = lax.dot_general(
         select, full, (((1,), (1,)), ((), ())), preferred_element_type=jnp.float32

time: 55.4 us -> 55.5 us (level)
  no operation moved by 1% of the time
where the time goes in v5:
time: 55.5 us; the launch traced here: 55.3 us
  Pallas kernels  24.5 us (44%)
  starting transfers between devices  15.6 us (28%)
  blocking collectives  12 us (22%)
  waiting for transfers between devices  2.39 us (4%)
  between operations  0.78 us (1%)
    ppermute x14, starting transfers between devices, hop(): return lax.ppermute(value, 'tp', pairs)  15.6 us
    pallas_call x3, Pallas kernels, wave(): pl.pallas_call(functools.partial(wave_kernel, count), out_shape=[jax.Shap...  13.6 us
    all_to_all x1, blocking collectives, on_device(): shares = lax.all_to_all(table, 'tp', 0, 0, tiled=True)  12 us
    pallas_call x1, Pallas kernels, on_device(): pl.pallas_call(own_kernel, out_shape=[jax.ShapeDtypeStruct((8, rows), jnp...  5.6 us
    pallas_call x1, Pallas kernels, last_wave(): pl.pallas_call(functools.partial(last_wave_kernel, n, new, [*blocks, *fou...  2.92 us
    ppermute x14, waiting for transfers between devices, hop(): return lax.ppermute(value, 'tp', pairs)  2.39 us
    pallas_call x1, Pallas kernels, on_device(): pl.pallas_call(norm_kernel, out_shape=[jax.ShapeDtypeStruct((kept, cut),...  1.73 us
  transfers between devices with their start and end apart: 14, of which 1 were waited for; matrix products, arithmetic and copies ran while one was open for 0% of the time, Pallas kernels for 35%

profile of v5, /device:TPU:0, one launch (start us, length us, event | category | flops | bytes accessed | tf_op | source)
XLA Modules:
  0.0 55.3 jit_solution(11670393935481635434)
XLA Ops:
  0.6 1.7 %norm.1 = (bf16[112,768]{1,0:T(8,128)(2,1)S(1)}, bf16[112,896]{1,0:T(8,128)(2,1)S(1)}, bf16[16,1664]{1,0:T(8,128)(2,1)S(1)}, f32[1,128]{1,0:T(1,128)S(1)}) custom-call(bf16[1600,128]{1,0:T(8,128)(2,1)} %bitcast.6, bf16[1600]{0:T(1024)(128)(2,1)} %gain_any.1, s32[128]{0:T(128)} %targets_any.1, s32[4]{0:T(128)} %lengths_any.1, s32[128]{0:T(128)} %mask_any.1), custom_call_target="tpu_custom_call" | custom-call | tf_op jit(solution)/shard_map/norm/pallas_call | solution.py:308
  2.4 3.0 %collective-permute-start.10 = (bf16[112,896]{1,0:T(8,128)(2,1)S(1)}, bf16[112,896]{1,0:T(8,128)(2,1)S(1)}, u32[]{:S(2)}, u32[]{:S(2)}) collective-permute-start(bf16[112,896]{1,0:T(8,128)(2,1)S(1)} %get-tuple-element.50.second), channel_id=1, source_target_pairs={{0,4},{8,0},{16,8},{24,16},{28,24},{20,28},{12,20},{4,12},{1,5},{9... | collective-permute-start | bytes 602120 | tf_op jit(solution)/shard_map/ppermute | solution.py:306
  5.4 0.1 collective-permute-start.8
  5.5 2.0 %collective-permute-start.7 = (bf16[112,768]{1,0:T(8,128)(2,1)S(1)}, bf16[112,768]{1,0:T(8,128)(2,1)S(1)}, u32[]{:S(2)}, u32[]{:S(2)}) collective-permute-start(bf16[112,768]{1,0:T(8,128)(2,1)S(1)} %get-tuple-element.49.first), channel_id=1, source_target_pairs={{0,8},{8,16},{16,24},{24,28},{28,20},{20,12},{12,4},{4,0},{1,9},{9... | collective-permute-start | bytes 516104 | tf_op jit(solution)/shard_map/ppermute | solution.py:306
  7.5 0.1 collective-permute-start.9
  7.5 5.6 %own.1 = (f32[8,128]{1,0:T(8,128)S(1)}, bf16[1600,4000]{1,0:T(8,128)(2,1)S(1)}) custom-call(bf16[1600,4000]{1,0:T(8,128)(2,1)} %head_any.1, bf16[112,768]{1,0:T(8,128)(2,1)S(1)} %get-tuple-element.49.first, bf16[112,896]{1,0:T(8,128)(2,1)S(1)} %get-tuple-element.50.second), custom_call_target="tpu_custom_call" | custom-call | flops 1433600000 | bytes 12800000 | tf_op jit(solution)/shard_map/own/pallas_call | solution.py:330
  13.1 2.4 %collective-permute-done.7.refs_0_ = bf16[112,768]{1,0:T(8,128)(2,1)S(1)} collective-permute-done((bf16[112,768]{1,0:T(8,128)(2,1)S(1)}, bf16[112,768]{1,0:T(8,128)(2,1)S(1)}, u32[]{:S(2)}, u32[]{:S(2)}) %collective-permute-start.7) | collective-permute-done | bytes 172064 | tf_op jit(solution)/shard_map/ppermute | solution.py:306
  15.5 0.0 collective-permute-done.9.refs_2_
  15.5 0.0 collective-permute-done.10.refs_3_
  15.5 0.0 collective-permute-done.8.refs_1_
  15.5 0.5 collective-permute-start.11
  16.0 1.6 %collective-permute-start.12 = (bf16[112,768]{1,0:T(8,128)(2,1)S(1)}, bf16[112,768]{1,0:T(8,128)(2,1)S(1)}, u32[]{:S(2)}, u32[]{:S(2)}) collective-permute-start(bf16[112,768]{1,0:T(8,128)(2,1)S(1)} %collective-permute-done.9.refs_2_), channel_id=1, source_target_pairs={{0,4},{8,0},{16,8},{24,16},{28,24},{20,28},{12,20},{4,12},{1,5},{9... | collective-permute-start | bytes 516104 | tf_op jit(solution)/shard_map/ppermute | solution.py:306
  17.6 0.4 collective-permute-start.15
  18.0 1.6 %collective-permute-start.16 = (bf16[112,896]{1,0:T(8,128)(2,1)S(1)}, bf16[112,896]{1,0:T(8,128)(2,1)S(1)}, u32[]{:S(2)}, u32[]{:S(2)}) collective-permute-start(bf16[112,896]{1,0:T(8,128)(2,1)S(1)} %collective-permute-done.10.refs_3_), channel_id=1, source_target_pairs={{0,4},{8,0},{16,8},{24,16},{28,24},{20,28},{12,20},{4,12},{1,5},{9... | collective-permute-start | bytes 602120 | tf_op jit(solution)/shard_map/ppermute | solution.py:306
  19.6 4.5 %wave2.3 = (f32[8,128]{1,0:T(8,128)S(1)}, f32[8,128]{1,0:T(8,128)S(1)}) custom-call(bf16[1600,4000]{1,0:T(8,128)(2,1)S(1)} %get-tuple-element.52.head, bf16[112,768]{1,0:T(8,128)(2,1)S(1)} %collective-permute-done.7.refs_0_, bf16[112,896]{1,0:T(8,128)(2,1)S(1)} %collective-permute-done.8.refs_1_, bf16[112,768]{1,0:T(8,128)(2,1)S(1)} %collective-permute-done.9.refs_2_, ...), custom_call_target="tpu_custom_call" | custom-call | flops 2867200000 | bytes 12800000 | tf_op jit(solution)/shard_map/wave2/pallas_call | solution.py:261
  24.2 0.0 collective-permute-done.11.refs_0_
  24.2 0.0 collective-permute-done.12.refs_2_
  24.2 0.5 collective-permute-start.13
  24.7 1.6 %collective-permute-start.14 = (bf16[112,768]{1,0:T(8,128)(2,1)S(1)}, bf16[112,768]{1,0:T(8,128)(2,1)S(1)}, u32[]{:S(2)}, u32[]{:S(2)}) collective-permute-start(bf16[112,768]{1,0:T(8,128)(2,1)S(1)} %collective-permute-done.12.refs_2_), channel_id=1, source_target_pairs={{0,4},{8,0},{16,8},{24,16},{28,24},{20,28},{12,20},{4,12},{1,5},{9... | collective-permute-start | bytes 516104 | tf_op jit(solution)/shard_map/ppermute | solution.py:306
  26.3 0.0 collective-permute-done.15.refs_1_
  26.3 0.0 collective-permute-done.16.refs_3_
  26.3 0.8 %collective-permute-start.18 = (bf16[112,896]{1,0:T(8,128)(2,1)S(1)}, bf16[112,896]{1,0:T(8,128)(2,1)S(1)}, u32[]{:S(2)}, u32[]{:S(2)}) collective-permute-start(bf16[112,896]{1,0:T(8,128)(2,1)S(1)} %collective-permute-done.15.refs_1_), channel_id=1, source_target_pairs={{0,8},{8,16},{16,24},{24,28},{28,20},{20,12},{12,4},{4,0},{1,9},{9... | collective-permute-start | bytes 602120 | tf_op jit(solution)/shard_map/ppermute | solution.py:306
  27.1 1.2 %collective-permute-start.19 = (bf16[112,896]{1,0:T(8,128)(2,1)S(1)}, bf16[112,896]{1,0:T(8,128)(2,1)S(1)}, u32[]{:S(2)}, u32[]{:S(2)}) collective-permute-start(bf16[112,896]{1,0:T(8,128)(2,1)S(1)} %collective-permute-done.16.refs_3_), channel_id=1, source_target_pairs={{0,4},{8,0},{16,8},{24,16},{28,24},{20,28},{12,20},{4,12},{1,5},{9... | collective-permute-start | bytes 602120 | tf_op jit(solution)/shard_map/ppermute | solution.py:306
  28.3 4.5 %wave2.4 = (f32[8,128]{1,0:T(8,128)S(1)}, f32[8,128]{1,0:T(8,128)S(1)}) custom-call(bf16[1600,4000]{1,0:T(8,128)(2,1)S(1)} %get-tuple-element.52.head, bf16[112,768]{1,0:T(8,128)(2,1)S(1)} %collective-permute-done.11.refs_0_, bf16[112,896]{1,0:T(8,128)(2,1)S(1)} %collective-permute-done.15.refs_1_, bf16[112,768]{1,0:T(8,128)(2,1)S(1)} %collective-permute-done.12.refs_2_, ...), custom_call_target="tpu_custom_call" | custom-call | flops 2867200000 | bytes 12800000 | tf_op jit(solution)/shard_map/wave2/pallas_call | solution.py:261
  32.8 0.0 collective-permute-done.13.refs_0_
  32.8 0.0 collective-permute-done.14.refs_2_
  32.8 0.9 %collective-permute-start.17 = (bf16[112,768]{1,0:T(8,128)(2,1)S(1)}, bf16[112,768]{1,0:T(8,128)(2,1)S(1)}, u32[]{:S(2)}, u32[]{:S(2)}) collective-permute-start(bf16[112,768]{1,0:T(8,128)(2,1)S(1)} %collective-permute-done.13.refs_0_), channel_id=1, source_target_pairs={{0,8},{8,16},{16,24},{24,28},{28,20},{20,12},{12,4},{4,0},{1,9},{9... | collective-permute-start | bytes 516104 | tf_op jit(solution)/shard_map/ppermute | solution.py:306
  33.7 0.0 collective-permute-done.18.refs_1_
  33.7 0.0 collective-permute-done.19.refs_3_
  33.7 1.4 %collective-permute-start.20 = (bf16[112,896]{1,0:T(8,128)(2,1)S(1)}, bf16[112,896]{1,0:T(8,128)(2,1)S(1)}, u32[]{:S(2)}, u32[]{:S(2)}) collective-permute-start(bf16[112,896]{1,0:T(8,128)(2,1)S(1)} %collective-permute-done.19.refs_3_), channel_id=1, source_target_pairs={{0,4},{8,0},{16,8},{24,16},{28,24},{20,28},{12,20},{4,12},{1,5},{9... | collective-permute-start | bytes 602120 | tf_op jit(solution)/shard_map/ppermute | solution.py:306
  35.1 4.5 %wave2.5 = (f32[8,128]{1,0:T(8,128)S(1)}, f32[8,128]{1,0:T(8,128)S(1)}) custom-call(bf16[1600,4000]{1,0:T(8,128)(2,1)S(1)} %get-tuple-element.52.head, bf16[112,768]{1,0:T(8,128)(2,1)S(1)} %collective-permute-done.13.refs_0_, bf16[112,896]{1,0:T(8,128)(2,1)S(1)} %collective-permute-done.18.refs_1_, bf16[112,768]{1,0:T(8,128)(2,1)S(1)} %collective-permute-done.14.refs_2_, ...), custom_call_target="tpu_custom_call" | custom-call | flops 2867200000 | bytes 12800000 | tf_op jit(solution)/shard_map/wave2/pallas_call | solution.py:261
  39.6 0.0 collective-permute-done.17.refs_0_
  39.6 0.0 collective-permute-done.20.refs_1_
  39.7 2.9 %last1.1 = (f32[8,8,128]{2,1,0:T(8,128)S(1)}, f32[1,128]{1,0:T(1,128)S(1)}) custom-call(bf16[1600,4000]{1,0:T(8,128)(2,1)S(1)} %get-tuple-element.52.head, bf16[112,768]{1,0:T(8,128)(2,1)S(1)} %collective-permute-done.17.refs_0_, bf16[112,896]{1,0:T(8,128)(2,1)S(1)} %collective-permute-done.20.refs_1_, f32[8,128]{1,0:T(8,128)S(1)} %get-tuple-element.72.refs_2_, ...), custom_call_target="tpu_custom_call" | custom-call | flops 1433600000 | bytes 12800000 | tf_op jit(solution)/shard_map/last1/pallas_call | solution.py:277
  42.7 12.0 %all_to_all.10.shares = f32[8,8,128]{2,1,0:T(8,128)S(1)} all-to-all(f32[8,8,128]{2,1,0:T(8,128)S(1)} %get-tuple-element.79), channel_id=1, replica_groups=mesh['tp'=8,'dp'=4] {'tp'}, dimensions={0} | all-to-all | bytes 65536 | tf_op jit(solution)/shard_map/all_to_all | solution.py:369
  54.6 0.7 %combine.1 = (f32[1,128]{1,0:T(1,128)}, f32[1,128]{1,0:T(1,128)}) custom-call(f32[1,128]{1,0:T(1,128)S(1)} %get-tuple-element.48.place, f32[8,8,128]{2,1,0:T(8,128)S(1)} %all_to_all.10.shares, f32[8,8,128]{2,1,0:T(8,128)S(1)} %get-tuple-element.84.more), custom_call_target="tpu_custom_call" | custom-call | tf_op jit(solution)/shard_map/combine/pallas_call | solution.py:377
  (2 shorter events, 0.0 us)
Async XLA Ops:
  2.4 13.1 %collective-permute-start.10 = (bf16[112,896]{1,0:T(8,128)(2,1)S(1)}, bf16[112,896]{1,0:T(8,128)(2,1)S(1)}, u32[]{:S(2)}, u32[]{:S(2)}) collective-permute-start(bf16[112,896]{1,0:T(8,128)(2,1)S(1)} %get-tuple-element.50.second), channel_id=1, source_target_pairs={{0,4},{8,0},{16,8},{24,16},{28,24},{20,28},{12,20},{4,12},{1,5},{9... | collective-permute-start | bytes 602120 | tf_op jit(solution)/shard_map/ppermute | solution.py:306
  5.4 10.1 %collective-permute-start.8 = (bf16[112,896]{1,0:T(8,128)(2,1)S(1)}, bf16[112,896]{1,0:T(8,128)(2,1)S(1)}, u32[]{:S(2)}, u32[]{:S(2)}) collective-permute-start(bf16[112,896]{1,0:T(8,128)(2,1)S(1)} %get-tuple-element.50.second), channel_id=1, source_target_pairs={{0,8},{8,16},{16,24},{24,28},{28,20},{20,12},{12,4},{4,0},{1,9},{9... | collective-permute-start | bytes 602120 | tf_op jit(solution)/shard_map/ppermute | solution.py:306
  5.5 10.0 %collective-permute-start.7 = (bf16[112,768]{1,0:T(8,128)(2,1)S(1)}, bf16[112,768]{1,0:T(8,128)(2,1)S(1)}, u32[]{:S(2)}, u32[]{:S(2)}) collective-permute-start(bf16[112,768]{1,0:T(8,128)(2,1)S(1)} %get-tuple-element.49.first), channel_id=1, source_target_pairs={{0,8},{8,16},{16,24},{24,28},{28,20},{20,12},{12,4},{4,0},{1,9},{9... | collective-permute-start | bytes 516104 | tf_op jit(solution)/shard_map/ppermute | solution.py:306
  7.5 8.0 %collective-permute-start.9 = (bf16[112,768]{1,0:T(8,128)(2,1)S(1)}, bf16[112,768]{1,0:T(8,128)(2,1)S(1)}, u32[]{:S(2)}, u32[]{:S(2)}) collective-permute-start(bf16[112,768]{1,0:T(8,128)(2,1)S(1)} %get-tuple-element.49.first), channel_id=1, source_target_pairs={{0,4},{8,0},{16,8},{24,16},{28,24},{20,28},{12,20},{4,12},{1,5},{9... | collective-permute-start | bytes 516104 | tf_op jit(solution)/shard_map/ppermute | solution.py:306
  15.5 8.6 %collective-permute-start.11 = (bf16[112,768]{1,0:T(8,128)(2,1)S(1)}, bf16[112,768]{1,0:T(8,128)(2,1)S(1)}, u32[]{:S(2)}, u32[]{:S(2)}) collective-permute-start(bf16[112,768]{1,0:T(8,128)(2,1)S(1)} %collective-permute-done.7.refs_0_), channel_id=1, source_target_pairs={{0,8},{8,16},{16,24},{24,28},{28,20},{20,12},{12,4},{4,0},{1,9},{9... | collective-permute-start | bytes 516104 | tf_op jit(solution)/shard_map/ppermute | solution.py:306
  16.0 8.2 %collective-permute-start.12 = (bf16[112,768]{1,0:T(8,128)(2,1)S(1)}, bf16[112,768]{1,0:T(8,128)(2,1)S(1)}, u32[]{:S(2)}, u32[]{:S(2)}) collective-permute-start(bf16[112,768]{1,0:T(8,128)(2,1)S(1)} %collective-permute-done.9.refs_2_), channel_id=1, source_target_pairs={{0,4},{8,0},{16,8},{24,16},{28,24},{20,28},{12,20},{4,12},{1,5},{9... | collective-permute-start | bytes 516104 | tf_op jit(solution)/shard_map/ppermute | solution.py:306
  17.6 8.7 %collective-permute-start.15 = (bf16[112,896]{1,0:T(8,128)(2,1)S(1)}, bf16[112,896]{1,0:T(8,128)(2,1)S(1)}, u32[]{:S(2)}, u32[]{:S(2)}) collective-permute-start(bf16[112,896]{1,0:T(8,128)(2,1)S(1)} %collective-permute-done.8.refs_1_), channel_id=1, source_target_pairs={{0,8},{8,16},{16,24},{24,28},{28,20},{20,12},{12,4},{4,0},{1,9},{9... | collective-permute-start | bytes 602120 | tf_op jit(solution)/shard_map/ppermute | solution.py:306
  18.0 8.2 %collective-permute-start.16 = (bf16[112,896]{1,0:T(8,128)(2,1)S(1)}, bf16[112,896]{1,0:T(8,128)(2,1)S(1)}, u32[]{:S(2)}, u32[]{:S(2)}) collective-permute-start(bf16[112,896]{1,0:T(8,128)(2,1)S(1)} %collective-permute-done.10.refs_3_), channel_id=1, source_target_pairs={{0,4},{8,0},{16,8},{24,16},{28,24},{20,28},{12,20},{4,12},{1,5},{9... | collective-permute-start | bytes 602120 | tf_op jit(solution)/shard_map/ppermute | solution.py:306
  24.2 8.7 %collective-permute-start.13 = (bf16[112,768]{1,0:T(8,128)(2,1)S(1)}, bf16[112,768]{1,0:T(8,128)(2,1)S(1)}, u32[]{:S(2)}, u32[]{:S(2)}) collective-permute-start(bf16[112,768]{1,0:T(8,128)(2,1)S(1)} %collective-permute-done.11.refs_0_), channel_id=1, source_target_pairs={{0,8},{8,16},{16,24},{24,28},{28,20},{20,12},{12,4},{4,0},{1,9},{9... | collective-permute-start | bytes 516104 | tf_op jit(solution)/shard_map/ppermute | solution.py:306
  24.7 8.2 %collective-permute-start.14 = (bf16[112,768]{1,0:T(8,128)(2,1)S(1)}, bf16[112,768]{1,0:T(8,128)(2,1)S(1)}, u32[]{:S(2)}, u32[]{:S(2)}) collective-permute-start(bf16[112,768]{1,0:T(8,128)(2,1)S(1)} %collective-permute-done.12.refs_2_), channel_id=1, source_target_pairs={{0,4},{8,0},{16,8},{24,16},{28,24},{20,28},{12,20},{4,12},{1,5},{9... | collective-permute-start | bytes 516104 | tf_op jit(solution)/shard_map/ppermute | solution.py:306
  26.3 7.5 %collective-permute-start.18 = (bf16[112,896]{1,0:T(8,128)(2,1)S(1)}, bf16[112,896]{1,0:T(8,128)(2,1)S(1)}, u32[]{:S(2)}, u32[]{:S(2)}) collective-permute-start(bf16[112,896]{1,0:T(8,128)(2,1)S(1)} %collective-permute-done.15.refs_1_), channel_id=1, source_target_pairs={{0,8},{8,16},{16,24},{24,28},{28,20},{20,12},{12,4},{4,0},{1,9},{9... | collective-permute-start | bytes 602120 | tf_op jit(solution)/shard_map/ppermute | solution.py:306
  27.1 6.7 %collective-permute-start.19 = (bf16[112,896]{1,0:T(8,128)(2,1)S(1)}, bf16[112,896]{1,0:T(8,128)(2,1)S(1)}, u32[]{:S(2)}, u32[]{:S(2)}) collective-permute-start(bf16[112,896]{1,0:T(8,128)(2,1)S(1)} %collective-permute-done.16.refs_3_), channel_id=1, source_target_pairs={{0,4},{8,0},{16,8},{24,16},{28,24},{20,28},{12,20},{4,12},{1,5},{9... | collective-permute-start | bytes 602120 | tf_op jit(solution)/shard_map/ppermute | solution.py:306
  32.8 6.8 %collective-permute-start.17 = (bf16[112,768]{1,0:T(8,128)(2,1)S(1)}, bf16[112,768]{1,0:T(8,128)(2,1)S(1)}, u32[]{:S(2)}, u32[]{:S(2)}) collective-permute-start(bf16[112,768]{1,0:T(8,128)(2,1)S(1)} %collective-permute-done.13.refs_0_), channel_id=1, source_target_pairs={{0,8},{8,16},{16,24},{24,28},{28,20},{20,12},{12,4},{4,0},{1,9},{9... | collective-permute-start | bytes 516104 | tf_op jit(solution)/shard_map/ppermute | solution.py:306
  33.7 5.9 %collective-permute-start.20 = (bf16[112,896]{1,0:T(8,128)(2,1)S(1)}, bf16[112,896]{1,0:T(8,128)(2,1)S(1)}, u32[]{:S(2)}, u32[]{:S(2)}) collective-permute-start(bf16[112,896]{1,0:T(8,128)(2,1)S(1)} %collective-permute-done.19.refs_3_), channel_id=1, source_target_pairs={{0,4},{8,0},{16,8},{24,16},{28,24},{20,28},{12,20},{4,12},{1,5},{9... | collective-permute-start | bytes 602120 | tf_op jit(solution)/shard_map/ppermute | solution.py:306

commit v6 on v4

--- a/solution.py
+++ b/solution.py
@@ -229,13 +229,11 @@
 def final_kernel(kept, place, shares, more, logprob, entropy):
     rows = place.shape[1]
     down = lax.broadcasted_iota(jnp.int32, (rows, rows), 0)
-    here = (down.astype(jnp.float32) == place[...]) & (down < kept)
-    there = (down + kept).astype(jnp.float32) == place[...]
+    here = down.astype(jnp.float32) == place[...]
     for out, first, rest in zip((logprob, entropy), merge(shares), merge(more)):
-        first = jnp.broadcast_to(first, (rows, rows)).T
-        rest = jnp.broadcast_to(rest, (rows, rows)).T
-        both = jnp.where(here, first, jnp.where(there, rest, 0.0))
-        out[...] = jnp.sum(both, axis=0, keepdims=True)
+        both = jnp.concatenate([first[:, :kept], rest[:, : rows - kept]], axis=1)
+        both = jnp.broadcast_to(both, (rows, rows)).T
+        out[...] = jnp.sum(jnp.where(here, both, 0.0), axis=0, keepdims=True)
 
 
 def wave_scratch(count, rows, width):

time: 55.4 us -> 55.5 us (level)
  no operation moved by 1% of the time
where the time goes in v6:
time: 55.5 us; the launch traced here: 55.3 us
  Pallas kernels  24.5 us (44%)
  starting transfers between devices  15.6 us (28%)
  blocking collectives  12 us (22%)
  waiting for transfers between devices  2.39 us (4%)
  between operations  0.78 us (1%)
    ppermute x14, starting transfers between devices, hop(): return lax.ppermute(value, 'tp', pairs)  15.6 us
    pallas_call x3, Pallas kernels, wave(): pl.pallas_call(functools.partial(wave_kernel, count), out_shape=[jax.Shap...  13.6 us
    all_to_all x1, blocking collectives, on_device(): shares = lax.all_to_all(table, 'tp', 0, 0, tiled=True)  12 us
    pallas_call x1, Pallas kernels, on_device(): pl.pallas_call(own_kernel, out_shape=[jax.ShapeDtypeStruct((8, rows), jnp...  5.59 us
    pallas_call x1, Pallas kernels, last_wave(): pl.pallas_call(functools.partial(last_wave_kernel, n, new, [*blocks, *fou...  2.92 us
    ppermute x14, waiting for transfers between devices, hop(): return lax.ppermute(value, 'tp', pairs)  2.39 us
    pallas_call x1, Pallas kernels, on_device(): pl.pallas_call(norm_kernel, out_shape=[jax.ShapeDtypeStruct((kept, cut),...  1.64 us
  transfers between devices with their start and end apart: 14, of which 1 were waited for; matrix products, arithmetic and copies ran while one was open for 0% of the time, Pallas kernels for 35%

profile of v6, /device:TPU:0, one launch (start us, length us, event | category | flops | bytes accessed | tf_op | source)
XLA Modules:
  0.0 55.3 jit_solution(1216238910309427209)
XLA Ops:
  0.6 1.6 %norm.1 = (bf16[112,768]{1,0:T(8,128)(2,1)S(1)}, bf16[112,896]{1,0:T(8,128)(2,1)S(1)}, bf16[16,1664]{1,0:T(8,128)(2,1)S(1)}, f32[1,128]{1,0:T(1,128)S(1)}) custom-call(bf16[1600,128]{1,0:T(8,128)(2,1)} %bitcast.6, bf16[1600]{0:T(1024)(128)(2,1)} %gain_any.1, s32[128]{0:T(128)} %targets_any.1, s32[4]{0:T(128)} %lengths_any.1, s32[128]{0:T(128)} %mask_any.1), custom_call_target="tpu_custom_call" | custom-call | tf_op jit(solution)/shard_map/norm/pallas_call | solution.py:305
  2.3 3.0 %collective-permute-start.10 = (bf16[112,896]{1,0:T(8,128)(2,1)S(1)}, bf16[112,896]{1,0:T(8,128)(2,1)S(1)}, u32[]{:S(2)}, u32[]{:S(2)}) collective-permute-start(bf16[112,896]{1,0:T(8,128)(2,1)S(1)} %get-tuple-element.50.second), channel_id=1, source_target_pairs={{0,4},{8,0},{16,8},{24,16},{28,24},{20,28},{12,20},{4,12},{1,5},{9... | collective-permute-start | bytes 602120 | tf_op jit(solution)/shard_map/ppermute | solution.py:303
  5.3 0.2 collective-permute-start.8
  5.4 2.0 %collective-permute-start.7 = (bf16[112,768]{1,0:T(8,128)(2,1)S(1)}, bf16[112,768]{1,0:T(8,128)(2,1)S(1)}, u32[]{:S(2)}, u32[]{:S(2)}) collective-permute-start(bf16[112,768]{1,0:T(8,128)(2,1)S(1)} %get-tuple-element.49.first), channel_id=1, source_target_pairs={{0,8},{8,16},{16,24},{24,28},{28,20},{20,12},{12,4},{4,0},{1,9},{9... | collective-permute-start | bytes 516104 | tf_op jit(solution)/shard_map/ppermute | solution.py:303
  7.4 0.1 collective-permute-start.9
  7.4 5.6 %own.1 = (f32[8,128]{1,0:T(8,128)S(1)}, bf16[1600,4000]{1,0:T(8,128)(2,1)S(1)}) custom-call(bf16[1600,4000]{1,0:T(8,128)(2,1)} %head_any.1, bf16[112,768]{1,0:T(8,128)(2,1)S(1)} %get-tuple-element.49.first, bf16[112,896]{1,0:T(8,128)(2,1)S(1)} %get-tuple-element.50.second), custom_call_target="tpu_custom_call" | custom-call | flops 1433600000 | bytes 12800000 | tf_op jit(solution)/shard_map/own/pallas_call | solution.py:327
  13.0 2.4 %collective-permute-done.7.refs_0_ = bf16[112,768]{1,0:T(8,128)(2,1)S(1)} collective-permute-done((bf16[112,768]{1,0:T(8,128)(2,1)S(1)}, bf16[112,768]{1,0:T(8,128)(2,1)S(1)}, u32[]{:S(2)}, u32[]{:S(2)}) %collective-permute-start.7) | collective-permute-done | bytes 172064 | tf_op jit(solution)/shard_map/ppermute | solution.py:303
  15.4 0.0 collective-permute-done.9.refs_2_
  15.4 0.0 collective-permute-done.10.refs_3_
  15.4 0.0 collective-permute-done.8.refs_1_
  15.4 0.5 collective-permute-start.11
  15.9 1.6 %collective-permute-start.12 = (bf16[112,768]{1,0:T(8,128)(2,1)S(1)}, bf16[112,768]{1,0:T(8,128)(2,1)S(1)}, u32[]{:S(2)}, u32[]{:S(2)}) collective-permute-start(bf16[112,768]{1,0:T(8,128)(2,1)S(1)} %collective-permute-done.9.refs_2_), channel_id=1, source_target_pairs={{0,4},{8,0},{16,8},{24,16},{28,24},{20,28},{12,20},{4,12},{1,5},{9... | collective-permute-start | bytes 516104 | tf_op jit(solution)/shard_map/ppermute | solution.py:303
  17.5 0.4 collective-permute-start.15
  17.9 1.6 %collective-permute-start.16 = (bf16[112,896]{1,0:T(8,128)(2,1)S(1)}, bf16[112,896]{1,0:T(8,128)(2,1)S(1)}, u32[]{:S(2)}, u32[]{:S(2)}) collective-permute-start(bf16[112,896]{1,0:T(8,128)(2,1)S(1)} %collective-permute-done.10.refs_3_), channel_id=1, source_target_pairs={{0,4},{8,0},{16,8},{24,16},{28,24},{20,28},{12,20},{4,12},{1,5},{9... | collective-permute-start | bytes 602120 | tf_op jit(solution)/shard_map/ppermute | solution.py:303
  19.5 4.5 %wave2.3 = (f32[8,128]{1,0:T(8,128)S(1)}, f32[8,128]{1,0:T(8,128)S(1)}) custom-call(bf16[1600,4000]{1,0:T(8,128)(2,1)S(1)} %get-tuple-element.52.head, bf16[112,768]{1,0:T(8,128)(2,1)S(1)} %collective-permute-done.7.refs_0_, bf16[112,896]{1,0:T(8,128)(2,1)S(1)} %collective-permute-done.8.refs_1_, bf16[112,768]{1,0:T(8,128)(2,1)S(1)} %collective-permute-done.9.refs_2_, ...), custom_call_target="tpu_custom_call" | custom-call | flops 2867200000 | bytes 12800000 | tf_op jit(solution)/shard_map/wave2/pallas_call | solution.py:258
  24.1 0.0 collective-permute-done.11.refs_0_
  24.1 0.0 collective-permute-done.12.refs_2_
  24.1 0.5 collective-permute-start.13
  24.6 1.6 %collective-permute-start.14 = (bf16[112,768]{1,0:T(8,128)(2,1)S(1)}, bf16[112,768]{1,0:T(8,128)(2,1)S(1)}, u32[]{:S(2)}, u32[]{:S(2)}) collective-permute-start(bf16[112,768]{1,0:T(8,128)(2,1)S(1)} %collective-permute-done.12.refs_2_), channel_id=1, source_target_pairs={{0,4},{8,0},{16,8},{24,16},{28,24},{20,28},{12,20},{4,12},{1,5},{9... | collective-permute-start | bytes 516104 | tf_op jit(solution)/shard_map/ppermute | solution.py:303
  26.2 0.0 collective-permute-done.15.refs_1_
  26.2 0.0 collective-permute-done.16.refs_3_
  26.2 0.8 %collective-permute-start.18 = (bf16[112,896]{1,0:T(8,128)(2,1)S(1)}, bf16[112,896]{1,0:T(8,128)(2,1)S(1)}, u32[]{:S(2)}, u32[]{:S(2)}) collective-permute-start(bf16[112,896]{1,0:T(8,128)(2,1)S(1)} %collective-permute-done.15.refs_1_), channel_id=1, source_target_pairs={{0,8},{8,16},{16,24},{24,28},{28,20},{20,12},{12,4},{4,0},{1,9},{9... | collective-permute-start | bytes 602120 | tf_op jit(solution)/shard_map/ppermute | solution.py:303
  27.0 1.2 %collective-permute-start.19 = (bf16[112,896]{1,0:T(8,128)(2,1)S(1)}, bf16[112,896]{1,0:T(8,128)(2,1)S(1)}, u32[]{:S(2)}, u32[]{:S(2)}) collective-permute-start(bf16[112,896]{1,0:T(8,128)(2,1)S(1)} %collective-permute-done.16.refs_3_), channel_id=1, source_target_pairs={{0,4},{8,0},{16,8},{24,16},{28,24},{20,28},{12,20},{4,12},{1,5},{9... | collective-permute-start | bytes 602120 | tf_op jit(solution)/shard_map/ppermute | solution.py:303
  28.2 4.5 %wave2.4 = (f32[8,128]{1,0:T(8,128)S(1)}, f32[8,128]{1,0:T(8,128)S(1)}) custom-call(bf16[1600,4000]{1,0:T(8,128)(2,1)S(1)} %get-tuple-element.52.head, bf16[112,768]{1,0:T(8,128)(2,1)S(1)} %collective-permute-done.11.refs_0_, bf16[112,896]{1,0:T(8,128)(2,1)S(1)} %collective-permute-done.15.refs_1_, bf16[112,768]{1,0:T(8,128)(2,1)S(1)} %collective-permute-done.12.refs_2_, ...), custom_call_target="tpu_custom_call" | custom-call | flops 2867200000 | bytes 12800000 | tf_op jit(solution)/shard_map/wave2/pallas_call | solution.py:258
  32.7 0.0 collective-permute-done.13.refs_0_
  32.8 0.0 collective-permute-done.14.refs_2_
  32.8 0.9 %collective-permute-start.17 = (bf16[112,768]{1,0:T(8,128)(2,1)S(1)}, bf16[112,768]{1,0:T(8,128)(2,1)S(1)}, u32[]{:S(2)}, u32[]{:S(2)}) collective-permute-start(bf16[112,768]{1,0:T(8,128)(2,1)S(1)} %collective-permute-done.13.refs_0_), channel_id=1, source_target_pairs={{0,8},{8,16},{16,24},{24,28},{28,20},{20,12},{12,4},{4,0},{1,9},{9... | collective-permute-start | bytes 516104 | tf_op jit(solution)/shard_map/ppermute | solution.py:303
  33.6 0.0 collective-permute-done.18.refs_1_
  33.6 0.0 collective-permute-done.19.refs_3_
  33.6 1.4 %collective-permute-start.20 = (bf16[112,896]{1,0:T(8,128)(2,1)S(1)}, bf16[112,896]{1,0:T(8,128)(2,1)S(1)}, u32[]{:S(2)}, u32[]{:S(2)}) collective-permute-start(bf16[112,896]{1,0:T(8,128)(2,1)S(1)} %collective-permute-done.19.refs_3_), channel_id=1, source_target_pairs={{0,4},{8,0},{16,8},{24,16},{28,24},{20,28},{12,20},{4,12},{1,5},{9... | collective-permute-start | bytes 602120 | tf_op jit(solution)/shard_map/ppermute | solution.py:303
  35.0 4.5 %wave2.5 = (f32[8,128]{1,0:T(8,128)S(1)}, f32[8,128]{1,0:T(8,128)S(1)}) custom-call(bf16[1600,4000]{1,0:T(8,128)(2,1)S(1)} %get-tuple-element.52.head, bf16[112,768]{1,0:T(8,128)(2,1)S(1)} %collective-permute-done.13.refs_0_, bf16[112,896]{1,0:T(8,128)(2,1)S(1)} %collective-permute-done.18.refs_1_, bf16[112,768]{1,0:T(8,128)(2,1)S(1)} %collective-permute-done.14.refs_2_, ...), custom_call_target="tpu_custom_call" | custom-call | flops 2867200000 | bytes 12800000 | tf_op jit(solution)/shard_map/wave2/pallas_call | solution.py:258
  39.5 0.0 collective-permute-done.17.refs_0_
  39.5 0.0 collective-permute-done.20.refs_1_
  39.6 2.9 %last1.1 = (f32[8,8,128]{2,1,0:T(8,128)S(1)}, f32[1,128]{1,0:T(1,128)S(1)}) custom-call(bf16[1600,4000]{1,0:T(8,128)(2,1)S(1)} %get-tuple-element.52.head, bf16[112,768]{1,0:T(8,128)(2,1)S(1)} %collective-permute-done.17.refs_0_, bf16[112,896]{1,0:T(8,128)(2,1)S(1)} %collective-permute-done.20.refs_1_, f32[8,128]{1,0:T(8,128)S(1)} %get-tuple-element.72.refs_2_, ...), custom_call_target="tpu_custom_call" | custom-call | flops 1433600000 | bytes 12800000 | tf_op jit(solution)/shard_map/last1/pallas_call | solution.py:274
  42.6 12.0 %all_to_all.10.shares = f32[8,8,128]{2,1,0:T(8,128)S(1)} all-to-all(f32[8,8,128]{2,1,0:T(8,128)S(1)} %get-tuple-element.79), channel_id=1, replica_groups=mesh['tp'=8,'dp'=4] {'tp'}, dimensions={0} | all-to-all | bytes 65536 | tf_op jit(solution)/shard_map/all_to_all | solution.py:366
  54.5 0.7 %combine.1 = (f32[1,128]{1,0:T(1,128)}, f32[1,128]{1,0:T(1,128)}) custom-call(f32[1,128]{1,0:T(1,128)S(1)} %get-tuple-element.48.place, f32[8,8,128]{2,1,0:T(8,128)S(1)} %all_to_all.10.shares, f32[8,8,128]{2,1,0:T(8,128)S(1)} %get-tuple-element.84.more), custom_call_target="tpu_custom_call" | custom-call | tf_op jit(solution)/shard_map/combine/pallas_call | solution.py:374
  (2 shorter events, 0.0 us)
Async XLA Ops:
  2.3 13.1 %collective-permute-start.10 = (bf16[112,896]{1,0:T(8,128)(2,1)S(1)}, bf16[112,896]{1,0:T(8,128)(2,1)S(1)}, u32[]{:S(2)}, u32[]{:S(2)}) collective-permute-start(bf16[112,896]{1,0:T(8,128)(2,1)S(1)} %get-tuple-element.50.second), channel_id=1, source_target_pairs={{0,4},{8,0},{16,8},{24,16},{28,24},{20,28},{12,20},{4,12},{1,5},{9... | collective-permute-start | bytes 602120 | tf_op jit(solution)/shard_map/ppermute | solution.py:303
  5.3 10.1 %collective-permute-start.8 = (bf16[112,896]{1,0:T(8,128)(2,1)S(1)}, bf16[112,896]{1,0:T(8,128)(2,1)S(1)}, u32[]{:S(2)}, u32[]{:S(2)}) collective-permute-start(bf16[112,896]{1,0:T(8,128)(2,1)S(1)} %get-tuple-element.50.second), channel_id=1, source_target_pairs={{0,8},{8,16},{16,24},{24,28},{28,20},{20,12},{12,4},{4,0},{1,9},{9... | collective-permute-start | bytes 602120 | tf_op jit(solution)/shard_map/ppermute | solution.py:303
  5.4 10.0 %collective-permute-start.7 = (bf16[112,768]{1,0:T(8,128)(2,1)S(1)}, bf16[112,768]{1,0:T(8,128)(2,1)S(1)}, u32[]{:S(2)}, u32[]{:S(2)}) collective-permute-start(bf16[112,768]{1,0:T(8,128)(2,1)S(1)} %get-tuple-element.49.first), channel_id=1, source_target_pairs={{0,8},{8,16},{16,24},{24,28},{28,20},{20,12},{12,4},{4,0},{1,9},{9... | collective-permute-start | bytes 516104 | tf_op jit(solution)/shard_map/ppermute | solution.py:303
  7.4 8.0 %collective-permute-start.9 = (bf16[112,768]{1,0:T(8,128)(2,1)S(1)}, bf16[112,768]{1,0:T(8,128)(2,1)S(1)}, u32[]{:S(2)}, u32[]{:S(2)}) collective-permute-start(bf16[112,768]{1,0:T(8,128)(2,1)S(1)} %get-tuple-element.49.first), channel_id=1, source_target_pairs={{0,4},{8,0},{16,8},{24,16},{28,24},{20,28},{12,20},{4,12},{1,5},{9... | collective-permute-start | bytes 516104 | tf_op jit(solution)/shard_map/ppermute | solution.py:303
  15.4 8.7 %collective-permute-start.11 = (bf16[112,768]{1,0:T(8,128)(2,1)S(1)}, bf16[112,768]{1,0:T(8,128)(2,1)S(1)}, u32[]{:S(2)}, u32[]{:S(2)}) collective-permute-start(bf16[112,768]{1,0:T(8,128)(2,1)S(1)} %collective-permute-done.7.refs_0_), channel_id=1, source_target_pairs={{0,8},{8,16},{16,24},{24,28},{28,20},{20,12},{12,4},{4,0},{1,9},{9... | collective-permute-start | bytes 516104 | tf_op jit(solution)/shard_map/ppermute | solution.py:303
  15.9 8.2 %collective-permute-start.12 = (bf16[112,768]{1,0:T(8,128)(2,1)S(1)}, bf16[112,768]{1,0:T(8,128)(2,1)S(1)}, u32[]{:S(2)}, u32[]{:S(2)}) collective-permute-start(bf16[112,768]{1,0:T(8,128)(2,1)S(1)} %collective-permute-done.9.refs_2_), channel_id=1, source_target_pairs={{0,4},{8,0},{16,8},{24,16},{28,24},{20,28},{12,20},{4,12},{1,5},{9... | collective-permute-start | bytes 516104 | tf_op jit(solution)/shard_map/ppermute | solution.py:303
  17.5 8.7 %collective-permute-start.15 = (bf16[112,896]{1,0:T(8,128)(2,1)S(1)}, bf16[112,896]{1,0:T(8,128)(2,1)S(1)}, u32[]{:S(2)}, u32[]{:S(2)}) collective-permute-start(bf16[112,896]{1,0:T(8,128)(2,1)S(1)} %collective-permute-done.8.refs_1_), channel_id=1, source_target_pairs={{0,8},{8,16},{16,24},{24,28},{28,20},{20,12},{12,4},{4,0},{1,9},{9... | collective-permute-start | bytes 602120 | tf_op jit(solution)/shard_map/ppermute | solution.py:303
  17.9 8.2 %collective-permute-start.16 = (bf16[112,896]{1,0:T(8,128)(2,1)S(1)}, bf16[112,896]{1,0:T(8,128)(2,1)S(1)}, u32[]{:S(2)}, u32[]{:S(2)}) collective-permute-start(bf16[112,896]{1,0:T(8,128)(2,1)S(1)} %collective-permute-done.10.refs_3_), channel_id=1, source_target_pairs={{0,4},{8,0},{16,8},{24,16},{28,24},{20,28},{12,20},{4,12},{1,5},{9... | collective-permute-start | bytes 602120 | tf_op jit(solution)/shard_map/ppermute | solution.py:303
  24.1 8.7 %collective-permute-start.13 = (bf16[112,768]{1,0:T(8,128)(2,1)S(1)}, bf16[112,768]{1,0:T(8,128)(2,1)S(1)}, u32[]{:S(2)}, u32[]{:S(2)}) collective-permute-start(bf16[112,768]{1,0:T(8,128)(2,1)S(1)} %collective-permute-done.11.refs_0_), channel_id=1, source_target_pairs={{0,8},{8,16},{16,24},{24,28},{28,20},{20,12},{12,4},{4,0},{1,9},{9... | collective-permute-start | bytes 516104 | tf_op jit(solution)/shard_map/ppermute | solution.py:303
  24.6 8.2 %collective-permute-start.14 = (bf16[112,768]{1,0:T(8,128)(2,1)S(1)}, bf16[112,768]{1,0:T(8,128)(2,1)S(1)}, u32[]{:S(2)}, u32[]{:S(2)}) collective-permute-start(bf16[112,768]{1,0:T(8,128)(2,1)S(1)} %collective-permute-done.12.refs_2_), channel_id=1, source_target_pairs={{0,4},{8,0},{16,8},{24,16},{28,24},{20,28},{12,20},{4,12},{1,5},{9... | collective-permute-start | bytes 516104 | tf_op jit(solution)/shard_map/ppermute | solution.py:303
  26.2 7.4 %collective-permute-start.18 = (bf16[112,896]{1,0:T(8,128)(2,1)S(1)}, bf16[112,896]{1,0:T(8,128)(2,1)S(1)}, u32[]{:S(2)}, u32[]{:S(2)}) collective-permute-start(bf16[112,896]{1,0:T(8,128)(2,1)S(1)} %collective-permute-done.15.refs_1_), channel_id=1, source_target_pairs={{0,8},{8,16},{16,24},{24,28},{28,20},{20,12},{12,4},{4,0},{1,9},{9... | collective-permute-start | bytes 602120 | tf_op jit(solution)/shard_map/ppermute | solution.py:303
  27.0 6.6 %collective-permute-start.19 = (bf16[112,896]{1,0:T(8,128)(2,1)S(1)}, bf16[112,896]{1,0:T(8,128)(2,1)S(1)}, u32[]{:S(2)}, u32[]{:S(2)}) collective-permute-start(bf16[112,896]{1,0:T(8,128)(2,1)S(1)} %collective-permute-done.16.refs_3_), channel_id=1, source_target_pairs={{0,4},{8,0},{16,8},{24,16},{28,24},{20,28},{12,20},{4,12},{1,5},{9... | collective-permute-start | bytes 602120 | tf_op jit(solution)/shard_map/ppermute | solution.py:303
  32.8 6.8 %collective-permute-start.17 = (bf16[112,768]{1,0:T(8,128)(2,1)S(1)}, bf16[112,768]{1,0:T(8,128)(2,1)S(1)}, u32[]{:S(2)}, u32[]{:S(2)}) collective-permute-start(bf16[112,768]{1,0:T(8,128)(2,1)S(1)} %collective-permute-done.13.refs_0_), channel_id=1, source_target_pairs={{0,8},{8,16},{16,24},{24,28},{28,20},{20,12},{12,4},{4,0},{1,9},{9... | collective-permute-start | bytes 516104 | tf_op jit(solution)/shard_map/ppermute | solution.py:303
  33.6 5.9 %collective-permute-start.20 = (bf16[112,896]{1,0:T(8,128)(2,1)S(1)}, bf16[112,896]{1,0:T(8,128)(2,1)S(1)}, u32[]{:S(2)}, u32[]{:S(2)}) collective-permute-start(bf16[112,896]{1,0:T(8,128)(2,1)S(1)} %collective-permute-done.19.refs_3_), channel_id=1, source_target_pairs={{0,4},{8,0},{16,8},{24,16},{28,24},{20,28},{12,20},{4,12},{1,5},{9... | collective-permute-start | bytes 602120 | tf_op jit(solution)/shard_map/ppermute | solution.py:303
